TPU v7x, 256 devices: a whole 4x4x8 slice. The times are simulated.
256 devices in a mesh: slab: 4 (over y), tile: 64 (over x, z, core).
Axes of the slice: x: 4, y: 4, z: 8, core: 2. Of those that a mesh axis runs over, the one named last changes fastest.
Arguments:
- wavefield: float32 [4, 2, 2048, 2048], P(None, None, 'tile'), may hold values from -6 to 6
- slowness: float32 [4, 2048, 2048], P('slab', 'tile'), may hold values from 0.5 to 1
- angular_freq: float32 [4], replicated, may hold values from 1 to 3
- filter_taps: float32 [4, 8, 2], replicated, may hold values from -1.5 to 1.5
Outputs:
- images: float32 [4, 2048, 2048], P('slab', 'tile')
All inputs are finite; a program needn't handle non-finite values.
Results may differ from a plain program's by a relative error of at most 0.00002.
Values sent between devices are 32-bit elements; how exact they have to be, the bound alone decides.
No kernel may reach another device: no remote copies, remote signals or barrier semaphores. Data moves between devices by JAX's collectives and lax.ppermute only.
A program may use at most 64 MiB of HBM per device.

v0:
```python
import jax
import jax.numpy as jnp
from jax import lax
from jax.sharding import PartitionSpec as P

TERMS = 8


def padded_2(block, sides, width):
    for axis, dim in sides:
        count = lax.axis_size(axis)
        forward = [(i, i + 1) for i in range(count - 1)]
        backward = [(target, source) for source, target in forward]
        low = lax.ppermute(
            lax.slice_in_dim(block, block.shape[dim] - width, None, axis=dim), axis, forward
        )
        high = lax.ppermute(lax.slice_in_dim(block, 0, width, axis=dim), axis, backward)
        block = jnp.concatenate([low, block, high], axis=dim)
    return block


def passed_along(block, axis, distance):
    devices = range(lax.axis_size(axis))
    route = [(i - distance, i) for i in devices if i - distance in devices]
    return lax.ppermute(block, axis, route)


def stencil(padded):
    middle = padded[:, 1:-1, 1:-1]
    beside = padded[:, :-2, 1:-1] + padded[:, 2:, 1:-1] + padded[:, 1:-1, :-2] + padded[:, 1:-1, 2:]
    diagonal = padded[:, :-2, :-2] + padded[:, :-2, 2:] + padded[:, 2:, :-2] + padded[:, 2:, 2:]
    return -0.5 * middle + 0.25 * beside + 0.125 * diagonal


def neighbour_apply(current, layer_slow):
    extended = padded_2(current, (("tile", 1),), 1)
    padded = jnp.pad(extended, ((0, 0), (0, 0), (1, 1)))
    return layer_slow * stencil(padded)


def descend(current, slow_ext, slow_mid, freq_value, taps_here):

    def operate(source):
        return neighbour_apply(source, slow_ext)

    previous = current
    latest = operate(current)
    first_mid = previous
    second_mid = latest
    accum_real = taps_here[0, 0] * first_mid[0] - taps_here[0, 1] * first_mid[1]
    accum_imag = taps_here[0, 0] * first_mid[1] + taps_here[0, 1] * first_mid[0]
    accum_real = accum_real + taps_here[1, 0] * second_mid[0] - taps_here[1, 1] * second_mid[1]
    accum_imag = accum_imag + taps_here[1, 0] * second_mid[1] + taps_here[1, 1] * second_mid[0]
    for order_index in range(2, TERMS):
        following = 2.0 * operate(latest) - previous
        previous, latest = (latest, following)
        accum_real = (
            accum_real
            + taps_here[order_index, 0] * latest[0]
            - taps_here[order_index, 1] * latest[1]
        )
        accum_imag = (
            accum_imag
            + taps_here[order_index, 0] * latest[1]
            + taps_here[order_index, 1] * latest[0]
        )
    phase_angle = freq_value * slow_mid
    cosine = jnp.cos(phase_angle)
    sine_part = jnp.sin(phase_angle)
    return jnp.stack(
        [accum_real * cosine - accum_imag * sine_part, accum_real * sine_part + accum_imag * cosine]
    )


def local(wavefield, slowness, angular_freq, filter_taps):
    freq_count = wavefield.shape[0]
    section_count = lax.axis_size("slab")
    section_index = lax.axis_index("slab")
    tick_count = freq_count + section_count - 1
    incoming = jnp.zeros(wavefield.shape[1:], jnp.float32)
    images = jnp.zeros(slowness.shape, jnp.float32)
    for moment in range(tick_count):
        freq_index = moment - section_index
        active = jnp.logical_and(freq_index >= 0, freq_index < freq_count)
        chosen = jnp.clip(freq_index, 0, freq_count - 1)
        surface = lax.dynamic_index_in_dim(wavefield, chosen, 0, keepdims=False)
        current = jnp.where(section_index == 0, surface, incoming)
        freq_value = lax.dynamic_index_in_dim(angular_freq, chosen, 0, keepdims=False)
        taps_here = lax.dynamic_index_in_dim(filter_taps, chosen, 0, keepdims=False)
        current = descend(current, slowness[0], slowness[0], freq_value, taps_here)
        images = images.at[0].add(jnp.where(active, current[0], 0.0))
        if moment + 1 < tick_count:
            incoming = passed_along(current, "slab", 1)
    return images


def solution(mesh):
    placed = (P(None, None, "tile", None), P("slab", "tile", None), P(), P())
    return jax.shard_map(
        local, mesh=mesh, in_specs=placed, out_specs=P("slab", "tile", None), check_vma=False
    )
```

profile of v0, /device:TPU:6, one launch (start us, length us, event | category | flops | bytes accessed | tf_op | source)
XLA Modules:
  0.0 673.9 jit_solution(11941019840680189770)
XLA Ops:
  3.1 7.5 %collective-permute-start.1 = (f32[2,1,2048]{2,1,0:T(1,128)S(1)}, f32[2,1,2048]{2,1,0:T(1,128)S(1)}, u32[]{:S(2)}, u32[]{:S(2)}) collective-permute-start(f32[2,1,2048]{2,1,0:T(1,128)S(1)} %get-tuple-element.204), channel_id=1, source_target_pairs={{1,0},{2,1},{3,2},{4,3},{5,4},{6,5},{7,6},{8,7},{9,8},{10,9},{11,1... | collective-permute-start | bytes 49160 | tf_op jit(solution)/shard_map/ppermute | solution.py:17
  14.9 5.8 collective-permute-start.3
  25.0 5.8 collective-permute-start.5
  35.1 5.8 collective-permute-start.7
  45.2 5.8 collective-permute-start.9
  55.4 5.8 collective-permute-start.11
  65.5 5.8 collective-permute-start.13
  73.6 12.2 %multiply_subtract_fusion.10 = (f32[1,32,2048]{2,1,0:T(8,128)S(1)}, f32[1,32,2048]{2,1,0:T(8,128)S(1)}, f32[1,32,2048]{2,1,0:T(8,128)S(1)}) fusion(f32[1,32,2048]{2,1,0:T(8,128)S(1)} %copy-done, f32[]{:T(128)} %bitcast.20, f32[2,32,2048]{2,1,0:T(8,128)S(1)} %fusion.329, f32[]{:T(128)} %bitcast.19, f32[]{:T(128)} %bitcast.18, ...), kind=kLoop, calls=%fused_computation.885 | loop fusion | flops 4325376 | bytes 5242948 | tf_op jit(solution)/shard_map/sub | solution.py:71
  91.3 8.0 %collective-permute-done.14 = f32[2,32,2048]{2,1,0:T(8,128)S(1)} collective-permute-done((f32[2,32,2048]{2,1,0:T(8,128)S(1)}, f32[2,32,2048]{2,1,0:T(8,128)S(1)}, u32[]{:S(2)}, u32[]{:S(2)}) %collective-permute-start.14) | collective-permute-done | bytes 524320 | tf_op jit(solution)/shard_map/ppermute | solution.py:25
  101.3 6.3 collective-permute-start.16
  111.9 6.0 collective-permute-start.18
  122.0 5.8 collective-permute-start.20
  132.1 5.8 collective-permute-start.22
  142.2 5.8 collective-permute-start.24
  152.3 5.8 collective-permute-start.26
  162.4 5.8 collective-permute-start.28
  170.6 12.2 %multiply_subtract_fusion.8 = (f32[1,32,2048]{2,1,0:T(8,128)S(1)}, f32[1,32,2048]{2,1,0:T(8,128)S(1)}, f32[1,32,2048]{2,1,0:T(8,128)S(1)}) fusion(f32[1,32,2048]{2,1,0:T(8,128)S(1)} %copy-done, f32[]{:T(128)} %bitcast.40, f32[2,32,2048]{2,1,0:T(8,128)S(1)} %fusion.275, f32[]{:T(128)} %bitcast.39, f32[]{:T(128)} %bitcast.38, f32[2,32,2048]{2,1,0:T(8,128)S(1)} %fusion.283, ...), kind=kLoop, calls=%fused_computation.881 | loop fusion | flops 4325376 | bytes 5242948 | tf_op jit(solution)/shard_map/sub | solution.py:71
  188.6 7.4 %collective-permute-done.29 = f32[2,32,2048]{2,1,0:T(8,128)S(1)} collective-permute-done((f32[2,32,2048]{2,1,0:T(8,128)S(1)}, f32[2,32,2048]{2,1,0:T(8,128)S(1)}, u32[]{:S(2)}, u32[]{:S(2)}) %collective-permute-start.29) | collective-permute-done | bytes 524320 | tf_op jit(solution)/shard_map/ppermute | solution.py:25
  198.0 6.9 %collective-permute-start.31 = (f32[2,1,2048]{2,1,0:T(1,128)S(1)}, f32[2,1,2048]{2,1,0:T(1,128)S(1)}, u32[]{:S(2)}, u32[]{:S(2)}) collective-permute-start(f32[2,1,2048]{2,1,0:T(1,128)S(1)} %get-tuple-element.176), channel_id=1, source_target_pairs={{1,0},{2,1},{3,2},{4,3},{5,4},{6,5},{7,6},{8,7},{9,8},{10,9},{11,1... | collective-permute-start | bytes 49160 | tf_op jit(solution)/shard_map/ppermute | solution.py:17
  209.2 5.8 collective-permute-start.33
  219.3 5.8 collective-permute-start.35
  229.4 6.2 collective-permute-start.37
  239.5 5.8 collective-permute-start.39
  249.6 5.8 collective-permute-start.41
  259.7 5.8 collective-permute-start.43
  267.9 12.1 %multiply_subtract_fusion.6 = (f32[1,32,2048]{2,1,0:T(8,128)S(1)}, f32[1,32,2048]{2,1,0:T(8,128)S(1)}, f32[1,32,2048]{2,1,0:T(8,128)S(1)}) fusion(f32[1,32,2048]{2,1,0:T(8,128)S(1)} %copy-done, f32[]{:T(128)} %bitcast.59, f32[2,32,2048]{2,1,0:T(8,128)S(1)} %fusion.221, f32[]{:T(128)} %bitcast.58, f32[]{:T(128)} %bitcast.57, f32[2,32,2048]{2,1,0:T(8,128)S(1)} %fusion.229, ...), kind=kLoop, calls=%fused_computation.877 | loop fusion | flops 4325376 | bytes 5242948 | tf_op jit(solution)/shard_map/sub | solution.py:71
  281.7 4.1 collective-permute-start.44
  285.8 7.4 %collective-permute-done.44 = f32[2,32,2048]{2,1,0:T(8,128)S(1)} collective-permute-done((f32[2,32,2048]{2,1,0:T(8,128)S(1)}, f32[2,32,2048]{2,1,0:T(8,128)S(1)}, u32[]{:S(2)}, u32[]{:S(2)}) %collective-permute-start.44) | collective-permute-done | bytes 524320 | tf_op jit(solution)/shard_map/ppermute | solution.py:25
  295.2 6.9 %collective-permute-start.46 = (f32[2,1,2048]{2,1,0:T(1,128)S(1)}, f32[2,1,2048]{2,1,0:T(1,128)S(1)}, u32[]{:S(2)}, u32[]{:S(2)}) collective-permute-start(f32[2,1,2048]{2,1,0:T(1,128)S(1)} %get-tuple-element.162), channel_id=1, source_target_pairs={{1,0},{2,1},{3,2},{4,3},{5,4},{6,5},{7,6},{8,7},{9,8},{10,9},{11,1... | collective-permute-start | bytes 49160 | tf_op jit(solution)/shard_map/ppermute | solution.py:17
  306.5 5.8 collective-permute-start.48
  316.6 5.8 collective-permute-start.50
  326.7 5.8 collective-permute-start.52
  336.8 5.8 collective-permute-start.54
  346.9 5.9 collective-permute-start.56
  357.0 5.8 collective-permute-start.58
  365.1 12.2 %multiply_subtract_fusion.4 = (f32[1,32,2048]{2,1,0:T(8,128)S(1)}, f32[1,32,2048]{2,1,0:T(8,128)S(1)}, f32[1,32,2048]{2,1,0:T(8,128)S(1)}) fusion(f32[1,32,2048]{2,1,0:T(8,128)S(1)} %copy-done, f32[]{:T(128)} %bitcast.78, f32[2,32,2048]{2,1,0:T(8,128)S(1)} %fusion.167, f32[]{:T(128)} %bitcast.77, f32[]{:T(128)} %bitcast.76, f32[2,32,2048]{2,1,0:T(8,128)S(1)} %fusion.175, ...), kind=kLoop, calls=%fused_computation.873 | loop fusion | flops 4325376 | bytes 5242948 | tf_op jit(solution)/shard_map/sub | solution.py:71
  383.1 7.4 %collective-permute-done.59 = f32[2,32,2048]{2,1,0:T(8,128)S(1)} collective-permute-done((f32[2,32,2048]{2,1,0:T(8,128)S(1)}, f32[2,32,2048]{2,1,0:T(8,128)S(1)}, u32[]{:S(2)}, u32[]{:S(2)}) %collective-permute-start.59) | collective-permute-done | bytes 524320 | tf_op jit(solution)/shard_map/ppermute | solution.py:25
  392.5 6.9 %collective-permute-start.61 = (f32[2,1,2048]{2,1,0:T(1,128)S(1)}, f32[2,1,2048]{2,1,0:T(1,128)S(1)}, u32[]{:S(2)}, u32[]{:S(2)}) collective-permute-start(f32[2,1,2048]{2,1,0:T(1,128)S(1)} %get-tuple-element.148), channel_id=1, source_target_pairs={{1,0},{2,1},{3,2},{4,3},{5,4},{6,5},{7,6},{8,7},{9,8},{10,9},{11,1... | collective-permute-start | bytes 49160 | tf_op jit(solution)/shard_map/ppermute | solution.py:17
  403.8 5.8 collective-permute-start.63
  413.9 5.8 collective-permute-start.65
  424.0 5.8 collective-permute-start.67
  434.1 5.8 collective-permute-start.69
  444.2 5.8 collective-permute-start.71
  454.3 6.0 collective-permute-start.73
  462.4 12.1 %multiply_subtract_fusion.2 = (f32[1,32,2048]{2,1,0:T(8,128)S(1)}, f32[1,32,2048]{2,1,0:T(8,128)S(1)}, f32[1,32,2048]{2,1,0:T(8,128)S(1)}) fusion(f32[1,32,2048]{2,1,0:T(8,128)S(1)} %copy-done, f32[]{:T(128)} %bitcast.97, f32[2,32,2048]{2,1,0:T(8,128)S(1)} %fusion.113, f32[]{:T(128)} %bitcast.96, f32[]{:T(128)} %bitcast.95, f32[2,32,2048]{2,1,0:T(8,128)S(1)} %fusion.121, ...), kind=kLoop, calls=%fused_computation.869 | loop fusion | flops 4325376 | bytes 5242948 | tf_op jit(solution)/shard_map/sub | solution.py:71
  480.4 7.5 %collective-permute-done.74 = f32[2,32,2048]{2,1,0:T(8,128)S(1)} collective-permute-done((f32[2,32,2048]{2,1,0:T(8,128)S(1)}, f32[2,32,2048]{2,1,0:T(8,128)S(1)}, u32[]{:S(2)}, u32[]{:S(2)}) %collective-permute-start.74) | collective-permute-done | bytes 524320 | tf_op jit(solution)/shard_map/ppermute | solution.py:25
  490.0 6.8 %collective-permute-start.76 = (f32[2,1,2048]{2,1,0:T(1,128)S(1)}, f32[2,1,2048]{2,1,0:T(1,128)S(1)}, u32[]{:S(2)}, u32[]{:S(2)}) collective-permute-start(f32[2,1,2048]{2,1,0:T(1,128)S(1)} %get-tuple-element.134), channel_id=1, source_target_pairs={{1,0},{2,1},{3,2},{4,3},{5,4},{6,5},{7,6},{8,7},{9,8},{10,9},{11,1... | collective-permute-start | bytes 49160 | tf_op jit(solution)/shard_map/ppermute | solution.py:17
  501.1 5.8 collective-permute-start.78
  511.2 5.8 collective-permute-start.80
  521.3 5.8 collective-permute-start.82
  531.4 5.8 collective-permute-start.84
  541.5 5.8 collective-permute-start.86
  551.6 5.8 collective-permute-start.88
  559.8 12.2 %multiply_subtract_fusion = (f32[1,32,2048]{2,1,0:T(8,128)S(1)}, f32[1,32,2048]{2,1,0:T(8,128)S(1)}, f32[1,32,2048]{2,1,0:T(8,128)S(1)}) fusion(f32[1,32,2048]{2,1,0:T(8,128)S(1)} %copy-done, f32[]{:T(128)} %bitcast.116, f32[2,32,2048]{2,1,0:T(8,128)S(1)} %fusion.59, f32[]{:T(128)} %bitcast.115, f32[]{:T(128)} %bitcast.114, f32[2,32,2048]{2,1,0:T(8,128)S(1)} %fusion.67, ...), kind=kLoop, calls=%fused_computation.865 | loop fusion | flops 4325376 | bytes 5242948 | tf_op jit(solution)/shard_map/sub | solution.py:71
  573.7 4.4 collective-permute-start.89
  578.1 7.1 %collective-permute-done.89 = f32[2,32,2048]{2,1,0:T(8,128)S(1)} collective-permute-done((f32[2,32,2048]{2,1,0:T(8,128)S(1)}, f32[2,32,2048]{2,1,0:T(8,128)S(1)}, u32[]{:S(2)}, u32[]{:S(2)}) %collective-permute-start.89) | collective-permute-done | bytes 524320 | tf_op jit(solution)/shard_map/ppermute | solution.py:25
  587.2 6.9 %collective-permute-start.91 = (f32[2,1,2048]{2,1,0:T(1,128)S(1)}, f32[2,1,2048]{2,1,0:T(1,128)S(1)}, u32[]{:S(2)}, u32[]{:S(2)}) collective-permute-start(f32[2,1,2048]{2,1,0:T(1,128)S(1)} %get-tuple-element.120), channel_id=1, source_target_pairs={{1,0},{2,1},{3,2},{4,3},{5,4},{6,5},{7,6},{8,7},{9,8},{10,9},{11,1... | collective-permute-start | bytes 49160 | tf_op jit(solution)/shard_map/ppermute | solution.py:17
  598.5 5.8 collective-permute-start.93
  608.5 5.8 collective-permute-start.95
  618.6 5.8 collective-permute-start.97
  628.8 5.8 collective-permute-start.99
  638.9 5.8 collective-permute-start.101
  649.8 5.8 collective-permute-start.103
  660.6 12.9 %select_add_fusion = f32[1,32,2048]{2,1,0:T(8,128)} fusion(f32[1,32,2048]{2,1,0:T(8,128)S(1)} %copy-done, f32[2,32,2048]{2,1,0:T(8,128)S(1)} %fusion.5, f32[2,32,2048]{2,1,0:T(8,128)S(1)} %copy-done.4, f32[2,32,2048]{2,1,0:T(8,128)S(1)} %fusion.21, f32[2,32,2048]{2,1,0:T(8,128)S(1)} %fusion.29, f32[2,32,2048]{2,1,0:T(8,128)S(1)} %fusion.37, ...), kind=kLoop, calls=%fused_computation.863 | loop fusion | flops 5177344 | bytes 6291531 | tf_op jit(solution)/shard_map/add | solution.py:91
  (365 shorter events, 241.2 us)
Async XLA Ops:
  1.2 9.4 %collective-permute-start = (f32[2,1,2048]{2,1,0:T(1,128)S(1)}, f32[2,1,2048]{2,1,0:T(1,128)S(1)}, u32[]{:S(2)}, u32[]{:S(2)}) collective-permute-start(f32[2,1,2048]{2,1,0:T(1,128)S(1)} %get-tuple-element.203), channel_id=1, source_target_pairs={{0,1},{1,2},{2,3},{3,4},{4,5},{5,6},{6,7},{7,8},{8,9},{9,10},{10,1... | collective-permute-start | bytes 49160 | tf_op jit(solution)/shard_map/ppermute | solution.py:14
  3.1 8.9 %collective-permute-start.1 = (f32[2,1,2048]{2,1,0:T(1,128)S(1)}, f32[2,1,2048]{2,1,0:T(1,128)S(1)}, u32[]{:S(2)}, u32[]{:S(2)}) collective-permute-start(f32[2,1,2048]{2,1,0:T(1,128)S(1)} %get-tuple-element.204), channel_id=1, source_target_pairs={{1,0},{2,1},{3,2},{4,3},{5,4},{6,5},{7,6},{8,7},{9,8},{10,9},{11,1... | collective-permute-start | bytes 49160 | tf_op jit(solution)/shard_map/ppermute | solution.py:17
  13.0 7.7 %collective-permute-start.2 = (f32[2,1,2048]{2,1,0:T(1,128)S(1)}, f32[2,1,2048]{2,1,0:T(1,128)S(1)}, u32[]{:S(2)}, u32[]{:S(2)}) collective-permute-start(f32[2,1,2048]{2,1,0:T(1,128)S(1)} %get-tuple-element.201), channel_id=1, source_target_pairs={{0,1},{1,2},{2,3},{3,4},{4,5},{5,6},{6,7},{7,8},{8,9},{9,10},{10,1... | collective-permute-start | bytes 49160 | tf_op jit(solution)/shard_map/ppermute | solution.py:14
  23.1 7.7 %collective-permute-start.4 = (f32[2,1,2048]{2,1,0:T(1,128)S(1)}, f32[2,1,2048]{2,1,0:T(1,128)S(1)}, u32[]{:S(2)}, u32[]{:S(2)}) collective-permute-start(f32[2,1,2048]{2,1,0:T(1,128)S(1)} %get-tuple-element.199), channel_id=1, source_target_pairs={{0,1},{1,2},{2,3},{3,4},{4,5},{5,6},{6,7},{7,8},{8,9},{9,10},{10,1... | collective-permute-start | bytes 49160 | tf_op jit(solution)/shard_map/ppermute | solution.py:14
  33.2 7.7 %collective-permute-start.6 = (f32[2,1,2048]{2,1,0:T(1,128)S(1)}, f32[2,1,2048]{2,1,0:T(1,128)S(1)}, u32[]{:S(2)}, u32[]{:S(2)}) collective-permute-start(f32[2,1,2048]{2,1,0:T(1,128)S(1)} %get-tuple-element.197), channel_id=1, source_target_pairs={{0,1},{1,2},{2,3},{3,4},{4,5},{5,6},{6,7},{7,8},{8,9},{9,10},{10,1... | collective-permute-start | bytes 49160 | tf_op jit(solution)/shard_map/ppermute | solution.py:14
  35.1 7.2 %collective-permute-start.7 = (f32[2,1,2048]{2,1,0:T(1,128)S(1)}, f32[2,1,2048]{2,1,0:T(1,128)S(1)}, u32[]{:S(2)}, u32[]{:S(2)}) collective-permute-start(f32[2,1,2048]{2,1,0:T(1,128)S(1)} %get-tuple-element.198), channel_id=1, source_target_pairs={{1,0},{2,1},{3,2},{4,3},{5,4},{6,5},{7,6},{8,7},{9,8},{10,9},{11,1... | collective-permute-start | bytes 49160 | tf_op jit(solution)/shard_map/ppermute | solution.py:17
  43.3 7.8 %collective-permute-start.8 = (f32[2,1,2048]{2,1,0:T(1,128)S(1)}, f32[2,1,2048]{2,1,0:T(1,128)S(1)}, u32[]{:S(2)}, u32[]{:S(2)}) collective-permute-start(f32[2,1,2048]{2,1,0:T(1,128)S(1)} %get-tuple-element.195), channel_id=1, source_target_pairs={{0,1},{1,2},{2,3},{3,4},{4,5},{5,6},{6,7},{7,8},{8,9},{9,10},{10,1... | collective-permute-start | bytes 49160 | tf_op jit(solution)/shard_map/ppermute | solution.py:14
  53.4 7.7 %collective-permute-start.10 = (f32[2,1,2048]{2,1,0:T(1,128)S(1)}, f32[2,1,2048]{2,1,0:T(1,128)S(1)}, u32[]{:S(2)}, u32[]{:S(2)}) collective-permute-start(f32[2,1,2048]{2,1,0:T(1,128)S(1)} %get-tuple-element.193), channel_id=1, source_target_pairs={{0,1},{1,2},{2,3},{3,4},{4,5},{5,6},{6,7},{7,8},{8,9},{9,10},{10,1... | collective-permute-start | bytes 49160 | tf_op jit(solution)/shard_map/ppermute | solution.py:14
  63.5 9.1 %collective-permute-start.12 = (f32[2,1,2048]{2,1,0:T(1,128)S(1)}, f32[2,1,2048]{2,1,0:T(1,128)S(1)}, u32[]{:S(2)}, u32[]{:S(2)}) collective-permute-start(f32[2,1,2048]{2,1,0:T(1,128)S(1)} %get-tuple-element.191), channel_id=1, source_target_pairs={{0,1},{1,2},{2,3},{3,4},{4,5},{5,6},{6,7},{7,8},{8,9},{9,10},{10,1... | collective-permute-start | bytes 49160 | tf_op jit(solution)/shard_map/ppermute | solution.py:14
  65.5 7.2 %collective-permute-start.13 = (f32[2,1,2048]{2,1,0:T(1,128)S(1)}, f32[2,1,2048]{2,1,0:T(1,128)S(1)}, u32[]{:S(2)}, u32[]{:S(2)}) collective-permute-start(f32[2,1,2048]{2,1,0:T(1,128)S(1)} %get-tuple-element.192), channel_id=1, source_target_pairs={{1,0},{2,1},{3,2},{4,3},{5,4},{6,5},{7,6},{8,7},{9,8},{10,9},{11,1... | collective-permute-start | bytes 49160 | tf_op jit(solution)/shard_map/ppermute | solution.py:17
  87.8 11.5 %collective-permute-start.14 = (f32[2,32,2048]{2,1,0:T(8,128)S(1)}, f32[2,32,2048]{2,1,0:T(8,128)S(1)}, u32[]{:S(2)}, u32[]{:S(2)}) collective-permute-start(f32[2,32,2048]{2,1,0:T(8,128)S(1)} %pad_maximum_fusion.98), channel_id=1, source_target_pairs={{0,64},{64,128},{128,192},{1,65},{65,129},{129,193},{2,66},{66,130... | collective-permute-start | bytes 1572872 | tf_op jit(solution)/shard_map/ppermute | solution.py:25
  99.3 8.3 %collective-permute-start.15 = (f32[2,1,2048]{2,1,0:T(1,128)S(1)}, f32[2,1,2048]{2,1,0:T(1,128)S(1)}, u32[]{:S(2)}, u32[]{:S(2)}) collective-permute-start(f32[2,1,2048]{2,1,0:T(1,128)S(1)} %get-tuple-element.189), channel_id=1, source_target_pairs={{0,1},{1,2},{2,3},{3,4},{4,5},{5,6},{6,7},{7,8},{8,9},{9,10},{10,1... | collective-permute-start | bytes 49160 | tf_op jit(solution)/shard_map/ppermute | solution.py:14
  101.3 7.7 %collective-permute-start.16 = (f32[2,1,2048]{2,1,0:T(1,128)S(1)}, f32[2,1,2048]{2,1,0:T(1,128)S(1)}, u32[]{:S(2)}, u32[]{:S(2)}) collective-permute-start(f32[2,1,2048]{2,1,0:T(1,128)S(1)} %get-tuple-element.190), channel_id=1, source_target_pairs={{1,0},{2,1},{3,2},{4,3},{5,4},{6,5},{7,6},{8,7},{9,8},{10,9},{11,1... | collective-permute-start | bytes 49160 | tf_op jit(solution)/shard_map/ppermute | solution.py:17
  110.0 7.9 %collective-permute-start.17 = (f32[2,1,2048]{2,1,0:T(1,128)S(1)}, f32[2,1,2048]{2,1,0:T(1,128)S(1)}, u32[]{:S(2)}, u32[]{:S(2)}) collective-permute-start(f32[2,1,2048]{2,1,0:T(1,128)S(1)} %get-tuple-element.187), channel_id=1, source_target_pairs={{0,1},{1,2},{2,3},{3,4},{4,5},{5,6},{6,7},{7,8},{8,9},{9,10},{10,1... | collective-permute-start | bytes 49160 | tf_op jit(solution)/shard_map/ppermute | solution.py:14
  120.1 7.7 %collective-permute-start.19 = (f32[2,1,2048]{2,1,0:T(1,128)S(1)}, f32[2,1,2048]{2,1,0:T(1,128)S(1)}, u32[]{:S(2)}, u32[]{:S(2)}) collective-permute-start(f32[2,1,2048]{2,1,0:T(1,128)S(1)} %get-tuple-element.185), channel_id=1, source_target_pairs={{0,1},{1,2},{2,3},{3,4},{4,5},{5,6},{6,7},{7,8},{8,9},{9,10},{10,1... | collective-permute-start | bytes 49160 | tf_op jit(solution)/shard_map/ppermute | solution.py:14
  130.2 7.7 %collective-permute-start.21 = (f32[2,1,2048]{2,1,0:T(1,128)S(1)}, f32[2,1,2048]{2,1,0:T(1,128)S(1)}, u32[]{:S(2)}, u32[]{:S(2)}) collective-permute-start(f32[2,1,2048]{2,1,0:T(1,128)S(1)} %get-tuple-element.183), channel_id=1, source_target_pairs={{0,1},{1,2},{2,3},{3,4},{4,5},{5,6},{6,7},{7,8},{8,9},{9,10},{10,1... | collective-permute-start | bytes 49160 | tf_op jit(solution)/shard_map/ppermute | solution.py:14
  140.3 7.7 %collective-permute-start.23 = (f32[2,1,2048]{2,1,0:T(1,128)S(1)}, f32[2,1,2048]{2,1,0:T(1,128)S(1)}, u32[]{:S(2)}, u32[]{:S(2)}) collective-permute-start(f32[2,1,2048]{2,1,0:T(1,128)S(1)} %get-tuple-element.181), channel_id=1, source_target_pairs={{0,1},{1,2},{2,3},{3,4},{4,5},{5,6},{6,7},{7,8},{8,9},{9,10},{10,1... | collective-permute-start | bytes 49160 | tf_op jit(solution)/shard_map/ppermute | solution.py:14
  150.4 7.7 %collective-permute-start.25 = (f32[2,1,2048]{2,1,0:T(1,128)S(1)}, f32[2,1,2048]{2,1,0:T(1,128)S(1)}, u32[]{:S(2)}, u32[]{:S(2)}) collective-permute-start(f32[2,1,2048]{2,1,0:T(1,128)S(1)} %get-tuple-element.179), channel_id=1, source_target_pairs={{0,1},{1,2},{2,3},{3,4},{4,5},{5,6},{6,7},{7,8},{8,9},{9,10},{10,1... | collective-permute-start | bytes 49160 | tf_op jit(solution)/shard_map/ppermute | solution.py:14
  160.5 8.4 %collective-permute-start.27 = (f32[2,1,2048]{2,1,0:T(1,128)S(1)}, f32[2,1,2048]{2,1,0:T(1,128)S(1)}, u32[]{:S(2)}, u32[]{:S(2)}) collective-permute-start(f32[2,1,2048]{2,1,0:T(1,128)S(1)} %get-tuple-element.177), channel_id=1, source_target_pairs={{0,1},{1,2},{2,3},{3,4},{4,5},{5,6},{6,7},{7,8},{8,9},{9,10},{10,1... | collective-permute-start | bytes 49160 | tf_op jit(solution)/shard_map/ppermute | solution.py:14
  184.4 11.5 %collective-permute-start.29 = (f32[2,32,2048]{2,1,0:T(8,128)S(1)}, f32[2,32,2048]{2,1,0:T(8,128)S(1)}, u32[]{:S(2)}, u32[]{:S(2)}) collective-permute-start(f32[2,32,2048]{2,1,0:T(8,128)S(1)} %pad_maximum_fusion.99), channel_id=1, source_target_pairs={{0,64},{64,128},{128,192},{1,65},{65,129},{129,193},{2,66},{66,130... | collective-permute-start | bytes 1572872 | tf_op jit(solution)/shard_map/ppermute | solution.py:25
  196.0 8.9 %collective-permute-start.30 = (f32[2,1,2048]{2,1,0:T(1,128)S(1)}, f32[2,1,2048]{2,1,0:T(1,128)S(1)}, u32[]{:S(2)}, u32[]{:S(2)}) collective-permute-start(f32[2,1,2048]{2,1,0:T(1,128)S(1)} %get-tuple-element.175), channel_id=1, source_target_pairs={{0,1},{1,2},{2,3},{3,4},{4,5},{5,6},{6,7},{7,8},{8,9},{9,10},{10,1... | collective-permute-start | bytes 49160 | tf_op jit(solution)/shard_map/ppermute | solution.py:14
  198.0 8.3 %collective-permute-start.31 = (f32[2,1,2048]{2,1,0:T(1,128)S(1)}, f32[2,1,2048]{2,1,0:T(1,128)S(1)}, u32[]{:S(2)}, u32[]{:S(2)}) collective-permute-start(f32[2,1,2048]{2,1,0:T(1,128)S(1)} %get-tuple-element.176), channel_id=1, source_target_pairs={{1,0},{2,1},{3,2},{4,3},{5,4},{6,5},{7,6},{8,7},{9,8},{10,9},{11,1... | collective-permute-start | bytes 49160 | tf_op jit(solution)/shard_map/ppermute | solution.py:17
  207.3 7.7 %collective-permute-start.32 = (f32[2,1,2048]{2,1,0:T(1,128)S(1)}, f32[2,1,2048]{2,1,0:T(1,128)S(1)}, u32[]{:S(2)}, u32[]{:S(2)}) collective-permute-start(f32[2,1,2048]{2,1,0:T(1,128)S(1)} %get-tuple-element.173), channel_id=1, source_target_pairs={{0,1},{1,2},{2,3},{3,4},{4,5},{5,6},{6,7},{7,8},{8,9},{9,10},{10,1... | collective-permute-start | bytes 49160 | tf_op jit(solution)/shard_map/ppermute | solution.py:14
  217.4 7.7 %collective-permute-start.34 = (f32[2,1,2048]{2,1,0:T(1,128)S(1)}, f32[2,1,2048]{2,1,0:T(1,128)S(1)}, u32[]{:S(2)}, u32[]{:S(2)}) collective-permute-start(f32[2,1,2048]{2,1,0:T(1,128)S(1)} %get-tuple-element.171), channel_id=1, source_target_pairs={{0,1},{1,2},{2,3},{3,4},{4,5},{5,6},{6,7},{7,8},{8,9},{9,10},{10,1... | collective-permute-start | bytes 49160 | tf_op jit(solution)/shard_map/ppermute | solution.py:14
  227.5 8.1 %collective-permute-start.36 = (f32[2,1,2048]{2,1,0:T(1,128)S(1)}, f32[2,1,2048]{2,1,0:T(1,128)S(1)}, u32[]{:S(2)}, u32[]{:S(2)}) collective-permute-start(f32[2,1,2048]{2,1,0:T(1,128)S(1)} %get-tuple-element.169), channel_id=1, source_target_pairs={{0,1},{1,2},{2,3},{3,4},{4,5},{5,6},{6,7},{7,8},{8,9},{9,10},{10,1... | collective-permute-start | bytes 49160 | tf_op jit(solution)/shard_map/ppermute | solution.py:14
  237.6 7.7 %collective-permute-start.38 = (f32[2,1,2048]{2,1,0:T(1,128)S(1)}, f32[2,1,2048]{2,1,0:T(1,128)S(1)}, u32[]{:S(2)}, u32[]{:S(2)}) collective-permute-start(f32[2,1,2048]{2,1,0:T(1,128)S(1)} %get-tuple-element.167), channel_id=1, source_target_pairs={{0,1},{1,2},{2,3},{3,4},{4,5},{5,6},{6,7},{7,8},{8,9},{9,10},{10,1... | collective-permute-start | bytes 49160 | tf_op jit(solution)/shard_map/ppermute | solution.py:14
  247.7 7.7 %collective-permute-start.40 = (f32[2,1,2048]{2,1,0:T(1,128)S(1)}, f32[2,1,2048]{2,1,0:T(1,128)S(1)}, u32[]{:S(2)}, u32[]{:S(2)}) collective-permute-start(f32[2,1,2048]{2,1,0:T(1,128)S(1)} %get-tuple-element.165), channel_id=1, source_target_pairs={{0,1},{1,2},{2,3},{3,4},{4,5},{5,6},{6,7},{7,8},{8,9},{9,10},{10,1... | collective-permute-start | bytes 49160 | tf_op jit(solution)/shard_map/ppermute | solution.py:14
  257.8 8.4 %collective-permute-start.42 = (f32[2,1,2048]{2,1,0:T(1,128)S(1)}, f32[2,1,2048]{2,1,0:T(1,128)S(1)}, u32[]{:S(2)}, u32[]{:S(2)}) collective-permute-start(f32[2,1,2048]{2,1,0:T(1,128)S(1)} %get-tuple-element.163), channel_id=1, source_target_pairs={{0,1},{1,2},{2,3},{3,4},{4,5},{5,6},{6,7},{7,8},{8,9},{9,10},{10,1... | collective-permute-start | bytes 49160 | tf_op jit(solution)/shard_map/ppermute | solution.py:14
  281.7 11.5 %collective-permute-start.44 = (f32[2,32,2048]{2,1,0:T(8,128)S(1)}, f32[2,32,2048]{2,1,0:T(8,128)S(1)}, u32[]{:S(2)}, u32[]{:S(2)}) collective-permute-start(f32[2,32,2048]{2,1,0:T(8,128)S(1)} %pad_maximum_fusion.100), channel_id=1, source_target_pairs={{0,64},{64,128},{128,192},{1,65},{65,129},{129,193},{2,66},{66,130... | collective-permute-start | bytes 1572872 | tf_op jit(solution)/shard_map/ppermute | solution.py:25
  293.3 8.9 %collective-permute-start.45 = (f32[2,1,2048]{2,1,0:T(1,128)S(1)}, f32[2,1,2048]{2,1,0:T(1,128)S(1)}, u32[]{:S(2)}, u32[]{:S(2)}) collective-permute-start(f32[2,1,2048]{2,1,0:T(1,128)S(1)} %get-tuple-element.161), channel_id=1, source_target_pairs={{0,1},{1,2},{2,3},{3,4},{4,5},{5,6},{6,7},{7,8},{8,9},{9,10},{10,1... | collective-permute-start | bytes 49160 | tf_op jit(solution)/shard_map/ppermute | solution.py:14
  295.2 8.3 %collective-permute-start.46 = (f32[2,1,2048]{2,1,0:T(1,128)S(1)}, f32[2,1,2048]{2,1,0:T(1,128)S(1)}, u32[]{:S(2)}, u32[]{:S(2)}) collective-permute-start(f32[2,1,2048]{2,1,0:T(1,128)S(1)} %get-tuple-element.162), channel_id=1, source_target_pairs={{1,0},{2,1},{3,2},{4,3},{5,4},{6,5},{7,6},{8,7},{9,8},{10,9},{11,1... | collective-permute-start | bytes 49160 | tf_op jit(solution)/shard_map/ppermute | solution.py:17
  304.6 7.7 %collective-permute-start.47 = (f32[2,1,2048]{2,1,0:T(1,128)S(1)}, f32[2,1,2048]{2,1,0:T(1,128)S(1)}, u32[]{:S(2)}, u32[]{:S(2)}) collective-permute-start(f32[2,1,2048]{2,1,0:T(1,128)S(1)} %get-tuple-element.159), channel_id=1, source_target_pairs={{0,1},{1,2},{2,3},{3,4},{4,5},{5,6},{6,7},{7,8},{8,9},{9,10},{10,1... | collective-permute-start | bytes 49160 | tf_op jit(solution)/shard_map/ppermute | solution.py:14
  314.7 7.7 %collective-permute-start.49 = (f32[2,1,2048]{2,1,0:T(1,128)S(1)}, f32[2,1,2048]{2,1,0:T(1,128)S(1)}, u32[]{:S(2)}, u32[]{:S(2)}) collective-permute-start(f32[2,1,2048]{2,1,0:T(1,128)S(1)} %get-tuple-element.157), channel_id=1, source_target_pairs={{0,1},{1,2},{2,3},{3,4},{4,5},{5,6},{6,7},{7,8},{8,9},{9,10},{10,1... | collective-permute-start | bytes 49160 | tf_op jit(solution)/shard_map/ppermute | solution.py:14
  324.8 7.7 %collective-permute-start.51 = (f32[2,1,2048]{2,1,0:T(1,128)S(1)}, f32[2,1,2048]{2,1,0:T(1,128)S(1)}, u32[]{:S(2)}, u32[]{:S(2)}) collective-permute-start(f32[2,1,2048]{2,1,0:T(1,128)S(1)} %get-tuple-element.155), channel_id=1, source_target_pairs={{0,1},{1,2},{2,3},{3,4},{4,5},{5,6},{6,7},{7,8},{8,9},{9,10},{10,1... | collective-permute-start | bytes 49160 | tf_op jit(solution)/shard_map/ppermute | solution.py:14
  334.9 7.7 %collective-permute-start.53 = (f32[2,1,2048]{2,1,0:T(1,128)S(1)}, f32[2,1,2048]{2,1,0:T(1,128)S(1)}, u32[]{:S(2)}, u32[]{:S(2)}) collective-permute-start(f32[2,1,2048]{2,1,0:T(1,128)S(1)} %get-tuple-element.153), channel_id=1, source_target_pairs={{0,1},{1,2},{2,3},{3,4},{4,5},{5,6},{6,7},{7,8},{8,9},{9,10},{10,1... | collective-permute-start | bytes 49160 | tf_op jit(solution)/shard_map/ppermute | solution.py:14
  345.0 7.9 %collective-permute-start.55 = (f32[2,1,2048]{2,1,0:T(1,128)S(1)}, f32[2,1,2048]{2,1,0:T(1,128)S(1)}, u32[]{:S(2)}, u32[]{:S(2)}) collective-permute-start(f32[2,1,2048]{2,1,0:T(1,128)S(1)} %get-tuple-element.151), channel_id=1, source_target_pairs={{0,1},{1,2},{2,3},{3,4},{4,5},{5,6},{6,7},{7,8},{8,9},{9,10},{10,1... | collective-permute-start | bytes 49160 | tf_op jit(solution)/shard_map/ppermute | solution.py:14
  355.1 8.4 %collective-permute-start.57 = (f32[2,1,2048]{2,1,0:T(1,128)S(1)}, f32[2,1,2048]{2,1,0:T(1,128)S(1)}, u32[]{:S(2)}, u32[]{:S(2)}) collective-permute-start(f32[2,1,2048]{2,1,0:T(1,128)S(1)} %get-tuple-element.149), channel_id=1, source_target_pairs={{0,1},{1,2},{2,3},{3,4},{4,5},{5,6},{6,7},{7,8},{8,9},{9,10},{10,1... | collective-permute-start | bytes 49160 | tf_op jit(solution)/shard_map/ppermute | solution.py:14
  379.0 11.5 %collective-permute-start.59 = (f32[2,32,2048]{2,1,0:T(8,128)S(1)}, f32[2,32,2048]{2,1,0:T(8,128)S(1)}, u32[]{:S(2)}, u32[]{:S(2)}) collective-permute-start(f32[2,32,2048]{2,1,0:T(8,128)S(1)} %pad_maximum_fusion.101), channel_id=1, source_target_pairs={{0,64},{64,128},{128,192},{1,65},{65,129},{129,193},{2,66},{66,130... | collective-permute-start | bytes 1572872 | tf_op jit(solution)/shard_map/ppermute | solution.py:25
  390.6 8.9 %collective-permute-start.60 = (f32[2,1,2048]{2,1,0:T(1,128)S(1)}, f32[2,1,2048]{2,1,0:T(1,128)S(1)}, u32[]{:S(2)}, u32[]{:S(2)}) collective-permute-start(f32[2,1,2048]{2,1,0:T(1,128)S(1)} %get-tuple-element.147), channel_id=1, source_target_pairs={{0,1},{1,2},{2,3},{3,4},{4,5},{5,6},{6,7},{7,8},{8,9},{9,10},{10,1... | collective-permute-start | bytes 49160 | tf_op jit(solution)/shard_map/ppermute | solution.py:14
  392.5 8.3 %collective-permute-start.61 = (f32[2,1,2048]{2,1,0:T(1,128)S(1)}, f32[2,1,2048]{2,1,0:T(1,128)S(1)}, u32[]{:S(2)}, u32[]{:S(2)}) collective-permute-start(f32[2,1,2048]{2,1,0:T(1,128)S(1)} %get-tuple-element.148), channel_id=1, source_target_pairs={{1,0},{2,1},{3,2},{4,3},{5,4},{6,5},{7,6},{8,7},{9,8},{10,9},{11,1... | collective-permute-start | bytes 49160 | tf_op jit(solution)/shard_map/ppermute | solution.py:17
  401.9 7.7 %collective-permute-start.62 = (f32[2,1,2048]{2,1,0:T(1,128)S(1)}, f32[2,1,2048]{2,1,0:T(1,128)S(1)}, u32[]{:S(2)}, u32[]{:S(2)}) collective-permute-start(f32[2,1,2048]{2,1,0:T(1,128)S(1)} %get-tuple-element.145), channel_id=1, source_target_pairs={{0,1},{1,2},{2,3},{3,4},{4,5},{5,6},{6,7},{7,8},{8,9},{9,10},{10,1... | collective-permute-start | bytes 49160 | tf_op jit(solution)/shard_map/ppermute | solution.py:14
  412.0 7.7 %collective-permute-start.64 = (f32[2,1,2048]{2,1,0:T(1,128)S(1)}, f32[2,1,2048]{2,1,0:T(1,128)S(1)}, u32[]{:S(2)}, u32[]{:S(2)}) collective-permute-start(f32[2,1,2048]{2,1,0:T(1,128)S(1)} %get-tuple-element.143), channel_id=1, source_target_pairs={{0,1},{1,2},{2,3},{3,4},{4,5},{5,6},{6,7},{7,8},{8,9},{9,10},{10,1... | collective-permute-start | bytes 49160 | tf_op jit(solution)/shard_map/ppermute | solution.py:14
  422.1 7.7 %collective-permute-start.66 = (f32[2,1,2048]{2,1,0:T(1,128)S(1)}, f32[2,1,2048]{2,1,0:T(1,128)S(1)}, u32[]{:S(2)}, u32[]{:S(2)}) collective-permute-start(f32[2,1,2048]{2,1,0:T(1,128)S(1)} %get-tuple-element.141), channel_id=1, source_target_pairs={{0,1},{1,2},{2,3},{3,4},{4,5},{5,6},{6,7},{7,8},{8,9},{9,10},{10,1... | collective-permute-start | bytes 49160 | tf_op jit(solution)/shard_map/ppermute | solution.py:14
  432.2 7.7 %collective-permute-start.68 = (f32[2,1,2048]{2,1,0:T(1,128)S(1)}, f32[2,1,2048]{2,1,0:T(1,128)S(1)}, u32[]{:S(2)}, u32[]{:S(2)}) collective-permute-start(f32[2,1,2048]{2,1,0:T(1,128)S(1)} %get-tuple-element.139), channel_id=1, source_target_pairs={{0,1},{1,2},{2,3},{3,4},{4,5},{5,6},{6,7},{7,8},{8,9},{9,10},{10,1... | collective-permute-start | bytes 49160 | tf_op jit(solution)/shard_map/ppermute | solution.py:14
  442.3 7.7 %collective-permute-start.70 = (f32[2,1,2048]{2,1,0:T(1,128)S(1)}, f32[2,1,2048]{2,1,0:T(1,128)S(1)}, u32[]{:S(2)}, u32[]{:S(2)}) collective-permute-start(f32[2,1,2048]{2,1,0:T(1,128)S(1)} %get-tuple-element.137), channel_id=1, source_target_pairs={{0,1},{1,2},{2,3},{3,4},{4,5},{5,6},{6,7},{7,8},{8,9},{9,10},{10,1... | collective-permute-start | bytes 49160 | tf_op jit(solution)/shard_map/ppermute | solution.py:14
  452.4 8.6 %collective-permute-start.72 = (f32[2,1,2048]{2,1,0:T(1,128)S(1)}, f32[2,1,2048]{2,1,0:T(1,128)S(1)}, u32[]{:S(2)}, u32[]{:S(2)}) collective-permute-start(f32[2,1,2048]{2,1,0:T(1,128)S(1)} %get-tuple-element.135), channel_id=1, source_target_pairs={{0,1},{1,2},{2,3},{3,4},{4,5},{5,6},{6,7},{7,8},{8,9},{9,10},{10,1... | collective-permute-start | bytes 49160 | tf_op jit(solution)/shard_map/ppermute | solution.py:14
  476.3 11.6 %collective-permute-start.74 = (f32[2,32,2048]{2,1,0:T(8,128)S(1)}, f32[2,32,2048]{2,1,0:T(8,128)S(1)}, u32[]{:S(2)}, u32[]{:S(2)}) collective-permute-start(f32[2,32,2048]{2,1,0:T(8,128)S(1)} %pad_maximum_fusion.102), channel_id=1, source_target_pairs={{0,64},{64,128},{128,192},{1,65},{65,129},{129,193},{2,66},{66,130... | collective-permute-start | bytes 1572872 | tf_op jit(solution)/shard_map/ppermute | solution.py:25
  488.0 8.7 %collective-permute-start.75 = (f32[2,1,2048]{2,1,0:T(1,128)S(1)}, f32[2,1,2048]{2,1,0:T(1,128)S(1)}, u32[]{:S(2)}, u32[]{:S(2)}) collective-permute-start(f32[2,1,2048]{2,1,0:T(1,128)S(1)} %get-tuple-element.133), channel_id=1, source_target_pairs={{0,1},{1,2},{2,3},{3,4},{4,5},{5,6},{6,7},{7,8},{8,9},{9,10},{10,1... | collective-permute-start | bytes 49160 | tf_op jit(solution)/shard_map/ppermute | solution.py:14
  490.0 8.2 %collective-permute-start.76 = (f32[2,1,2048]{2,1,0:T(1,128)S(1)}, f32[2,1,2048]{2,1,0:T(1,128)S(1)}, u32[]{:S(2)}, u32[]{:S(2)}) collective-permute-start(f32[2,1,2048]{2,1,0:T(1,128)S(1)} %get-tuple-element.134), channel_id=1, source_target_pairs={{1,0},{2,1},{3,2},{4,3},{5,4},{6,5},{7,6},{8,7},{9,8},{10,9},{11,1... | collective-permute-start | bytes 49160 | tf_op jit(solution)/shard_map/ppermute | solution.py:17
  499.2 7.7 %collective-permute-start.77 = (f32[2,1,2048]{2,1,0:T(1,128)S(1)}, f32[2,1,2048]{2,1,0:T(1,128)S(1)}, u32[]{:S(2)}, u32[]{:S(2)}) collective-permute-start(f32[2,1,2048]{2,1,0:T(1,128)S(1)} %get-tuple-element.131), channel_id=1, source_target_pairs={{0,1},{1,2},{2,3},{3,4},{4,5},{5,6},{6,7},{7,8},{8,9},{9,10},{10,1... | collective-permute-start | bytes 49160 | tf_op jit(solution)/shard_map/ppermute | solution.py:14
  509.3 7.7 %collective-permute-start.79 = (f32[2,1,2048]{2,1,0:T(1,128)S(1)}, f32[2,1,2048]{2,1,0:T(1,128)S(1)}, u32[]{:S(2)}, u32[]{:S(2)}) collective-permute-start(f32[2,1,2048]{2,1,0:T(1,128)S(1)} %get-tuple-element.129), channel_id=1, source_target_pairs={{0,1},{1,2},{2,3},{3,4},{4,5},{5,6},{6,7},{7,8},{8,9},{9,10},{10,1... | collective-permute-start | bytes 49160 | tf_op jit(solution)/shard_map/ppermute | solution.py:14
  519.4 7.7 %collective-permute-start.81 = (f32[2,1,2048]{2,1,0:T(1,128)S(1)}, f32[2,1,2048]{2,1,0:T(1,128)S(1)}, u32[]{:S(2)}, u32[]{:S(2)}) collective-permute-start(f32[2,1,2048]{2,1,0:T(1,128)S(1)} %get-tuple-element.127), channel_id=1, source_target_pairs={{0,1},{1,2},{2,3},{3,4},{4,5},{5,6},{6,7},{7,8},{8,9},{9,10},{10,1... | collective-permute-start | bytes 49160 | tf_op jit(solution)/shard_map/ppermute | solution.py:14
  529.5 7.7 %collective-permute-start.83 = (f32[2,1,2048]{2,1,0:T(1,128)S(1)}, f32[2,1,2048]{2,1,0:T(1,128)S(1)}, u32[]{:S(2)}, u32[]{:S(2)}) collective-permute-start(f32[2,1,2048]{2,1,0:T(1,128)S(1)} %get-tuple-element.125), channel_id=1, source_target_pairs={{0,1},{1,2},{2,3},{3,4},{4,5},{5,6},{6,7},{7,8},{8,9},{9,10},{10,1... | collective-permute-start | bytes 49160 | tf_op jit(solution)/shard_map/ppermute | solution.py:14
  539.6 7.7 %collective-permute-start.85 = (f32[2,1,2048]{2,1,0:T(1,128)S(1)}, f32[2,1,2048]{2,1,0:T(1,128)S(1)}, u32[]{:S(2)}, u32[]{:S(2)}) collective-permute-start(f32[2,1,2048]{2,1,0:T(1,128)S(1)} %get-tuple-element.123), channel_id=1, source_target_pairs={{0,1},{1,2},{2,3},{3,4},{4,5},{5,6},{6,7},{7,8},{8,9},{9,10},{10,1... | collective-permute-start | bytes 49160 | tf_op jit(solution)/shard_map/ppermute | solution.py:14
  549.7 8.4 %collective-permute-start.87 = (f32[2,1,2048]{2,1,0:T(1,128)S(1)}, f32[2,1,2048]{2,1,0:T(1,128)S(1)}, u32[]{:S(2)}, u32[]{:S(2)}) collective-permute-start(f32[2,1,2048]{2,1,0:T(1,128)S(1)} %get-tuple-element.121), channel_id=1, source_target_pairs={{0,1},{1,2},{2,3},{3,4},{4,5},{5,6},{6,7},{7,8},{8,9},{9,10},{10,1... | collective-permute-start | bytes 49160 | tf_op jit(solution)/shard_map/ppermute | solution.py:14
  573.7 11.5 %collective-permute-start.89 = (f32[2,32,2048]{2,1,0:T(8,128)S(1)}, f32[2,32,2048]{2,1,0:T(8,128)S(1)}, u32[]{:S(2)}, u32[]{:S(2)}) collective-permute-start(f32[2,32,2048]{2,1,0:T(8,128)S(1)} %pad_maximum_fusion.103), channel_id=1, source_target_pairs={{0,64},{64,128},{128,192},{1,65},{65,129},{129,193},{2,66},{66,130... | collective-permute-start | bytes 1572872 | tf_op jit(solution)/shard_map/ppermute | solution.py:25
  585.3 8.9 %collective-permute-start.90 = (f32[2,1,2048]{2,1,0:T(1,128)S(1)}, f32[2,1,2048]{2,1,0:T(1,128)S(1)}, u32[]{:S(2)}, u32[]{:S(2)}) collective-permute-start(f32[2,1,2048]{2,1,0:T(1,128)S(1)} %get-tuple-element.119), channel_id=1, source_target_pairs={{0,1},{1,2},{2,3},{3,4},{4,5},{5,6},{6,7},{7,8},{8,9},{9,10},{10,1... | collective-permute-start | bytes 49160 | tf_op jit(solution)/shard_map/ppermute | solution.py:14
  587.2 8.3 %collective-permute-start.91 = (f32[2,1,2048]{2,1,0:T(1,128)S(1)}, f32[2,1,2048]{2,1,0:T(1,128)S(1)}, u32[]{:S(2)}, u32[]{:S(2)}) collective-permute-start(f32[2,1,2048]{2,1,0:T(1,128)S(1)} %get-tuple-element.120), channel_id=1, source_target_pairs={{1,0},{2,1},{3,2},{4,3},{5,4},{6,5},{7,6},{8,7},{9,8},{10,9},{11,1... | collective-permute-start | bytes 49160 | tf_op jit(solution)/shard_map/ppermute | solution.py:17
  596.5 7.7 %collective-permute-start.92 = (f32[2,1,2048]{2,1,0:T(1,128)S(1)}, f32[2,1,2048]{2,1,0:T(1,128)S(1)}, u32[]{:S(2)}, u32[]{:S(2)}) collective-permute-start(f32[2,1,2048]{2,1,0:T(1,128)S(1)} %get-tuple-element.117), channel_id=1, source_target_pairs={{0,1},{1,2},{2,3},{3,4},{4,5},{5,6},{6,7},{7,8},{8,9},{9,10},{10,1... | collective-permute-start | bytes 49160 | tf_op jit(solution)/shard_map/ppermute | solution.py:14
  606.6 7.7 %collective-permute-start.94 = (f32[2,1,2048]{2,1,0:T(1,128)S(1)}, f32[2,1,2048]{2,1,0:T(1,128)S(1)}, u32[]{:S(2)}, u32[]{:S(2)}) collective-permute-start(f32[2,1,2048]{2,1,0:T(1,128)S(1)} %get-tuple-element.115), channel_id=1, source_target_pairs={{0,1},{1,2},{2,3},{3,4},{4,5},{5,6},{6,7},{7,8},{8,9},{9,10},{10,1... | collective-permute-start | bytes 49160 | tf_op jit(solution)/shard_map/ppermute | solution.py:14
  616.7 7.7 %collective-permute-start.96 = (f32[2,1,2048]{2,1,0:T(1,128)S(1)}, f32[2,1,2048]{2,1,0:T(1,128)S(1)}, u32[]{:S(2)}, u32[]{:S(2)}) collective-permute-start(f32[2,1,2048]{2,1,0:T(1,128)S(1)} %get-tuple-element.113), channel_id=1, source_target_pairs={{0,1},{1,2},{2,3},{3,4},{4,5},{5,6},{6,7},{7,8},{8,9},{9,10},{10,1... | collective-permute-start | bytes 49160 | tf_op jit(solution)/shard_map/ppermute | solution.py:14
  626.8 7.7 %collective-permute-start.98 = (f32[2,1,2048]{2,1,0:T(1,128)S(1)}, f32[2,1,2048]{2,1,0:T(1,128)S(1)}, u32[]{:S(2)}, u32[]{:S(2)}) collective-permute-start(f32[2,1,2048]{2,1,0:T(1,128)S(1)} %get-tuple-element.111), channel_id=1, source_target_pairs={{0,1},{1,2},{2,3},{3,4},{4,5},{5,6},{6,7},{7,8},{8,9},{9,10},{10,1... | collective-permute-start | bytes 49160 | tf_op jit(solution)/shard_map/ppermute | solution.py:14
  636.9 7.7 %collective-permute-start.100 = (f32[2,1,2048]{2,1,0:T(1,128)S(1)}, f32[2,1,2048]{2,1,0:T(1,128)S(1)}, u32[]{:S(2)}, u32[]{:S(2)}) collective-permute-start(f32[2,1,2048]{2,1,0:T(1,128)S(1)} %get-tuple-element.109), channel_id=1, source_target_pairs={{0,1},{1,2},{2,3},{3,4},{4,5},{5,6},{6,7},{7,8},{8,9},{9,10},{10,1... | collective-permute-start | bytes 49160 | tf_op jit(solution)/shard_map/ppermute | solution.py:14
  647.8 8.4 %collective-permute-start.102 = (f32[2,1,2048]{2,1,0:T(1,128)S(1)}, f32[2,1,2048]{2,1,0:T(1,128)S(1)}, u32[]{:S(2)}, u32[]{:S(2)}) collective-permute-start(f32[2,1,2048]{2,1,0:T(1,128)S(1)} %get-tuple-element.107), channel_id=1, source_target_pairs={{0,1},{1,2},{2,3},{3,4},{4,5},{5,6},{6,7},{7,8},{8,9},{9,10},{10,1... | collective-permute-start | bytes 49160 | tf_op jit(solution)/shard_map/ppermute | solution.py:14
  (59 other events, 499.5 us)
where the time goes:
time: 686 us; the launch traced here: 674 us
  starting transfers between devices  409 us (60%)
  other arithmetic  147 us (21%)
  waiting for transfers between devices  107 us (16%)
  local copies, waits for them, and re-layouts  7.84 us (1%)
    ppermute x49, starting transfers between devices, padded_2(): lax.ppermute(lax.slice_in_dim(block, 0, width, axis=dim), axis, backward)  291 us
    ppermute x49, starting transfers between devices, padded_2(): lax.ppermute(lax.slice_in_dim(block, block.shape[dim] - width, None, axis...  94.1 us
    sub x6, other arithmetic, descend(): accum_real * cosine - accum_imag * sine_part  73 us
    ppermute x49, waiting for transfers between devices, padded_2(): lax.ppermute(lax.slice_in_dim(block, 0, width, axis=dim), axis, backward)  62.3 us
    ppermute x6, waiting for transfers between devices, passed_along(): return lax.ppermute(block, axis, route)  44.6 us
    sub x42, other arithmetic, descend(): following = 2.0 * operate(latest) - previous  28.2 us
    ppermute x6, starting transfers between devices, passed_along(): return lax.ppermute(block, axis, route)  24.4 us
    concatenate x49, other arithmetic, padded_2(): block = jnp.concatenate([low, block, high], axis=dim)  16.6 us
  transfers between devices with their start and end apart: 104, of which 54 were waited for; matrix products, arithmetic and copies ran while one was open for 1% of the time, Pallas kernels for 0%

commit v1 on v0

v1 whole, which is shorter than its diff:
```python
import math

import jax
import jax.numpy as jnp
import numpy as np
from jax import lax
from jax.experimental import pallas as pl
from jax.experimental.pallas import tpu as pltpu
from jax.sharding import PartitionSpec as P

TERMS = 8
DEPTHS = 4
FREQS = 4
LANES = 128
COMPS = 2 * FREQS
HALO = DEPTHS * (TERMS - 1)
ROWS = 32
SPAN = 3 * ROWS
COLS = 512
WIDE = COLS + LANES
BLOCK = 8
VMEM = pl.BlockSpec(memory_space=pltpu.VMEM)
ANY = pl.BlockSpec(memory_space=pl.ANY)
PARAMS = pltpu.CompilerParams(vmem_limit_bytes=48 * 1024 * 1024)


def fit(function, low, high, count):
    angle = (np.arange(400) + 0.5) * np.pi / 400
    q = 0.5 * (low + high) + 0.5 * (high - low) * np.cos(angle)
    rows = np.stack([q**power for power in range(count)], 1)
    return np.linalg.lstsq(rows, function(q), rcond=None)[0]


ARGUMENT_LIMIT = 1.6
SINE = fit(lambda q: np.sin(np.sqrt(q)) / np.sqrt(q), 0.0, ARGUMENT_LIMIT**2, 6)
COSINE = fit(lambda q: np.cos(np.sqrt(q)), 0.0, ARGUMENT_LIMIT**2, 6)


def edge_columns(load, block):
    last = 2048 // COLS - 1
    right = load(pl.multiple_of(jnp.minimum(block + 1, last) * COLS, LANES))
    left = load(pl.multiple_of(jnp.maximum(block * COLS - LANES, 0), LANES))
    right = jnp.where(block < last, right, 0.0)
    left = jnp.where(block > 0, left, 0.0)
    lane = lax.broadcasted_iota(jnp.int32, right.shape, right.ndim - 1)
    return jnp.where(lane < LANES // 2, right, left)


def pack_kernel(wave_ref, slow_ref, head_ref, tail_ref, *slow_out):
    here = lax.axis_index("slab")
    start = pl.multiple_of(here * COLS, COLS)

    def put(rows, lanes):
        turned = jnp.swapaxes(rows, 0, 1)
        return turned

    for group in range(ROWS // 8):
        for piece in range(WIDE // LANES):
            parts = []
            for comp in range(2):
                for freq in range(FREQS):
                    source = wave_ref.at[freq, comp, group * 8 : group * 8 + 8]
                    if piece < COLS // LANES:
                        parts.append(source[:, pl.ds(start + piece * LANES, LANES)])
                    else:
                        parts.append(edge_columns(lambda at: source[:, pl.ds(at, LANES)], here))
            turned = put(jnp.stack(parts), None)
            lanes = slice(piece * LANES, (piece + 1) * LANES)
            low = group * 8
            keep = min(low + 8, HALO) - low
            head_ref[low : low + keep, :, lanes] = turned[:keep]
            skip = max(ROWS - HALO - low, 0)
            tail_ref[low + skip - (ROWS - HALO) : low + 8 - (ROWS - HALO), :, lanes] = turned[skip:]
    for shift, out in enumerate(slow_out):
        block = lax.rem(here + shift, DEPTHS)
        out[:, :COLS] = slow_ref[0, :, pl.ds(pl.multiple_of(block * COLS, COLS), COLS)]
        out[:, COLS:] = edge_columns(lambda at: slow_ref[0, :, pl.ds(at, LANES)], block)


def edge_kernel(*refs):
    pieces, (first_ref, last_ref, stacked) = refs[:DEPTHS], refs[DEPTHS:]
    here = lax.axis_index("slab")
    for shift, piece in enumerate(pieces):
        stacked[lax.rem(here - shift + DEPTHS, DEPTHS)] = piece[...]
    low = 0
    for depth in range(DEPTHS):
        count = ROWS - 8 * depth
        first_ref[low : low + count] = stacked[depth, :count]
        last_ref[low : low + count] = stacked[depth, ROWS - count :]
        low += count


def main_kernel(head, tail, above, below, *refs):
    pieces, (edge_above, edge_below, omega, taps, image, terms, slow, wide, sems) = (
        refs[:DEPTHS],
        refs[DEPTHS:],
    )
    here = lax.axis_index("slab")
    copies = []

    def bring(source, target):
        copy = pltpu.make_async_copy(source, target, sems.at[len(copies)])
        copy.start()
        copies.append(copy)

    begin = ROWS - HALO
    bring(above, terms.at[0, begin:ROWS])
    bring(head, terms.at[0, ROWS : ROWS + HALO])
    bring(tail.at[HALO - begin :], terms.at[0, ROWS + HALO : 2 * ROWS])
    bring(below, terms.at[0, 2 * ROWS : 2 * ROWS + HALO])
    for shift, piece in enumerate(pieces):
        bring(piece, slow.at[lax.rem(here - shift + DEPTHS, DEPTHS), ROWS : 2 * ROWS])
    low = 0
    for depth in range(DEPTHS):
        count = ROWS - 8 * depth
        bring(edge_above.at[low : low + count], slow.at[depth, ROWS - count : ROWS])
        bring(edge_below.at[low : low + count], slow.at[depth, 2 * ROWS : 2 * ROWS + count])
        low += count
    for copy in copies:
        copy.wait()

    sublane = lax.broadcasted_iota(jnp.int32, (COMPS, LANES), 0)
    real = sublane < FREQS

    def coefficient(index):
        return jnp.where(real, -float(SINE[index]), float(COSINE[index])).astype(jnp.float32)

    def rows_loop(low, high, body):
        count = high - low
        full = count // BLOCK

        def step(index, carry):
            body(low + index * BLOCK, BLOCK)
            return carry

        lax.fori_loop(0, full, step, 0)
        if count % BLOCK:
            body(low + full * BLOCK, count % BLOCK)

    for depth in range(DEPTHS):
        reach = HALO - depth * (TERMS - 1)
        lower, upper = ROWS - reach, 2 * ROWS + reach

        def spread(start, count):
            for row in range(count):
                line = slow[depth, pl.ds(start + row, 1), :] * 2.0
                wide[start + row] = jnp.broadcast_to(line, (COMPS, WIDE))

        rows_loop(lower + 1, upper - 1, spread)
        for order in range(1, TERMS):

            def apply(start, count):
                source = terms[order - 1, pl.ds(start - 1, count + 2)]
                pairs = source[:-1] + source[1:]
                tall = pairs[:-1] + pairs[1:]
                beside = tall + pltpu.roll(tall, 1, 2)
                full = beside + pltpu.roll(beside, WIDE - 1, 2)
                fresh = wide[pl.ds(start, count)] * (0.125 * full - source[1:-1])
                if order == 1:
                    fresh = 0.5 * fresh
                else:
                    fresh = fresh - terms[order - 2, pl.ds(start, count)]
                terms[order, pl.ds(start, count)] = fresh

            rows_loop(lower + order, upper - order, apply)

        def finish(start, count):
            for piece in range(WIDE // LANES):
                lanes = slice(piece * LANES, (piece + 1) * LANES)
                straight, crossed = None, None
                for order in range(TERMS):
                    term = terms[order, pl.ds(start, count), :, lanes]
                    one, other = taps[order] * term, taps[TERMS + order] * term
                    straight = one if straight is None else straight + one
                    crossed = other if crossed is None else crossed + other
                filtered = straight + pltpu.roll(crossed, FREQS, 1)
                offset = omega[...] * wide[pl.ds(start, count), :, lanes] - math.pi / 2
                square = offset * offset
                poly = coefficient(5)
                for index in range(4, -1, -1):
                    poly = poly * square + coefficient(index)
                own = poly * jnp.where(real, offset, 1.0)
                other = pltpu.roll(own, FREQS, 1)
                cosine = jnp.where(real, own, other)
                sine = jnp.where(real, -other, own)
                terms[0, pl.ds(start, count), :, lanes] = (
                    filtered * cosine + pltpu.roll(filtered, FREQS, 1) * sine
                )

        rows_loop(lower + TERMS - 1, upper - TERMS + 1, finish)

        def gather(index, carry):
            start = pl.multiple_of(index * 8, 8)
            block = terms[0, pl.ds(ROWS + start, 8), :, :COLS]
            image[depth, pl.ds(start, 8)] = jnp.sum(block[:, :FREQS], axis=1)
            return carry

        lax.fori_loop(0, ROWS // 8, gather, 0)


def local(wavefield, slowness, angular_freq, filter_taps):
    tiles, slabs = lax.axis_size("tile"), lax.axis_size("slab")
    shape = jax.ShapeDtypeStruct
    f32 = jnp.float32
    packed = pl.pallas_call(
        pack_kernel,
        out_shape=[shape((HALO, COMPS, WIDE), f32)] * 2 + [shape((ROWS, WIDE), f32)] * DEPTHS,
        in_specs=[VMEM] * 2,
        out_specs=[VMEM] * (2 + DEPTHS),
        compiler_params=PARAMS,
        name="pack",
    )(wavefield, slowness)
    head, tail, pieces = packed[0], packed[1], packed[2:]
    up = [(i + 1, i) for i in range(tiles - 1)]
    down = [(i, i + 1) for i in range(tiles - 1)]
    pieces = [pieces[0]] + [
        lax.ppermute(pieces[k], "slab", [(i, (i + k) % slabs) for i in range(slabs)])
        for k in range(1, slabs)
    ]
    below = lax.ppermute(head, "tile", up)
    above = lax.ppermute(tail, "tile", down)
    edge_rows = sum(ROWS - 8 * depth for depth in range(DEPTHS))
    first, last = pl.pallas_call(
        edge_kernel,
        out_shape=[shape((edge_rows, WIDE), f32)] * 2,
        in_specs=[VMEM] * DEPTHS,
        out_specs=[VMEM] * 2,
        scratch_shapes=[pltpu.VMEM((DEPTHS, ROWS, WIDE), f32)],
        compiler_params=PARAMS,
        name="edges",
    )(*pieces)
    edge_below = lax.ppermute(first, "tile", up)
    edge_above = lax.ppermute(last, "tile", down)

    omega = jnp.tile(0.5 * angular_freq, 2)[:, None] * jnp.ones((1, LANES), f32)
    real, imag = filter_taps[:, :, 0].T, filter_taps[:, :, 1].T
    straight = jnp.concatenate([real, real], axis=1)
    crossed = jnp.concatenate([imag, -imag], axis=1)
    taps = jnp.concatenate([straight, crossed], axis=0)[:, :, None] * jnp.ones((1, 1, LANES), f32)

    image = pl.pallas_call(
        main_kernel,
        out_shape=shape((DEPTHS, ROWS, COLS), f32),
        in_specs=[ANY] * (4 + DEPTHS + 2) + [VMEM] * 2,
        out_specs=VMEM,
        scratch_shapes=[
            pltpu.VMEM((TERMS, SPAN, COMPS, WIDE), f32),
            pltpu.VMEM((DEPTHS, SPAN, WIDE), f32),
            pltpu.VMEM((SPAN, COMPS, WIDE), f32),
            pltpu.SemaphoreType.DMA((4 + 3 * DEPTHS,)),
        ],
        compiler_params=PARAMS,
        name="migrate",
    )(head, tail, above, below, *pieces, edge_above, edge_below, omega, taps)
    return lax.all_to_all(image, "slab", 0, 2, tiled=True)


def solution(mesh):
    placed = (P(None, None, "tile", None), P("slab", "tile", None), P(), P())
    return jax.shard_map(
        local, mesh=mesh, in_specs=placed, out_specs=P("slab", "tile", None), check_vma=False
    )
```

time: 686 us -> 103 us (0.15); the launches traced: 674 us -> 102 us
  starting transfers between devices: 409 us -> 23 us
  other arithmetic: 147 us -> 0.08 us
  waiting for transfers between devices: 107 us -> 6.07 us
  Pallas kernels: 0 us -> 59.1 us
  blocking collectives: 0 us -> 10.3 us
    ppermute x104 -> x7, starting transfers between devices: 409 us -> 23 us  [the longest x1 7.47 us: local(): below = lax.ppermute(head, 'tile', up)]
    sub x48 -> x0, other arithmetic: 101 us -> none  [the longest x6 73 us: descend(): accum_real * cosine - accum_imag * sine_part]
    ppermute x104 -> x7, waiting for transfers between devices: 107 us -> 6.07 us  [the longest x3 3.08 us: local(): lax.ppermute(pieces[k], 'slab', [(i, (i + k) % slabs) for i in range(slab...]
    pallas_call x0 -> x3, Pallas kernels: none -> 59.1 us  [the longest x1 58.9 us: local(): pl.pallas_call(main_kernel, out_shape=shape((DEPTHS, ROWS, COLS), f32), i...]
    add x7 -> x0, other arithmetic: 23 us -> none  [the longest x1 12.9 us: local(): images = images.at[0].add(jnp.where(active, current[0], 0.0))]
    concatenate x49 -> x1, other arithmetic: 16.6 us -> 0.08 us  [local(): jnp.concatenate([straight, crossed], axis=0)[:, :, None]]
    all_to_all x0 -> x1, blocking collectives: none -> 10.3 us  [local(): return lax.all_to_all(image, 'slab', 0, 2, tiled=True)]
  transfers between devices with their start and end apart: 104 -> 7, of which waited for: 54 -> 4; matrix products, arithmetic and copies ran while one was open for 1% -> 0% of each run, Pallas kernels for 0% -> 0%
where the time goes in v1:
time: 103 us; the launch traced here: 102 us
  Pallas kernels  59.1 us (57%)
  starting transfers between devices  23 us (22%)
  blocking collectives  10.3 us (10%)
  waiting for transfers between devices  6.07 us (6%)
  local copies, waits for them, and re-layouts  3.57 us (3%)
    pallas_call x1, Pallas kernels, local(): pl.pallas_call(main_kernel, out_shape=shape((DEPTHS, ROWS, COLS), f32), i...  58.9 us
    all_to_all x1, blocking collectives, local(): return lax.all_to_all(image, 'slab', 0, 2, tiled=True)  10.3 us
    ppermute x1, starting transfers between devices, local(): below = lax.ppermute(head, 'tile', up)  7.47 us
    ppermute x3, starting transfers between devices, local(): lax.ppermute(pieces[k], 'slab', [(i, (i + k) % slabs) for i in range(slab...  5.9 us
    ppermute x1, starting transfers between devices, local(): edge_below = lax.ppermute(first, 'tile', up)  5.75 us
    ppermute x3, waiting for transfers between devices, local(): lax.ppermute(pieces[k], 'slab', [(i, (i + k) % slabs) for i in range(slab...  3.08 us
    unnamed x8, local copies, waits for them, and re-layouts  2.55 us
  transfers between devices with their start and end apart: 7, of which 4 were waited for; matrix products, arithmetic and copies ran while one was open for 0% of the time, Pallas kernels for 0%

profile of v1, /device:TPU:6, one launch (start us, length us, event | category | flops | bytes accessed | tf_op | source)
XLA Modules:
  0.0 102.2 jit_solution(12183546258976720752)
XLA Ops:
  0.0 0.0 copy-start
  0.0 1.6 %copy-done = f32[4,2,32,2048]{3,2,1,0:T(8,128)S(1)} copy-done((f32[4,2,32,2048]{3,2,1,0:T(8,128)S(1)}, f32[4,2,32,2048]{3,2,1,0:T(8,128)}, u32[]{:S(2)}) %copy-start) | copy-done | bytes 2097176
  1.6 0.0 copy-start.1
  1.6 0.9 copy-done.1
  2.5 0.0 copy-start.2
  2.5 0.0 copy-start.3
  2.5 0.1 pack.1
  2.7 7.5 %collective-permute-start.1 = (f32[28,8,640]{2,1,0:T(8,128)S(1)}, f32[28,8,640]{2,1,0:T(8,128)S(1)}, u32[]{:S(2)}, u32[]{:S(2)}) collective-permute-start(f32[28,8,640]{2,1,0:T(8,128)S(1)} %get-tuple-element.13.head), channel_id=1, source_target_pairs={{1,0},{2,1},{3,2},{4,3},{5,4},{6,5},{7,6},{8,7},{9,8},{10,9},{11,1... | collective-permute-start | bytes 1720328 | tf_op jit(solution)/shard_map/ppermute | solution.py:220
  10.2 1.9 %collective-permute-start = (f32[28,8,640]{2,1,0:T(8,128)S(1)}, f32[28,8,640]{2,1,0:T(8,128)S(1)}, u32[]{:S(2)}, u32[]{:S(2)}) collective-permute-start(f32[28,8,640]{2,1,0:T(8,128)S(1)} %get-tuple-element.14.tail), channel_id=1, source_target_pairs={{0,1},{1,2},{2,3},{3,4},{4,5},{5,6},{6,7},{7,8},{8,9},{9,10},{10,1... | collective-permute-start | bytes 1720328 | tf_op jit(solution)/shard_map/ppermute | solution.py:221
  12.1 1.7 %collective-permute-start.2 = (f32[32,640]{1,0:T(8,128)S(1)}, f32[32,640]{1,0:T(8,128)S(1)}, u32[]{:S(2)}, u32[]{:S(2)}) collective-permute-start(f32[32,640]{1,0:T(8,128)S(1)} %get-tuple-element.16), channel_id=1, source_target_pairs={{0,64},{64,128},{128,192},{192,0},{1,65},{65,129},{129,193},{193,1... | collective-permute-start | bytes 245768 | tf_op jit(solution)/shard_map/ppermute | solution.py:217
  13.8 2.9 %collective-permute-start.3 = (f32[32,640]{1,0:T(8,128)S(1)}, f32[32,640]{1,0:T(8,128)S(1)}, u32[]{:S(2)}, u32[]{:S(2)}) collective-permute-start(f32[32,640]{1,0:T(8,128)S(1)} %get-tuple-element.17), channel_id=1, source_target_pairs={{0,128},{64,192},{128,0},{192,64},{1,129},{65,193},{129,1},{193,65... | collective-permute-start | bytes 245768 | tf_op jit(solution)/shard_map/ppermute | solution.py:217
  16.7 1.3 %collective-permute-start.4 = (f32[32,640]{1,0:T(8,128)S(1)}, f32[32,640]{1,0:T(8,128)S(1)}, u32[]{:S(2)}, u32[]{:S(2)}) collective-permute-start(f32[32,640]{1,0:T(8,128)S(1)} %get-tuple-element.18), channel_id=1, source_target_pairs={{0,192},{64,0},{128,64},{192,128},{1,193},{65,1},{129,65},{193,129... | collective-permute-start | bytes 245768 | tf_op jit(solution)/shard_map/ppermute | solution.py:217
  18.0 0.0 copy-done.2
  18.0 0.0 collective-permute-done.2.refs_1_
  18.0 1.9 %collective-permute-done.3.refs_2_ = f32[32,640]{1,0:T(8,128)S(1)} collective-permute-done((f32[32,640]{1,0:T(8,128)S(1)}, f32[32,640]{1,0:T(8,128)S(1)}, u32[]{:S(2)}, u32[]{:S(2)}) %collective-permute-start.3) | collective-permute-done | bytes 81952 | tf_op jit(solution)/shard_map/ppermute | solution.py:217
  20.0 1.1 %collective-permute-done.4.refs_3_ = f32[32,640]{1,0:T(8,128)S(1)} collective-permute-done((f32[32,640]{1,0:T(8,128)S(1)}, f32[32,640]{1,0:T(8,128)S(1)}, u32[]{:S(2)}, u32[]{:S(2)}) %collective-permute-start.4) | collective-permute-done | bytes 81952 | tf_op jit(solution)/shard_map/ppermute | solution.py:217
  21.1 0.1 edges.1
  21.2 1.9 %collective-permute-start.5 = (f32[80,640]{1,0:T(8,128)S(1)}, f32[80,640]{1,0:T(8,128)S(1)}, u32[]{:S(2)}, u32[]{:S(2)}) collective-permute-start(f32[80,640]{1,0:T(8,128)S(1)} %get-tuple-element.19), channel_id=1, source_target_pairs={{0,1},{1,2},{2,3},{3,4},{4,5},{5,6},{6,7},{7,8},{8,9},{9,10},{10,1... | collective-permute-start | bytes 614408 | tf_op jit(solution)/shard_map/ppermute | solution.py:233
  23.1 5.8 %collective-permute-start.6 = (f32[80,640]{1,0:T(8,128)S(1)}, f32[80,640]{1,0:T(8,128)S(1)}, u32[]{:S(2)}, u32[]{:S(2)}) collective-permute-start(f32[80,640]{1,0:T(8,128)S(1)} %get-tuple-element.20), channel_id=1, source_target_pairs={{1,0},{2,1},{3,2},{4,3},{5,4},{6,5},{7,6},{8,7},{9,8},{10,9},{11,1... | collective-permute-start | bytes 614408 | tf_op jit(solution)/shard_map/ppermute | solution.py:232
  28.9 0.0 copy-done.3
  28.9 0.1 mul.16
  29.0 0.1 maximum_maximum_fusion
  29.0 0.1 copy.6
  29.1 1.2 %collective-permute-done.5.refs_4_ = f32[80,640]{1,0:T(8,128)S(1)} collective-permute-done((f32[80,640]{1,0:T(8,128)S(1)}, f32[80,640]{1,0:T(8,128)S(1)}, u32[]{:S(2)}, u32[]{:S(2)}) %collective-permute-start.5) | collective-permute-done | bytes 204832 | tf_op jit(solution)/shard_map/ppermute | solution.py:233
  30.4 1.8 %collective-permute-done.6.refs_5_ = f32[80,640]{1,0:T(8,128)S(1)} collective-permute-done((f32[80,640]{1,0:T(8,128)S(1)}, f32[80,640]{1,0:T(8,128)S(1)}, u32[]{:S(2)}, u32[]{:S(2)}) %collective-permute-start.6) | collective-permute-done | bytes 204832 | tf_op jit(solution)/shard_map/ppermute | solution.py:232
  32.1 0.0 collective-permute-done.1.below
  32.1 0.0 collective-permute-done.above
  32.1 0.1 mul.17.refs_6_
  32.2 0.1 mul.18.refs_7_
  32.3 58.9 %migrate.1 = f32[4,32,512]{2,1,0:T(8,128)S(1)} custom-call(f32[28,8,640]{2,1,0:T(8,128)S(1)} %get-tuple-element.13.head, f32[28,8,640]{2,1,0:T(8,128)S(1)} %get-tuple-element.14.tail, f32[28,8,640]{2,1,0:T(8,128)S(1)} %collective-permute-done.above, f32[28,8,640]{2,1,0:T(8,128)S(1)} %collective-permute-done.1.below, ...), custom_call_target="tpu_custom_call" | custom-call | tf_op jit(solution)/shard_map/migrate/pallas_call | solution.py:241
  91.2 10.3 %all_to_all.18 = f32[4,32,512]{2,1,0:T(8,128)S(1)} all-to-all(f32[4,32,512]{2,1,0:T(8,128)S(1)} %migrate.1), channel_id=1, replica_groups=mesh['slab'=4,'tile'=64] {'slab'}, dimensions={0} | all-to-all | bytes 524288 | tf_op jit(solution)/shard_map/all_to_all | solution.py:255
  101.5 0.7 copy.8
  (4 shorter events, 0.0 us)
Async XLA Ops:
  0.0 1.6 %copy-start = (f32[4,2,32,2048]{3,2,1,0:T(8,128)S(1)}, f32[4,2,32,2048]{3,2,1,0:T(8,128)}, u32[]{:S(2)}) copy-start(f32[4,2,32,2048]{3,2,1,0:T(8,128)} %wave_ref.1) | copy-start | bytes 6291460
  1.6 0.9 copy-start.1
  2.5 15.5 %copy-start.2 = (f32[4,8,2]{1,2,0:T(2,128)S(1)}, f32[4,8,2]{1,2,0:T(2,128)}, u32[]{:S(2)}) copy-start(f32[4,8,2]{1,2,0:T(2,128)} %param.7) | copy-start | bytes 772
  2.5 26.3 %copy-start.3 = (f32[4]{0:T(128)S(1)}, f32[4]{0:T(128)}, u32[]{:S(2)}) copy-start(f32[4]{0:T(128)} %param.6) | copy-start | bytes 52
  2.7 29.4 %collective-permute-start.1 = (f32[28,8,640]{2,1,0:T(8,128)S(1)}, f32[28,8,640]{2,1,0:T(8,128)S(1)}, u32[]{:S(2)}, u32[]{:S(2)}) collective-permute-start(f32[28,8,640]{2,1,0:T(8,128)S(1)} %get-tuple-element.13.head), channel_id=1, source_target_pairs={{1,0},{2,1},{3,2},{4,3},{5,4},{6,5},{7,6},{8,7},{9,8},{10,9},{11,1... | collective-permute-start | bytes 1720328 | tf_op jit(solution)/shard_map/ppermute | solution.py:220
  10.2 21.9 %collective-permute-start = (f32[28,8,640]{2,1,0:T(8,128)S(1)}, f32[28,8,640]{2,1,0:T(8,128)S(1)}, u32[]{:S(2)}, u32[]{:S(2)}) collective-permute-start(f32[28,8,640]{2,1,0:T(8,128)S(1)} %get-tuple-element.14.tail), channel_id=1, source_target_pairs={{0,1},{1,2},{2,3},{3,4},{4,5},{5,6},{6,7},{7,8},{8,9},{9,10},{10,1... | collective-permute-start | bytes 1720328 | tf_op jit(solution)/shard_map/ppermute | solution.py:221
  12.1 5.9 %collective-permute-start.2 = (f32[32,640]{1,0:T(8,128)S(1)}, f32[32,640]{1,0:T(8,128)S(1)}, u32[]{:S(2)}, u32[]{:S(2)}) collective-permute-start(f32[32,640]{1,0:T(8,128)S(1)} %get-tuple-element.16), channel_id=1, source_target_pairs={{0,64},{64,128},{128,192},{192,0},{1,65},{65,129},{129,193},{193,1... | collective-permute-start | bytes 245768 | tf_op jit(solution)/shard_map/ppermute | solution.py:217
  13.8 6.2 %collective-permute-start.3 = (f32[32,640]{1,0:T(8,128)S(1)}, f32[32,640]{1,0:T(8,128)S(1)}, u32[]{:S(2)}, u32[]{:S(2)}) collective-permute-start(f32[32,640]{1,0:T(8,128)S(1)} %get-tuple-element.17), channel_id=1, source_target_pairs={{0,128},{64,192},{128,0},{192,64},{1,129},{65,193},{129,1},{193,65... | collective-permute-start | bytes 245768 | tf_op jit(solution)/shard_map/ppermute | solution.py:217
  16.7 4.4 %collective-permute-start.4 = (f32[32,640]{1,0:T(8,128)S(1)}, f32[32,640]{1,0:T(8,128)S(1)}, u32[]{:S(2)}, u32[]{:S(2)}) collective-permute-start(f32[32,640]{1,0:T(8,128)S(1)} %get-tuple-element.18), channel_id=1, source_target_pairs={{0,192},{64,0},{128,64},{192,128},{1,193},{65,1},{129,65},{193,129... | collective-permute-start | bytes 245768 | tf_op jit(solution)/shard_map/ppermute | solution.py:217
  21.2 9.2 %collective-permute-start.5 = (f32[80,640]{1,0:T(8,128)S(1)}, f32[80,640]{1,0:T(8,128)S(1)}, u32[]{:S(2)}, u32[]{:S(2)}) collective-permute-start(f32[80,640]{1,0:T(8,128)S(1)} %get-tuple-element.19), channel_id=1, source_target_pairs={{0,1},{1,2},{2,3},{3,4},{4,5},{5,6},{6,7},{7,8},{8,9},{9,10},{10,1... | collective-permute-start | bytes 614408 | tf_op jit(solution)/shard_map/ppermute | solution.py:233
  23.1 9.0 %collective-permute-start.6 = (f32[80,640]{1,0:T(8,128)S(1)}, f32[80,640]{1,0:T(8,128)S(1)}, u32[]{:S(2)}, u32[]{:S(2)}) collective-permute-start(f32[80,640]{1,0:T(8,128)S(1)} %get-tuple-element.20), channel_id=1, source_target_pairs={{1,0},{2,1},{3,2},{4,3},{5,4},{6,5},{7,6},{8,7},{9,8},{10,9},{11,1... | collective-permute-start | bytes 614408 | tf_op jit(solution)/shard_map/ppermute | solution.py:232

commit v2 on v1

--- a/solution.py
+++ b/solution.py
@@ -18,10 +18,19 @@
 SPAN = 3 * ROWS
 COLS = 512
 WIDE = COLS + LANES
-BLOCK = 8
+APPLY = 16
+FINISH = 4
+SPREAD = 8
 VMEM = pl.BlockSpec(memory_space=pltpu.VMEM)
 ANY = pl.BlockSpec(memory_space=pl.ANY)
 PARAMS = pltpu.CompilerParams(vmem_limit_bytes=48 * 1024 * 1024)
+
+SCRATCH = [
+    pltpu.VMEM((DEPTHS, SPAN, WIDE), jnp.float32),
+    pltpu.VMEM((SPAN, COMPS, WIDE), jnp.float32),
+    pltpu.VMEM((DEPTHS * ROWS, WIDE), jnp.float32),
+    pltpu.SemaphoreType.DMA((4 + 3 * DEPTHS,)),
+] + [pltpu.VMEM((SPAN, COMPS, WIDE), jnp.float32)] * TERMS
 
 
 def fit(function, low, high, count):
@@ -46,14 +55,28 @@
     return jnp.where(lane < LANES // 2, right, left)
 
 
-def pack_kernel(wave_ref, slow_ref, head_ref, tail_ref, *slow_out):
+def shuffle(column_axis):
+    vectors = WIDE // LANES
+    column = lax.broadcasted_iota(jnp.int32, (WIDE, WIDE), column_axis)
+    place = lax.broadcasted_iota(jnp.int32, (WIDE, WIDE), 1 - column_axis)
+    lane = place & (LANES - 1)
+    here = lane * vectors + (place >> 7)
+    return jnp.where(column == here, 1.0, 0.0).astype(jnp.bfloat16)
+
+
+def exact_dot(rows, matrix):
+    high = rows.astype(jnp.bfloat16)
+    rest = rows - high.astype(jnp.float32)
+    middle = rest.astype(jnp.bfloat16)
+    low = (rest - middle.astype(jnp.float32)).astype(jnp.bfloat16)
+    dots = [jnp.dot(part, matrix, preferred_element_type=jnp.float32) for part in (high, middle, low)]
+    return (dots[0] + dots[1]) + dots[2]
+
+
+def pack_kernel(wave_ref, slow_ref, head_ref, tail_ref, *refs):
+    slow_out, lined = refs[:DEPTHS], refs[DEPTHS]
     here = lax.axis_index("slab")
     start = pl.multiple_of(here * COLS, COLS)
-
-    def put(rows, lanes):
-        turned = jnp.swapaxes(rows, 0, 1)
-        return turned
-
     for group in range(ROWS // 8):
         for piece in range(WIDE // LANES):
             parts = []
@@ -64,17 +87,23 @@
                         parts.append(source[:, pl.ds(start + piece * LANES, LANES)])
                     else:
                         parts.append(edge_columns(lambda at: source[:, pl.ds(at, LANES)], here))
-            turned = put(jnp.stack(parts), None)
-            lanes = slice(piece * LANES, (piece + 1) * LANES)
-            low = group * 8
-            keep = min(low + 8, HALO) - low
-            head_ref[low : low + keep, :, lanes] = turned[:keep]
-            skip = max(ROWS - HALO - low, 0)
-            tail_ref[low + skip - (ROWS - HALO) : low + 8 - (ROWS - HALO), :, lanes] = turned[skip:]
+            turned = jnp.swapaxes(jnp.stack(parts), 0, 1).reshape(8 * COMPS, LANES)
+            low = group * 8 * COMPS
+            lined[low : low + 8 * COMPS, piece * LANES : (piece + 1) * LANES] = turned
+    for shift in range(DEPTHS):
+        block = lax.rem(here + shift, DEPTHS)
+        low = ROWS * COMPS + shift * ROWS
+        lined[low : low + ROWS, :COLS] = slow_ref[
+            0, :, pl.ds(pl.multiple_of(block * COLS, COLS), COLS)
+        ]
+        lined[low : low + ROWS, COLS:] = edge_columns(lambda at: slow_ref[0, :, pl.ds(at, LANES)], block)
+    lined[...] = exact_dot(lined[...], shuffle(0))
+    field = lined[: ROWS * COMPS].reshape(ROWS, COMPS, WIDE)
+    head_ref[...] = field[:HALO]
+    tail_ref[...] = field[ROWS - HALO :]
     for shift, out in enumerate(slow_out):
-        block = lax.rem(here + shift, DEPTHS)
-        out[:, :COLS] = slow_ref[0, :, pl.ds(pl.multiple_of(block * COLS, COLS), COLS)]
-        out[:, COLS:] = edge_columns(lambda at: slow_ref[0, :, pl.ds(at, LANES)], block)
+        low = ROWS * COMPS + shift * ROWS
+        out[...] = lined[low : low + ROWS]
 
 
 def edge_kernel(*refs):
@@ -91,7 +120,7 @@
 
 
 def main_kernel(head, tail, above, below, *refs):
-    pieces, (edge_above, edge_below, omega, taps, image, terms, slow, wide, sems) = (
+    pieces, (edge_above, edge_below, omega, taps, image, slow, wide, mixed, sems, *terms) = (
         refs[:DEPTHS],
         refs[DEPTHS:],
     )
@@ -104,10 +133,10 @@
         copies.append(copy)
 
     begin = ROWS - HALO
-    bring(above, terms.at[0, begin:ROWS])
-    bring(head, terms.at[0, ROWS : ROWS + HALO])
-    bring(tail.at[HALO - begin :], terms.at[0, ROWS + HALO : 2 * ROWS])
-    bring(below, terms.at[0, 2 * ROWS : 2 * ROWS + HALO])
+    bring(above, terms[0].at[begin:ROWS])
+    bring(head, terms[0].at[ROWS : ROWS + HALO])
+    bring(tail.at[HALO - begin :], terms[0].at[ROWS + HALO : 2 * ROWS])
+    bring(below, terms[0].at[2 * ROWS : 2 * ROWS + HALO])
     for shift, piece in enumerate(pieces):
         bring(piece, slow.at[lax.rem(here - shift + DEPTHS, DEPTHS), ROWS : 2 * ROWS])
     low = 0
@@ -125,17 +154,24 @@
     def coefficient(index):
         return jnp.where(real, -float(SINE[index]), float(COSINE[index])).astype(jnp.float32)
 
-    def rows_loop(low, high, body):
-        count = high - low
-        full = count // BLOCK
+    def rows_loop(low, high, size, body):
+        full = (high - low) // size
 
         def step(index, carry):
-            body(low + index * BLOCK, BLOCK)
+            body(low + index * size, size)
             return carry
 
         lax.fori_loop(0, full, step, 0)
-        if count % BLOCK:
-            body(low + full * BLOCK, count % BLOCK)
+        if (high - low) % size:
+            body(low + full * size, (high - low) % size)
+
+    def covering_loop(low, high, size, body):
+
+        def step(index, carry):
+            body(jnp.minimum(low + index * size, high - size), size)
+            return carry
+
+        lax.fori_loop(0, -(-(high - low) // size), step, 0)
 
     for depth in range(DEPTHS):
         reach = HALO - depth * (TERMS - 1)
@@ -146,56 +182,72 @@
                 line = slow[depth, pl.ds(start + row, 1), :] * 2.0
                 wide[start + row] = jnp.broadcast_to(line, (COMPS, WIDE))
 
-        rows_loop(lower + 1, upper - 1, spread)
+        covering_loop(lower + 1, upper - 1, SPREAD, spread)
         for order in range(1, TERMS):
 
             def apply(start, count):
-                source = terms[order - 1, pl.ds(start - 1, count + 2)]
-                pairs = source[:-1] + source[1:]
-                tall = pairs[:-1] + pairs[1:]
-                beside = tall + pltpu.roll(tall, 1, 2)
-                full = beside + pltpu.roll(beside, WIDE - 1, 2)
-                fresh = wide[pl.ds(start, count)] * (0.125 * full - source[1:-1])
-                if order == 1:
-                    fresh = 0.5 * fresh
-                else:
-                    fresh = fresh - terms[order - 2, pl.ds(start, count)]
-                terms[order, pl.ds(start, count)] = fresh
-
-            rows_loop(lower + order, upper - order, apply)
+                pieces = range(WIDE // LANES)
+
+                def load(ref, at):
+                    return [ref[at, :, p * LANES : (p + 1) * LANES] for p in pieces]
+
+                here_row = load(terms[order - 1], start)
+                pair = [a + b for a, b in zip(load(terms[order - 1], start - 1), here_row)]
+                for row in range(count):
+                    next_row = load(terms[order - 1], start + row + 1)
+                    next_pair = [a + b for a, b in zip(here_row, next_row)]
+                    tall = [a + b for a, b in zip(pair, next_pair)]
+                    before = pltpu.roll(tall[-1], 1, 1)
+                    after = pltpu.roll(tall[0], LANES - 1, 1)
+                    chain = [before] + tall + [after]
+                    sums = [a + b for a, b in zip(chain[:-1], chain[1:])]
+                    full = [a + b for a, b in zip(sums[:-1], sums[1:])]
+                    for p in pieces:
+                        lanes = slice(p * LANES, (p + 1) * LANES)
+                        fresh = wide[start + row, :, lanes] * (0.125 * full[p] - here_row[p])
+                        if order == 1:
+                            fresh = 0.5 * fresh
+                        else:
+                            fresh = fresh - terms[order - 2][start + row, :, lanes]
+                        terms[order][start + row, :, lanes] = fresh
+                    here_row, pair = next_row, next_pair
+
+            covering_loop(lower + order, upper - order, APPLY, apply)
 
         def finish(start, count):
-            for piece in range(WIDE // LANES):
-                lanes = slice(piece * LANES, (piece + 1) * LANES)
-                straight, crossed = None, None
-                for order in range(TERMS):
-                    term = terms[order, pl.ds(start, count), :, lanes]
-                    one, other = taps[order] * term, taps[TERMS + order] * term
-                    straight = one if straight is None else straight + one
-                    crossed = other if crossed is None else crossed + other
-                filtered = straight + pltpu.roll(crossed, FREQS, 1)
-                offset = omega[...] * wide[pl.ds(start, count), :, lanes] - math.pi / 2
-                square = offset * offset
-                poly = coefficient(5)
-                for index in range(4, -1, -1):
-                    poly = poly * square + coefficient(index)
-                own = poly * jnp.where(real, offset, 1.0)
-                other = pltpu.roll(own, FREQS, 1)
-                cosine = jnp.where(real, own, other)
-                sine = jnp.where(real, -other, own)
-                terms[0, pl.ds(start, count), :, lanes] = (
-                    filtered * cosine + pltpu.roll(filtered, FREQS, 1) * sine
-                )
-
-        rows_loop(lower + TERMS - 1, upper - TERMS + 1, finish)
+            for row in range(count):
+                for piece in range(WIDE // LANES):
+                    lanes = slice(piece * LANES, (piece + 1) * LANES)
+                    straight, crossed = None, None
+                    for order in range(TERMS):
+                        term = terms[order][start + row, :, lanes]
+                        one, other = taps[order] * term, taps[TERMS + order] * term
+                        straight = one if straight is None else straight + one
+                        crossed = other if crossed is None else crossed + other
+                    filtered = straight + pltpu.roll(crossed, FREQS, 0)
+                    offset = omega[...] * wide[start + row, :, lanes] - math.pi / 2
+                    square = offset * offset
+                    poly = coefficient(5)
+                    for index in range(4, -1, -1):
+                        poly = poly * square + coefficient(index)
+                    own = poly * jnp.where(real, offset, 1.0)
+                    other = pltpu.roll(own, FREQS, 0)
+                    cosine = jnp.where(real, own, other)
+                    sine = jnp.where(real, -other, own)
+                    terms[0][start + row, :, lanes] = (
+                        filtered * cosine + pltpu.roll(filtered, FREQS, 0) * sine
+                    )
+
+        rows_loop(lower + TERMS - 1, upper - TERMS + 1, FINISH, finish)
 
         def gather(index, carry):
             start = pl.multiple_of(index * 8, 8)
-            block = terms[0, pl.ds(ROWS + start, 8), :, :COLS]
-            image[depth, pl.ds(start, 8)] = jnp.sum(block[:, :FREQS], axis=1)
+            block = terms[0][pl.ds(ROWS + start, 8)]
+            mixed[pl.ds(depth * ROWS + start, 8)] = jnp.sum(block[:, :FREQS], axis=1)
             return carry
 
         lax.fori_loop(0, ROWS // 8, gather, 0)
+    image[...] = exact_dot(mixed[...], shuffle(1)[:, :COLS]).reshape(image.shape)
 
 
 def local(wavefield, slowness, angular_freq, filter_taps):
@@ -207,6 +259,7 @@
         out_shape=[shape((HALO, COMPS, WIDE), f32)] * 2 + [shape((ROWS, WIDE), f32)] * DEPTHS,
         in_specs=[VMEM] * 2,
         out_specs=[VMEM] * (2 + DEPTHS),
+        scratch_shapes=[pltpu.VMEM((ROWS * COMPS + DEPTHS * ROWS, WIDE), f32)],
         compiler_params=PARAMS,
         name="pack",
     )(wavefield, slowness)
@@ -243,12 +296,7 @@
         out_shape=shape((DEPTHS, ROWS, COLS), f32),
         in_specs=[ANY] * (4 + DEPTHS + 2) + [VMEM] * 2,
         out_specs=VMEM,
-        scratch_shapes=[
-            pltpu.VMEM((TERMS, SPAN, COMPS, WIDE), f32),
-            pltpu.VMEM((DEPTHS, SPAN, WIDE), f32),
-            pltpu.VMEM((SPAN, COMPS, WIDE), f32),
-            pltpu.SemaphoreType.DMA((4 + 3 * DEPTHS,)),
-        ],
+        scratch_shapes=SCRATCH,
         compiler_params=PARAMS,
         name="migrate",
     )(head, tail, above, below, *pieces, edge_above, edge_below, omega, taps)

time: 103 us -> 71.3 us (0.69)
  Pallas kernels: 59.1 us -> 27.9 us
    pallas_call x1, Pallas kernels: 58.9 us -> 26.2 us  [local(): pl.pallas_call(main_kernel, out_shape=shape((DEPTHS, ROWS, COLS), f32), i...]
    pallas_call x1, Pallas kernels: 0.15 us -> 1.62 us  [local(): pl.pallas_call(pack_kernel, out_shape=[shape((HALO, COMPS, WIDE), f32)] *...]
where the time goes in v2:
time: 71.3 us; the launch traced here: 71 us
  Pallas kernels  27.9 us (39%)
  starting transfers between devices  23 us (32%)
  blocking collectives  10.3 us (14%)
  waiting for transfers between devices  6.07 us (9%)
  local copies, waits for them, and re-layouts  3.57 us (5%)
    pallas_call x1, Pallas kernels, local(): pl.pallas_call(main_kernel, out_shape=shape((DEPTHS, ROWS, COLS), f32), i...  26.2 us
    all_to_all x1, blocking collectives, local(): return lax.all_to_all(image, 'slab', 0, 2, tiled=True)  10.3 us
    ppermute x1, starting transfers between devices, local(): below = lax.ppermute(head, 'tile', up)  7.47 us
    ppermute x3, starting transfers between devices, local(): lax.ppermute(pieces[k], 'slab', [(i, (i + k) % slabs) for i in range(slab...  5.9 us
    ppermute x1, starting transfers between devices, local(): edge_below = lax.ppermute(first, 'tile', up)  5.75 us
    ppermute x3, waiting for transfers between devices, local(): lax.ppermute(pieces[k], 'slab', [(i, (i + k) % slabs) for i in range(slab...  3.08 us
    unnamed x8, local copies, waits for them, and re-layouts  2.55 us
    ppermute x1, starting transfers between devices, local(): above = lax.ppermute(tail, 'tile', down)  1.92 us
  transfers between devices with their start and end apart: 7, of which 4 were waited for; matrix products, arithmetic and copies ran while one was open for 0% of the time, Pallas kernels for 0%

profile of v2, /device:TPU:6, one launch (start us, length us, event | category | flops | bytes accessed | tf_op | source)
XLA Modules:
  0.0 71.0 jit_solution(1137964276664132898)
XLA Ops:
  0.0 0.0 copy-start
  0.0 1.6 %copy-done = f32[4,2,32,2048]{3,2,1,0:T(8,128)S(1)} copy-done((f32[4,2,32,2048]{3,2,1,0:T(8,128)S(1)}, f32[4,2,32,2048]{3,2,1,0:T(8,128)}, u32[]{:S(2)}) %copy-start) | copy-done | bytes 2097176
  1.6 0.0 copy-start.1
  1.6 0.9 %copy-done.1 = f32[1,32,2048]{2,1,0:T(8,128)S(1)} copy-done((f32[1,32,2048]{2,1,0:T(8,128)S(1)}, f32[1,32,2048]{2,1,0:T(8,128)}, u32[]{:S(2)}) %copy-start.1) | copy-done | bytes 262168
  2.5 0.0 copy-start.2
  2.5 0.0 copy-start.3
  2.5 1.6 %pack.1 = (f32[28,8,640]{2,1,0:T(8,128)S(1)}, f32[28,8,640]{2,1,0:T(8,128)S(1)}, f32[32,640]{1,0:T(8,128)S(1)}, f32[32,640]{1,0:T(8,128)S(1)}, f32[32,640]{1,0:T(8,128)S(1)}, /*index=5*/f32[32,640]{1,0:T(8,128)S(1)}) custom-call(f32[4,2,32,2048]{3,2,1,0:T(8,128)S(1)} %copy-done, f32[1,32,2048]{2,1,0:T(8,128)S(1)} %copy-done.1), custom_call_target="tpu_custom_call" | custom-call | tf_op jit(solution)/shard_map/pack/pallas_call | solution.py:257
  4.2 7.5 %collective-permute-start.1 = (f32[28,8,640]{2,1,0:T(8,128)S(1)}, f32[28,8,640]{2,1,0:T(8,128)S(1)}, u32[]{:S(2)}, u32[]{:S(2)}) collective-permute-start(f32[28,8,640]{2,1,0:T(8,128)S(1)} %get-tuple-element.13.head), channel_id=1, source_target_pairs={{1,0},{2,1},{3,2},{4,3},{5,4},{6,5},{7,6},{8,7},{9,8},{10,9},{11,1... | collective-permute-start | bytes 1720328 | tf_op jit(solution)/shard_map/ppermute | solution.py:273
  11.6 1.9 %collective-permute-start = (f32[28,8,640]{2,1,0:T(8,128)S(1)}, f32[28,8,640]{2,1,0:T(8,128)S(1)}, u32[]{:S(2)}, u32[]{:S(2)}) collective-permute-start(f32[28,8,640]{2,1,0:T(8,128)S(1)} %get-tuple-element.14.tail), channel_id=1, source_target_pairs={{0,1},{1,2},{2,3},{3,4},{4,5},{5,6},{6,7},{7,8},{8,9},{9,10},{10,1... | collective-permute-start | bytes 1720328 | tf_op jit(solution)/shard_map/ppermute | solution.py:274
  13.6 1.7 %collective-permute-start.2 = (f32[32,640]{1,0:T(8,128)S(1)}, f32[32,640]{1,0:T(8,128)S(1)}, u32[]{:S(2)}, u32[]{:S(2)}) collective-permute-start(f32[32,640]{1,0:T(8,128)S(1)} %get-tuple-element.16), channel_id=1, source_target_pairs={{0,64},{64,128},{128,192},{192,0},{1,65},{65,129},{129,193},{193,1... | collective-permute-start | bytes 245768 | tf_op jit(solution)/shard_map/ppermute | solution.py:270
  15.2 2.9 %collective-permute-start.3 = (f32[32,640]{1,0:T(8,128)S(1)}, f32[32,640]{1,0:T(8,128)S(1)}, u32[]{:S(2)}, u32[]{:S(2)}) collective-permute-start(f32[32,640]{1,0:T(8,128)S(1)} %get-tuple-element.17), channel_id=1, source_target_pairs={{0,128},{64,192},{128,0},{192,64},{1,129},{65,193},{129,1},{193,65... | collective-permute-start | bytes 245768 | tf_op jit(solution)/shard_map/ppermute | solution.py:270
  18.1 1.3 %collective-permute-start.4 = (f32[32,640]{1,0:T(8,128)S(1)}, f32[32,640]{1,0:T(8,128)S(1)}, u32[]{:S(2)}, u32[]{:S(2)}) collective-permute-start(f32[32,640]{1,0:T(8,128)S(1)} %get-tuple-element.18), channel_id=1, source_target_pairs={{0,192},{64,0},{128,64},{192,128},{1,193},{65,1},{129,65},{193,129... | collective-permute-start | bytes 245768 | tf_op jit(solution)/shard_map/ppermute | solution.py:270
  19.5 0.0 copy-done.2
  19.5 0.0 collective-permute-done.2.refs_1_
  19.5 1.9 %collective-permute-done.3.refs_2_ = f32[32,640]{1,0:T(8,128)S(1)} collective-permute-done((f32[32,640]{1,0:T(8,128)S(1)}, f32[32,640]{1,0:T(8,128)S(1)}, u32[]{:S(2)}, u32[]{:S(2)}) %collective-permute-start.3) | collective-permute-done | bytes 81952 | tf_op jit(solution)/shard_map/ppermute | solution.py:270
  21.4 1.1 %collective-permute-done.4.refs_3_ = f32[32,640]{1,0:T(8,128)S(1)} collective-permute-done((f32[32,640]{1,0:T(8,128)S(1)}, f32[32,640]{1,0:T(8,128)S(1)}, u32[]{:S(2)}, u32[]{:S(2)}) %collective-permute-start.4) | collective-permute-done | bytes 81952 | tf_op jit(solution)/shard_map/ppermute | solution.py:270
  22.6 0.1 edges.1
  22.6 1.9 %collective-permute-start.5 = (f32[80,640]{1,0:T(8,128)S(1)}, f32[80,640]{1,0:T(8,128)S(1)}, u32[]{:S(2)}, u32[]{:S(2)}) collective-permute-start(f32[80,640]{1,0:T(8,128)S(1)} %get-tuple-element.19), channel_id=1, source_target_pairs={{0,1},{1,2},{2,3},{3,4},{4,5},{5,6},{6,7},{7,8},{8,9},{9,10},{10,1... | collective-permute-start | bytes 614408 | tf_op jit(solution)/shard_map/ppermute | solution.py:286
  24.6 5.8 %collective-permute-start.6 = (f32[80,640]{1,0:T(8,128)S(1)}, f32[80,640]{1,0:T(8,128)S(1)}, u32[]{:S(2)}, u32[]{:S(2)}) collective-permute-start(f32[80,640]{1,0:T(8,128)S(1)} %get-tuple-element.20), channel_id=1, source_target_pairs={{1,0},{2,1},{3,2},{4,3},{5,4},{6,5},{7,6},{8,7},{9,8},{10,9},{11,1... | collective-permute-start | bytes 614408 | tf_op jit(solution)/shard_map/ppermute | solution.py:285
  30.3 0.0 copy-done.3
  30.4 0.1 mul.16
  30.4 0.1 maximum_maximum_fusion
  30.5 0.1 copy.6
  30.6 1.2 %collective-permute-done.5.refs_4_ = f32[80,640]{1,0:T(8,128)S(1)} collective-permute-done((f32[80,640]{1,0:T(8,128)S(1)}, f32[80,640]{1,0:T(8,128)S(1)}, u32[]{:S(2)}, u32[]{:S(2)}) %collective-permute-start.5) | collective-permute-done | bytes 204832 | tf_op jit(solution)/shard_map/ppermute | solution.py:286
  31.8 1.8 %collective-permute-done.6.refs_5_ = f32[80,640]{1,0:T(8,128)S(1)} collective-permute-done((f32[80,640]{1,0:T(8,128)S(1)}, f32[80,640]{1,0:T(8,128)S(1)}, u32[]{:S(2)}, u32[]{:S(2)}) %collective-permute-start.6) | collective-permute-done | bytes 204832 | tf_op jit(solution)/shard_map/ppermute | solution.py:285
  33.6 0.0 collective-permute-done.1.below
  33.6 0.0 collective-permute-done.above
  33.6 0.1 mul.17.refs_6_
  33.7 0.1 mul.18.refs_7_
  33.7 26.2 %migrate.1 = f32[4,32,512]{2,1,0:T(8,128)S(1)} custom-call(f32[28,8,640]{2,1,0:T(8,128)S(1)} %get-tuple-element.13.head, f32[28,8,640]{2,1,0:T(8,128)S(1)} %get-tuple-element.14.tail, f32[28,8,640]{2,1,0:T(8,128)S(1)} %collective-permute-done.above, f32[28,8,640]{2,1,0:T(8,128)S(1)} %collective-permute-done.1.below, ...), custom_call_target="tpu_custom_call" | custom-call | tf_op jit(solution)/shard_map/migrate/pallas_call | solution.py:294
  60.0 10.3 %all_to_all.18 = f32[4,32,512]{2,1,0:T(8,128)S(1)} all-to-all(f32[4,32,512]{2,1,0:T(8,128)S(1)} %migrate.1), channel_id=1, replica_groups=mesh['slab'=4,'tile'=64] {'slab'}, dimensions={0} | all-to-all | bytes 524288 | tf_op jit(solution)/shard_map/all_to_all | solution.py:303
  70.3 0.7 %copy.8 = f32[1,4,4,8,512]{4,3,1,2,0:T(8,128)} copy(f32[1,4,4,8,512]{4,3,2,1,0:T(8,128)S(1)} %bitcast.11) | data formatting | bytes 524288 | tf_op jit(solution)/shard_map/all_to_all | solution.py:303
  (4 shorter events, 0.0 us)
Async XLA Ops:
  0.0 1.6 %copy-start = (f32[4,2,32,2048]{3,2,1,0:T(8,128)S(1)}, f32[4,2,32,2048]{3,2,1,0:T(8,128)}, u32[]{:S(2)}) copy-start(f32[4,2,32,2048]{3,2,1,0:T(8,128)} %wave_ref.1) | copy-start | bytes 6291460
  1.6 0.9 %copy-start.1 = (f32[1,32,2048]{2,1,0:T(8,128)S(1)}, f32[1,32,2048]{2,1,0:T(8,128)}, u32[]{:S(2)}) copy-start(f32[1,32,2048]{2,1,0:T(8,128)} %slow_ref.1) | copy-start | bytes 786436
  2.5 16.9 %copy-start.2 = (f32[4,8,2]{1,2,0:T(2,128)S(1)}, f32[4,8,2]{1,2,0:T(2,128)}, u32[]{:S(2)}) copy-start(f32[4,8,2]{1,2,0:T(2,128)} %param.7) | copy-start | bytes 772
  2.5 27.8 %copy-start.3 = (f32[4]{0:T(128)S(1)}, f32[4]{0:T(128)}, u32[]{:S(2)}) copy-start(f32[4]{0:T(128)} %param.6) | copy-start | bytes 52
  4.2 29.4 %collective-permute-start.1 = (f32[28,8,640]{2,1,0:T(8,128)S(1)}, f32[28,8,640]{2,1,0:T(8,128)S(1)}, u32[]{:S(2)}, u32[]{:S(2)}) collective-permute-start(f32[28,8,640]{2,1,0:T(8,128)S(1)} %get-tuple-element.13.head), channel_id=1, source_target_pairs={{1,0},{2,1},{3,2},{4,3},{5,4},{6,5},{7,6},{8,7},{9,8},{10,9},{11,1... | collective-permute-start | bytes 1720328 | tf_op jit(solution)/shard_map/ppermute | solution.py:273
  11.6 21.9 %collective-permute-start = (f32[28,8,640]{2,1,0:T(8,128)S(1)}, f32[28,8,640]{2,1,0:T(8,128)S(1)}, u32[]{:S(2)}, u32[]{:S(2)}) collective-permute-start(f32[28,8,640]{2,1,0:T(8,128)S(1)} %get-tuple-element.14.tail), channel_id=1, source_target_pairs={{0,1},{1,2},{2,3},{3,4},{4,5},{5,6},{6,7},{7,8},{8,9},{9,10},{10,1... | collective-permute-start | bytes 1720328 | tf_op jit(solution)/shard_map/ppermute | solution.py:274
  13.6 5.9 %collective-permute-start.2 = (f32[32,640]{1,0:T(8,128)S(1)}, f32[32,640]{1,0:T(8,128)S(1)}, u32[]{:S(2)}, u32[]{:S(2)}) collective-permute-start(f32[32,640]{1,0:T(8,128)S(1)} %get-tuple-element.16), channel_id=1, source_target_pairs={{0,64},{64,128},{128,192},{192,0},{1,65},{65,129},{129,193},{193,1... | collective-permute-start | bytes 245768 | tf_op jit(solution)/shard_map/ppermute | solution.py:270
  15.2 6.2 %collective-permute-start.3 = (f32[32,640]{1,0:T(8,128)S(1)}, f32[32,640]{1,0:T(8,128)S(1)}, u32[]{:S(2)}, u32[]{:S(2)}) collective-permute-start(f32[32,640]{1,0:T(8,128)S(1)} %get-tuple-element.17), channel_id=1, source_target_pairs={{0,128},{64,192},{128,0},{192,64},{1,129},{65,193},{129,1},{193,65... | collective-permute-start | bytes 245768 | tf_op jit(solution)/shard_map/ppermute | solution.py:270
  18.1 4.4 %collective-permute-start.4 = (f32[32,640]{1,0:T(8,128)S(1)}, f32[32,640]{1,0:T(8,128)S(1)}, u32[]{:S(2)}, u32[]{:S(2)}) collective-permute-start(f32[32,640]{1,0:T(8,128)S(1)} %get-tuple-element.18), channel_id=1, source_target_pairs={{0,192},{64,0},{128,64},{192,128},{1,193},{65,1},{129,65},{193,129... | collective-permute-start | bytes 245768 | tf_op jit(solution)/shard_map/ppermute | solution.py:270
  22.6 9.2 %collective-permute-start.5 = (f32[80,640]{1,0:T(8,128)S(1)}, f32[80,640]{1,0:T(8,128)S(1)}, u32[]{:S(2)}, u32[]{:S(2)}) collective-permute-start(f32[80,640]{1,0:T(8,128)S(1)} %get-tuple-element.19), channel_id=1, source_target_pairs={{0,1},{1,2},{2,3},{3,4},{4,5},{5,6},{6,7},{7,8},{8,9},{9,10},{10,1... | collective-permute-start | bytes 614408 | tf_op jit(solution)/shard_map/ppermute | solution.py:286
  24.6 9.0 %collective-permute-start.6 = (f32[80,640]{1,0:T(8,128)S(1)}, f32[80,640]{1,0:T(8,128)S(1)}, u32[]{:S(2)}, u32[]{:S(2)}) collective-permute-start(f32[80,640]{1,0:T(8,128)S(1)} %get-tuple-element.20), channel_id=1, source_target_pairs={{1,0},{2,1},{3,2},{4,3},{5,4},{6,5},{7,6},{8,7},{9,8},{10,9},{11,1... | collective-permute-start | bytes 614408 | tf_op jit(solution)/shard_map/ppermute | solution.py:285

commit v3 on v2

v3 whole, which is shorter than its diff:
```python
import math

import jax
import jax.numpy as jnp
import numpy as np
from jax import lax
from jax.experimental import pallas as pl
from jax.experimental.pallas import tpu as pltpu
from jax.sharding import PartitionSpec as P

TERMS = 8
DEPTHS = 4
FREQS = 4
LANES = 128
COMPS = 2 * FREQS
HALO = DEPTHS * (TERMS - 1)
ROWS = 32
SPAN = 3 * ROWS
GRID = 2048
COLS = 512
WIDE = COLS + LANES
MOST = 20
FINISH = 8
SPREAD = 8
VMEM = pl.BlockSpec(memory_space=pltpu.VMEM)
ANY = pl.BlockSpec(memory_space=pl.ANY)
HBM = pl.BlockSpec(memory_space=pltpu.HBM)
SMEM = pl.BlockSpec(memory_space=pltpu.SMEM)
PARAMS = pltpu.CompilerParams(vmem_limit_bytes=48 * 1024 * 1024)

SCRATCH = [
    pltpu.VMEM((DEPTHS, SPAN, WIDE), jnp.float32),
    pltpu.VMEM((SPAN, COMPS, WIDE), jnp.float32),
    pltpu.VMEM((DEPTHS * ROWS, WIDE), jnp.float32),
    pltpu.VMEM((DEPTHS, ROWS, COLS), jnp.float32),
    pltpu.VMEM((2 * TERMS, COMPS, LANES), jnp.float32),
    pltpu.SemaphoreType.DMA((5 + 2 * DEPTHS,)),
] + [pltpu.VMEM((SPAN, COMPS, WIDE), jnp.float32)] * TERMS


def fit(function, low, high, count):
    angle = (np.arange(400) + 0.5) * np.pi / 400
    q = 0.5 * (low + high) + 0.5 * (high - low) * np.cos(angle)
    rows = np.stack([q**power for power in range(count)], 1)
    return np.linalg.lstsq(rows, function(q), rcond=None)[0]


COEFFICIENTS = 6
ARGUMENT_LIMIT = 1.5
SINE = fit(lambda q: np.sin(np.sqrt(q)) / np.sqrt(q), 0.0, ARGUMENT_LIMIT**2, COEFFICIENTS)
COSINE = fit(lambda q: np.cos(np.sqrt(q)), 0.0, ARGUMENT_LIMIT**2, COEFFICIENTS)


def edge_columns(right, left, block):
    right = jnp.where(block < GRID // COLS - 1, right, 0.0)
    left = jnp.where(block > 0, left, 0.0)
    lane = lax.broadcasted_iota(jnp.int32, right.shape, right.ndim - 1)
    return jnp.where(lane < LANES // 2, right, left)


def edge_starts(block):
    right = jnp.minimum(block + 1, GRID // COLS - 1) * COLS
    left = jnp.maximum(block * COLS - LANES, 0)
    return pl.multiple_of(right, LANES), pl.multiple_of(left, LANES)


def shuffle(column_axis):
    vectors = WIDE // LANES
    column = lax.broadcasted_iota(jnp.int32, (WIDE, WIDE), column_axis)
    place = lax.broadcasted_iota(jnp.int32, (WIDE, WIDE), 1 - column_axis)
    lane = place & (LANES - 1)
    here = lane * vectors + (place >> 7)
    return jnp.where(column == here, 1.0, 0.0).astype(jnp.bfloat16)


def exact_dot(rows, matrix):
    high = rows.astype(jnp.bfloat16)
    rest = rows - high.astype(jnp.float32)
    middle = rest.astype(jnp.bfloat16)
    low = (rest - middle.astype(jnp.float32)).astype(jnp.bfloat16)
    dots = [jnp.dot(part, matrix, preferred_element_type=jnp.float32) for part in (high, middle, low)]
    return (dots[0] + dots[1]) + dots[2]


def slow_kernel(slow_ref, *refs):
    pieces, (held, sem) = refs[:DEPTHS], refs[DEPTHS:]
    here = lax.axis_index("slab")
    copy = pltpu.make_async_copy(slow_ref.at[0], held, sem)
    copy.start()
    copy.wait()
    for shift, out in enumerate(pieces):
        block = lax.rem(here + shift, DEPTHS)
        right, left = edge_starts(block)
        out[:, :COLS] = held[:, pl.ds(pl.multiple_of(block * COLS, COLS), COLS)]
        out[:, COLS:] = edge_columns(held[:, pl.ds(right, LANES)], held[:, pl.ds(left, LANES)], block)


def wave_kernel(wave_ref, head_ref, tail_ref, held, edges, lined, sems):
    here = lax.axis_index("slab")
    right, left = edge_starts(here)
    start = pl.multiple_of(here * COLS, COLS)
    copies = [
        pltpu.make_async_copy(wave_ref.at[:, :, :, pl.ds(start, COLS)], held, sems.at[0]),
        pltpu.make_async_copy(wave_ref.at[:, :, :, pl.ds(right, LANES)], edges.at[0], sems.at[1]),
        pltpu.make_async_copy(wave_ref.at[:, :, :, pl.ds(left, LANES)], edges.at[1], sems.at[2]),
    ]
    for copy in copies:
        copy.start()
    matrix = shuffle(0)
    for copy in copies:
        copy.wait()
    for group in range(ROWS // 8):
        rows = slice(group * 8, group * 8 + 8)
        for piece in range(WIDE // LANES):
            lanes = slice(piece * LANES, (piece + 1) * LANES)
            parts = []
            for comp in range(2):
                for freq in range(FREQS):
                    if piece < COLS // LANES:
                        parts.append(held[freq, comp, rows, lanes])
                    else:
                        parts.append(
                            edge_columns(edges[0, freq, comp, rows], edges[1, freq, comp, rows], here)
                        )
            turned = jnp.swapaxes(jnp.stack(parts), 0, 1).reshape(8 * COMPS, LANES)
            low = group * 8 * COMPS
            lined[low : low + 8 * COMPS, lanes] = turned
    field = exact_dot(lined[...], matrix).reshape(ROWS, COMPS, WIDE)
    head_ref[...] = field[:HALO]
    tail_ref[...] = field[ROWS - HALO :]


def edge_kernel(*refs):
    pieces, (own_ref, first_ref, last_ref, lined) = refs[:DEPTHS], refs[DEPTHS:]
    here = lax.axis_index("slab")
    for shift, piece in enumerate(pieces):
        depth = lax.rem(here - shift + DEPTHS, DEPTHS)
        lined[pl.ds(pl.multiple_of(depth * ROWS, ROWS), ROWS)] = piece[...]
    own = exact_dot(lined[...], shuffle(0)).reshape(DEPTHS, ROWS, WIDE)
    own_ref[...] = own
    low = 0
    for depth in range(DEPTHS):
        count = ROWS - 8 * depth
        first_ref[low : low + count] = own[depth, :count]
        last_ref[low : low + count] = own[depth, ROWS - count :]
        low += count


def block_rows(count):
    return min(range(8, MOST + 1), key=lambda size: -(-count // size) * (size + 8))


def main_kernel(
    head, tail, above, below, own, edge_above, edge_below, omega_ref, taps_ref, *refs
):
    images, (slow, wide, mixed, held, taps, sems, *terms) = refs[:DEPTHS], refs[DEPTHS:]
    here = lax.axis_index("slab")
    copies = []

    def bring(source, target):
        copy = pltpu.make_async_copy(source, target, sems.at[len(copies)])
        copy.start()
        copies.append(copy)

    begin = ROWS - HALO
    bring(above, terms[0].at[begin:ROWS])
    bring(head, terms[0].at[ROWS : ROWS + HALO])
    bring(tail.at[HALO - begin :], terms[0].at[ROWS + HALO : 2 * ROWS])
    bring(below, terms[0].at[2 * ROWS : 2 * ROWS + HALO])
    bring(own, slow.at[:, ROWS : 2 * ROWS])
    low = 0
    for depth in range(DEPTHS):
        count = ROWS - 8 * depth
        bring(edge_above.at[low : low + count], slow.at[depth, ROWS - count : ROWS])
        bring(edge_below.at[low : low + count], slow.at[depth, 2 * ROWS : 2 * ROWS + count])
        low += count
    matrix = shuffle(1)[:, :COLS]
    sublane = lax.broadcasted_iota(jnp.int32, (COMPS, LANES), 0)
    real = sublane < FREQS

    def of_frequency(value):
        vector = jnp.full((COMPS, LANES), value(FREQS - 1), jnp.float32)
        for freq in range(FREQS - 1):
            vector = jnp.where((sublane & (FREQS - 1)) == freq, value(freq), vector)
        return vector

    def tap(part, order):
        return of_frequency(lambda freq: taps_ref[(freq * TERMS + order) * 2 + part])

    omega = of_frequency(lambda freq: 0.5 * omega_ref[freq])
    straight_taps = [tap(0, order) for order in range(TERMS)]
    crossed_taps = [jnp.where(real, tap(1, order), -tap(1, order)) for order in range(TERMS)]
    for order in range(TERMS):
        taps[order] = straight_taps[order]
        taps[TERMS + order] = crossed_taps[order]

    for copy in copies[4:]:
        copy.wait()

    def coefficient(index):
        return jnp.where(real, -float(SINE[index]), float(COSINE[index])).astype(jnp.float32)

    def rows_loop(low, high, size, body):
        full = (high - low) // size

        def step(index, carry):
            body(low + index * size, size)
            return carry

        lax.fori_loop(0, full, step, 0)
        if (high - low) % size:
            body(low + full * size, (high - low) % size)

    def covering_loop(low, high, size, body):

        def step(index, carry):
            body(jnp.minimum(low + index * size, high - size), size)
            return carry

        lax.fori_loop(0, -(-(high - low) // size), step, 0)

    for depth in range(DEPTHS):
        reach = HALO - depth * (TERMS - 1)
        lower, upper = ROWS - reach, 2 * ROWS + reach

        def spread(start, count):
            for row in range(count):
                line = slow[depth, pl.ds(start + row, 1), :] * 2.0
                wide[start + row] = jnp.broadcast_to(line, (COMPS, WIDE))

        covering_loop(lower + 1, upper - 1, SPREAD, spread)
        if depth == 0:
            for copy in copies[:4]:
                copy.wait()
        for order in range(1, TERMS):

            def apply(start, count):
                pieces = range(WIDE // LANES)

                def load(ref, at):
                    return [ref[at, :, p * LANES : (p + 1) * LANES] for p in pieces]

                here_row = load(terms[order - 1], start)
                pair = [a + b for a, b in zip(load(terms[order - 1], start - 1), here_row)]
                for row in range(count):
                    next_row = load(terms[order - 1], start + row + 1)
                    next_pair = [a + b for a, b in zip(here_row, next_row)]
                    tall = [a + b for a, b in zip(pair, next_pair)]
                    before = pltpu.roll(tall[-1], 1, 1)
                    after = pltpu.roll(tall[0], LANES - 1, 1)
                    chain = [before] + tall + [after]
                    sums = [a + b for a, b in zip(chain[:-1], chain[1:])]
                    full = [a + b for a, b in zip(sums[:-1], sums[1:])]
                    for p in pieces:
                        lanes = slice(p * LANES, (p + 1) * LANES)
                        fresh = wide[start + row, :, lanes] * (0.125 * full[p] - here_row[p])
                        if order == 1:
                            fresh = 0.5 * fresh
                        else:
                            fresh = fresh - terms[order - 2][start + row, :, lanes]
                        terms[order][start + row, :, lanes] = fresh
                    here_row, pair = next_row, next_pair

            covering_loop(lower + order, upper - order, block_rows(upper - lower - 2 * order), apply)

        def finish(start, count):
            rows = range(count)
            for piece in range(WIDE // LANES):
                lanes = slice(piece * LANES, (piece + 1) * LANES)
                straight, crossed = [None] * count, [None] * count
                for order in range(TERMS):
                    one, other = taps[order], taps[TERMS + order]
                    for row in rows:
                        term = terms[order][start + row, :, lanes]
                        along, across = one * term, other * term
                        straight[row] = along if order == 0 else straight[row] + along
                        crossed[row] = across if order == 0 else crossed[row] + across
                offsets = [omega * wide[start + row, :, lanes] - math.pi / 2 for row in rows]
                squares = [offset * offset for offset in offsets]
                polys = [coefficient(COEFFICIENTS - 1)] * count
                for index in range(COEFFICIENTS - 2, -1, -1):
                    polys = [poly * square + coefficient(index) for poly, square in zip(polys, squares)]
                for row in rows:
                    filtered = straight[row] + pltpu.roll(crossed[row], FREQS, 0)
                    own = polys[row] * jnp.where(real, offsets[row], 1.0)
                    other = pltpu.roll(own, FREQS, 0)
                    cosine = jnp.where(real, own, other)
                    sine = jnp.where(real, -other, own)
                    terms[0][start + row, :, lanes] = (
                        filtered * cosine + pltpu.roll(filtered, FREQS, 0) * sine
                    )

        rows_loop(lower + TERMS - 1, upper - TERMS + 1, FINISH, finish)

        def gather(index, carry):
            start = pl.multiple_of(index * 8, 8)
            block = terms[0][pl.ds(ROWS + start, 8)]
            mixed[pl.ds(depth * ROWS + start, 8)] = jnp.sum(block[:, :FREQS], axis=1)
            return carry

        lax.fori_loop(0, ROWS // 8, gather, 0)
    held[...] = exact_dot(mixed[...], matrix).reshape(held.shape)
    for shift, image in enumerate(images):
        image[...] = held[lax.rem(here + shift, DEPTHS)]


def join_kernel(*refs):
    pieces, (out, sems) = refs[:DEPTHS], refs[DEPTHS:]
    here = lax.axis_index("slab")
    copies = []
    for shift, piece in enumerate(pieces):
        block = lax.rem(here - shift + DEPTHS, DEPTHS)
        columns = pl.ds(pl.multiple_of(block * COLS, COLS), COLS)
        copies.append(pltpu.make_async_copy(piece, out.at[0, :, columns], sems.at[shift]))
        copies[-1].start()
    for copy in copies:
        copy.wait()


def local(wavefield, slowness, angular_freq, filter_taps):
    tiles, slabs = lax.axis_size("tile"), lax.axis_size("slab")
    f32 = jnp.float32

    def call(kernel, name, operands, places, shapes, scratch, out_place=VMEM):
        return pl.pallas_call(
            kernel,
            out_shape=[jax.ShapeDtypeStruct(shape, f32) for shape in shapes],
            in_specs=places,
            out_specs=[out_place] * len(shapes),
            scratch_shapes=scratch,
            compiler_params=PARAMS,
            name=name,
        )(*operands)

    def around(pieces):
        return [pieces[0]] + [
            lax.ppermute(pieces[k], "slab", [(i, (i + k) % slabs) for i in range(slabs)])
            for k in range(1, slabs)
        ]

    def beside(first, last):
        up = [(i + 1, i) for i in range(tiles - 1)]
        down = [(i, i + 1) for i in range(tiles - 1)]
        return lax.ppermute(first, "tile", up), lax.ppermute(last, "tile", down)

    dma = pltpu.SemaphoreType.DMA
    pieces = call(
        slow_kernel, "slow", (slowness,), [HBM], [(ROWS, WIDE)] * DEPTHS,
        [pltpu.VMEM((ROWS, GRID), f32), dma],
    )
    pieces = around(pieces)
    head, tail = call(
        wave_kernel, "wave", (wavefield,), [HBM], [(HALO, COMPS, WIDE)] * 2,
        [
            pltpu.VMEM((FREQS, 2, ROWS, COLS), f32),
            pltpu.VMEM((2, FREQS, 2, ROWS, LANES), f32),
            pltpu.VMEM((ROWS * COMPS, WIDE), f32),
            dma((3,)),
        ],
    )
    below, above = beside(head, tail)
    edge_rows = sum(ROWS - 8 * depth for depth in range(DEPTHS))
    own, first, last = call(
        edge_kernel, "edges", pieces, [VMEM] * DEPTHS,
        [(DEPTHS, ROWS, WIDE)] + [(edge_rows, WIDE)] * 2,
        [pltpu.VMEM((DEPTHS * ROWS, WIDE), f32)],
    )
    edge_below, edge_above = beside(first, last)
    images = call(
        main_kernel, "migrate",
        (head, tail, above, below, own, edge_above, edge_below, angular_freq, filter_taps.reshape(-1)),
        [ANY] * 7 + [SMEM] * 2, [(ROWS, COLS)] * DEPTHS, SCRATCH,
    )
    return call(
        join_kernel, "join", around(images), [ANY] * DEPTHS, [(1, ROWS, GRID)], [dma((DEPTHS,))], ANY
    )[0]


def solution(mesh):
    placed = (P(None, None, "tile", None), P("slab", "tile", None), P(), P())
    return jax.shard_map(
        local, mesh=mesh, in_specs=placed, out_specs=P("slab", "tile", None), check_vma=False
    )
```

time: 71.3 us -> 66.7 us (0.935)
  blocking collectives: 10.3 us -> 0 us
  starting transfers between devices: 23 us -> 27.3 us
  waiting for transfers between devices: 6.07 us -> 10.1 us
  local copies, waits for them, and re-layouts: 3.57 us -> 1.8 us
  Pallas kernels: 27.9 us -> 27.1 us
    all_to_all x1 -> x0, blocking collectives: 10.3 us -> none  [local(): return lax.all_to_all(image, 'slab', 0, 2, tiled=True)]
    ppermute x7 -> x10, starting transfers between devices: 23 us -> 27.3 us  [the longest x4 17.1 us: beside(): return (lax.ppermute(first, 'tile', up), lax.ppermute(last, 'tile', down))]
    ppermute x7 -> x10, waiting for transfers between devices: 6.07 us -> 10.1 us  [the longest x6 7.08 us: around(): lax.ppermute(pieces[k], 'slab', [(i, (i + k) % slabs) for i in range(slab...]
    unnamed x8 -> x9, local copies, waits for them, and re-layouts: 2.55 us -> 1.7 us
    pallas_call x3 -> x5, Pallas kernels: 27.9 us -> 27.1 us  [call(): pl.pallas_call(kernel, out_shape=[jax.ShapeDtypeStruct(shape, f32) for sh...]
    all_to_all x1 -> x0, local copies, waits for them, and re-layouts: 0.72 us -> none  [local(): return lax.all_to_all(image, 'slab', 0, 2, tiled=True)]
  transfers between devices with their start and end apart: 7 -> 10, of which waited for: 4 -> 7; matrix products, arithmetic and copies ran while one was open for 0% -> 0% of each run, Pallas kernels for 0% -> 1%
where the time goes in v3:
time: 66.7 us; the launch traced here: 66.5 us
  starting transfers between devices  27.3 us (41%)
  Pallas kernels  27.1 us (41%)
  waiting for transfers between devices  10.1 us (15%)
  local copies, waits for them, and re-layouts  1.8 us (3%)
    pallas_call x5, Pallas kernels, call(): pl.pallas_call(kernel, out_shape=[jax.ShapeDtypeStruct(shape, f32) for sh...  27.1 us
    ppermute x4, starting transfers between devices, beside(): return (lax.ppermute(first, 'tile', up), lax.ppermute(last, 'tile', down))  17.1 us
    ppermute x6, starting transfers between devices, around(): lax.ppermute(pieces[k], 'slab', [(i, (i + k) % slabs) for i in range(slab...  10.3 us
    ppermute x6, waiting for transfers between devices, around(): lax.ppermute(pieces[k], 'slab', [(i, (i + k) % slabs) for i in range(slab...  7.08 us
    ppermute x4, waiting for transfers between devices, beside(): return (lax.ppermute(first, 'tile', up), lax.ppermute(last, 'tile', down))  3.04 us
    unnamed x9, local copies, waits for them, and re-layouts  1.7 us
  transfers between devices with their start and end apart: 10, of which 7 were waited for; matrix products, arithmetic and copies ran while one was open for 0% of the time, Pallas kernels for 1%

profile of v3, /device:TPU:6, one launch (start us, length us, event | category | flops | bytes accessed | tf_op | source)
XLA Modules:
  0.0 66.5 jit_solution(6758233640241695515)
XLA Ops:
  0.0 0.0 copy-start
  0.0 1.6 %copy-done = f32[4,2,32,2048]{3,2,1,0:T(8,128)S(1)} copy-done((f32[4,2,32,2048]{3,2,1,0:T(8,128)S(1)}, f32[4,2,32,2048]{3,2,1,0:T(8,128)}, u32[]{:S(2)}) %copy-start) | copy-done | bytes 2097176
  1.6 0.0 copy-start.1
  1.6 0.0 copy-start.3
  1.6 0.0 copy-start.2
  1.6 1.5 %wave.1 = (f32[28,8,640]{2,1,0:T(8,128)S(1)}, f32[28,8,640]{2,1,0:T(8,128)S(1)}) custom-call(f32[4,2,32,2048]{3,2,1,0:T(8,128)S(1)} %copy-done), custom_call_target="tpu_custom_call" | custom-call | tf_op jit(solution)/shard_map/wave/pallas_call | solution.py:325
  3.1 7.5 %collective-permute-start.1 = (f32[28,8,640]{2,1,0:T(8,128)S(1)}, f32[28,8,640]{2,1,0:T(8,128)S(1)}, u32[]{:S(2)}, u32[]{:S(2)}) collective-permute-start(f32[28,8,640]{2,1,0:T(8,128)S(1)} %get-tuple-element.18.head), channel_id=1, source_target_pairs={{1,0},{2,1},{3,2},{4,3},{5,4},{6,5},{7,6},{8,7},{9,8},{10,9},{11,1... | collective-permute-start | bytes 1720328 | tf_op jit(solution)/shard_map/ppermute | solution.py:344
  10.5 1.9 %collective-permute-start = (f32[28,8,640]{2,1,0:T(8,128)S(1)}, f32[28,8,640]{2,1,0:T(8,128)S(1)}, u32[]{:S(2)}, u32[]{:S(2)}) collective-permute-start(f32[28,8,640]{2,1,0:T(8,128)S(1)} %get-tuple-element.19.tail), channel_id=1, source_target_pairs={{0,1},{1,2},{2,3},{3,4},{4,5},{5,6},{6,7},{7,8},{8,9},{9,10},{10,1... | collective-permute-start | bytes 1720328 | tf_op jit(solution)/shard_map/ppermute | solution.py:344
  12.5 0.0 copy-done.1
  12.5 0.1 slow.1
  12.6 1.7 %collective-permute-start.2 = (f32[32,640]{1,0:T(8,128)S(1)}, f32[32,640]{1,0:T(8,128)S(1)}, u32[]{:S(2)}, u32[]{:S(2)}) collective-permute-start(f32[32,640]{1,0:T(8,128)S(1)} %get-tuple-element.21), channel_id=1, source_target_pairs={{0,64},{64,128},{128,192},{192,0},{1,65},{65,129},{129,193},{193,1... | collective-permute-start | bytes 245768 | tf_op jit(solution)/shard_map/ppermute | solution.py:337
  14.2 2.9 %collective-permute-start.3 = (f32[32,640]{1,0:T(8,128)S(1)}, f32[32,640]{1,0:T(8,128)S(1)}, u32[]{:S(2)}, u32[]{:S(2)}) collective-permute-start(f32[32,640]{1,0:T(8,128)S(1)} %get-tuple-element.22), channel_id=1, source_target_pairs={{0,128},{64,192},{128,0},{192,64},{1,129},{65,193},{129,1},{193,65... | collective-permute-start | bytes 245768 | tf_op jit(solution)/shard_map/ppermute | solution.py:337
  17.1 1.3 %collective-permute-start.4 = (f32[32,640]{1,0:T(8,128)S(1)}, f32[32,640]{1,0:T(8,128)S(1)}, u32[]{:S(2)}, u32[]{:S(2)}) collective-permute-start(f32[32,640]{1,0:T(8,128)S(1)} %get-tuple-element.23), channel_id=1, source_target_pairs={{0,192},{64,0},{128,64},{192,128},{1,193},{65,1},{129,65},{193,129... | collective-permute-start | bytes 245768 | tf_op jit(solution)/shard_map/ppermute | solution.py:337
  18.5 0.0 collective-permute-done.2.refs_1_
  18.5 1.9 %collective-permute-done.3.refs_2_ = f32[32,640]{1,0:T(8,128)S(1)} collective-permute-done((f32[32,640]{1,0:T(8,128)S(1)}, f32[32,640]{1,0:T(8,128)S(1)}, u32[]{:S(2)}, u32[]{:S(2)}) %collective-permute-start.3) | collective-permute-done | bytes 81952 | tf_op jit(solution)/shard_map/ppermute | solution.py:337
  20.4 1.1 %collective-permute-done.4.refs_3_ = f32[32,640]{1,0:T(8,128)S(1)} collective-permute-done((f32[32,640]{1,0:T(8,128)S(1)}, f32[32,640]{1,0:T(8,128)S(1)}, u32[]{:S(2)}, u32[]{:S(2)}) %collective-permute-start.4) | collective-permute-done | bytes 81952 | tf_op jit(solution)/shard_map/ppermute | solution.py:337
  21.6 0.8 %edges.1 = (f32[4,32,640]{2,1,0:T(8,128)S(1)}, f32[80,640]{1,0:T(8,128)S(1)}, f32[80,640]{1,0:T(8,128)S(1)}) custom-call(f32[32,640]{1,0:T(8,128)S(1)} %get-tuple-element.20.refs_0_, f32[32,640]{1,0:T(8,128)S(1)} %collective-permute-done.2.refs_1_, f32[32,640]{1,0:T(8,128)S(1)} %collective-permute-done.3.refs_2_, f32[32,640]{1,0:T(8,128)S(1)} %collective-permute-done.4.refs_3_), custom_call_target="tpu_custom_call" | custom-call | tf_op jit(solution)/shard_map/edges/pallas_call | solution.py:325
  22.3 1.9 %collective-permute-start.5 = (f32[80,640]{1,0:T(8,128)S(1)}, f32[80,640]{1,0:T(8,128)S(1)}, u32[]{:S(2)}, u32[]{:S(2)}) collective-permute-start(f32[80,640]{1,0:T(8,128)S(1)} %get-tuple-element.25), channel_id=1, source_target_pairs={{0,1},{1,2},{2,3},{3,4},{4,5},{5,6},{6,7},{7,8},{8,9},{9,10},{10,1... | collective-permute-start | bytes 614408 | tf_op jit(solution)/shard_map/ppermute | solution.py:344
  24.3 5.8 %collective-permute-start.6 = (f32[80,640]{1,0:T(8,128)S(1)}, f32[80,640]{1,0:T(8,128)S(1)}, u32[]{:S(2)}, u32[]{:S(2)}) collective-permute-start(f32[80,640]{1,0:T(8,128)S(1)} %get-tuple-element.26), channel_id=1, source_target_pairs={{1,0},{2,1},{3,2},{4,3},{5,4},{6,5},{7,6},{8,7},{9,8},{10,9},{11,1... | collective-permute-start | bytes 614408 | tf_op jit(solution)/shard_map/ppermute | solution.py:344
  30.0 0.0 copy-done.3
  30.0 0.1 copy.6
  30.1 0.1 reshape.3.taps_ref
  30.2 1.3 %collective-permute-done.5.edge_above = f32[80,640]{1,0:T(8,128)S(1)} collective-permute-done((f32[80,640]{1,0:T(8,128)S(1)}, f32[80,640]{1,0:T(8,128)S(1)}, u32[]{:S(2)}, u32[]{:S(2)}) %collective-permute-start.5) | collective-permute-done | bytes 204832 | tf_op jit(solution)/shard_map/ppermute | solution.py:344
  31.5 1.8 %collective-permute-done.6.edge_below = f32[80,640]{1,0:T(8,128)S(1)} collective-permute-done((f32[80,640]{1,0:T(8,128)S(1)}, f32[80,640]{1,0:T(8,128)S(1)}, u32[]{:S(2)}, u32[]{:S(2)}) %collective-permute-start.6) | collective-permute-done | bytes 204832 | tf_op jit(solution)/shard_map/ppermute | solution.py:344
  33.3 0.0 collective-permute-done.1.below
  33.3 0.0 collective-permute-done.above
  33.3 0.0 copy-done.2
  33.3 24.1 %migrate.1 = (f32[32,512]{1,0:T(8,128)S(1)}, f32[32,512]{1,0:T(8,128)S(1)}, f32[32,512]{1,0:T(8,128)S(1)}, f32[32,512]{1,0:T(8,128)S(1)}) custom-call(f32[28,8,640]{2,1,0:T(8,128)S(1)} %get-tuple-element.18.head, f32[28,8,640]{2,1,0:T(8,128)S(1)} %get-tuple-element.19.tail, f32[28,8,640]{2,1,0:T(8,128)S(1)} %collective-permute-done.above, ...), custom_call_target="tpu_custom_call" | custom-call | tf_op jit(solution)/shard_map/migrate/pallas_call | solution.py:325
  57.4 0.6 collective-permute-start.7
  57.9 3.5 %collective-permute-start.8 = (f32[32,512]{1,0:T(8,128)S(1)}, f32[32,512]{1,0:T(8,128)S(1)}, u32[]{:S(2)}, u32[]{:S(2)}) collective-permute-start(f32[32,512]{1,0:T(8,128)S(1)} %get-tuple-element.29), channel_id=1, source_target_pairs={{0,128},{64,192},{128,0},{192,64},{1,129},{65,193},{129,1},{193,65... | collective-permute-start | bytes 196616 | tf_op jit(solution)/shard_map/ppermute | solution.py:337
  61.5 0.3 collective-permute-start.9
  61.7 1.2 %collective-permute-done.7.refs_1_ = f32[32,512]{1,0:T(8,128)S(1)} collective-permute-done((f32[32,512]{1,0:T(8,128)S(1)}, f32[32,512]{1,0:T(8,128)S(1)}, u32[]{:S(2)}, u32[]{:S(2)}) %collective-permute-start.7) | collective-permute-done | bytes 65568 | tf_op jit(solution)/shard_map/ppermute | solution.py:337
  62.9 1.5 %collective-permute-done.8.refs_2_ = f32[32,512]{1,0:T(8,128)S(1)} collective-permute-done((f32[32,512]{1,0:T(8,128)S(1)}, f32[32,512]{1,0:T(8,128)S(1)}, u32[]{:S(2)}, u32[]{:S(2)}) %collective-permute-start.8) | collective-permute-done | bytes 65568 | tf_op jit(solution)/shard_map/ppermute | solution.py:337
  64.4 1.3 %collective-permute-done.9.refs_3_ = f32[32,512]{1,0:T(8,128)S(1)} collective-permute-done((f32[32,512]{1,0:T(8,128)S(1)}, f32[32,512]{1,0:T(8,128)S(1)}, u32[]{:S(2)}, u32[]{:S(2)}) %collective-permute-start.9) | collective-permute-done | bytes 65568 | tf_op jit(solution)/shard_map/ppermute | solution.py:337
  65.7 0.7 %join.1 = f32[1,32,2048]{2,1,0:T(8,128)} custom-call(f32[32,512]{1,0:T(8,128)S(1)} %get-tuple-element.27.refs_0_, f32[32,512]{1,0:T(8,128)S(1)} %collective-permute-done.7.refs_1_, f32[32,512]{1,0:T(8,128)S(1)} %collective-permute-done.8.refs_2_, f32[32,512]{1,0:T(8,128)S(1)} %collective-permute-done.9.refs_3_), custom_call_target="tpu_custom_call" | custom-call | tf_op jit(solution)/shard_map/join/pallas_call | solution.py:325
Async XLA Ops:
  0.0 1.6 %copy-start = (f32[4,2,32,2048]{3,2,1,0:T(8,128)S(1)}, f32[4,2,32,2048]{3,2,1,0:T(8,128)}, u32[]{:S(2)}) copy-start(f32[4,2,32,2048]{3,2,1,0:T(8,128)} %wave_ref.1) | copy-start | bytes 6291460
  1.6 10.9 %copy-start.1 = (f32[1,32,2048]{2,1,0:T(8,128)S(1)}, f32[1,32,2048]{2,1,0:T(8,128)}, u32[]{:S(2)}) copy-start(f32[1,32,2048]{2,1,0:T(8,128)} %slow_ref.1) | copy-start | bytes 786436
  1.6 28.4 %copy-start.3 = (f32[4,8,2]{1,2,0:T(2,128)S(1)}, f32[4,8,2]{1,2,0:T(2,128)}, u32[]{:S(2)}) copy-start(f32[4,8,2]{1,2,0:T(2,128)} %param.7) | copy-start | bytes 772
  1.6 31.7 %copy-start.2 = (f32[4]{0:T(128)S(1)}, f32[4]{0:T(128)}, u32[]{:S(2)}) copy-start(f32[4]{0:T(128)} %omega_ref.1) | copy-start | bytes 52
  3.1 30.2 %collective-permute-start.1 = (f32[28,8,640]{2,1,0:T(8,128)S(1)}, f32[28,8,640]{2,1,0:T(8,128)S(1)}, u32[]{:S(2)}, u32[]{:S(2)}) collective-permute-start(f32[28,8,640]{2,1,0:T(8,128)S(1)} %get-tuple-element.18.head), channel_id=1, source_target_pairs={{1,0},{2,1},{3,2},{4,3},{5,4},{6,5},{7,6},{8,7},{9,8},{10,9},{11,1... | collective-permute-start | bytes 1720328 | tf_op jit(solution)/shard_map/ppermute | solution.py:344
  10.5 22.7 %collective-permute-start = (f32[28,8,640]{2,1,0:T(8,128)S(1)}, f32[28,8,640]{2,1,0:T(8,128)S(1)}, u32[]{:S(2)}, u32[]{:S(2)}) collective-permute-start(f32[28,8,640]{2,1,0:T(8,128)S(1)} %get-tuple-element.19.tail), channel_id=1, source_target_pairs={{0,1},{1,2},{2,3},{3,4},{4,5},{5,6},{6,7},{7,8},{8,9},{9,10},{10,1... | collective-permute-start | bytes 1720328 | tf_op jit(solution)/shard_map/ppermute | solution.py:344
  12.6 5.9 %collective-permute-start.2 = (f32[32,640]{1,0:T(8,128)S(1)}, f32[32,640]{1,0:T(8,128)S(1)}, u32[]{:S(2)}, u32[]{:S(2)}) collective-permute-start(f32[32,640]{1,0:T(8,128)S(1)} %get-tuple-element.21), channel_id=1, source_target_pairs={{0,64},{64,128},{128,192},{192,0},{1,65},{65,129},{129,193},{193,1... | collective-permute-start | bytes 245768 | tf_op jit(solution)/shard_map/ppermute | solution.py:337
  14.2 6.2 %collective-permute-start.3 = (f32[32,640]{1,0:T(8,128)S(1)}, f32[32,640]{1,0:T(8,128)S(1)}, u32[]{:S(2)}, u32[]{:S(2)}) collective-permute-start(f32[32,640]{1,0:T(8,128)S(1)} %get-tuple-element.22), channel_id=1, source_target_pairs={{0,128},{64,192},{128,0},{192,64},{1,129},{65,193},{129,1},{193,65... | collective-permute-start | bytes 245768 | tf_op jit(solution)/shard_map/ppermute | solution.py:337
  17.1 4.4 %collective-permute-start.4 = (f32[32,640]{1,0:T(8,128)S(1)}, f32[32,640]{1,0:T(8,128)S(1)}, u32[]{:S(2)}, u32[]{:S(2)}) collective-permute-start(f32[32,640]{1,0:T(8,128)S(1)} %get-tuple-element.23), channel_id=1, source_target_pairs={{0,192},{64,0},{128,64},{192,128},{1,193},{65,1},{129,65},{193,129... | collective-permute-start | bytes 245768 | tf_op jit(solution)/shard_map/ppermute | solution.py:337
  22.3 9.2 %collective-permute-start.5 = (f32[80,640]{1,0:T(8,128)S(1)}, f32[80,640]{1,0:T(8,128)S(1)}, u32[]{:S(2)}, u32[]{:S(2)}) collective-permute-start(f32[80,640]{1,0:T(8,128)S(1)} %get-tuple-element.25), channel_id=1, source_target_pairs={{0,1},{1,2},{2,3},{3,4},{4,5},{5,6},{6,7},{7,8},{8,9},{9,10},{10,1... | collective-permute-start | bytes 614408 | tf_op jit(solution)/shard_map/ppermute | solution.py:344
  24.3 9.0 %collective-permute-start.6 = (f32[80,640]{1,0:T(8,128)S(1)}, f32[80,640]{1,0:T(8,128)S(1)}, u32[]{:S(2)}, u32[]{:S(2)}) collective-permute-start(f32[80,640]{1,0:T(8,128)S(1)} %get-tuple-element.26), channel_id=1, source_target_pairs={{1,0},{2,1},{3,2},{4,3},{5,4},{6,5},{7,6},{8,7},{9,8},{10,9},{11,1... | collective-permute-start | bytes 614408 | tf_op jit(solution)/shard_map/ppermute | solution.py:344
  57.4 5.6 %collective-permute-start.7 = (f32[32,512]{1,0:T(8,128)S(1)}, f32[32,512]{1,0:T(8,128)S(1)}, u32[]{:S(2)}, u32[]{:S(2)}) collective-permute-start(f32[32,512]{1,0:T(8,128)S(1)} %get-tuple-element.28), channel_id=1, source_target_pairs={{0,64},{64,128},{128,192},{192,0},{1,65},{65,129},{129,193},{193,1... | collective-permute-start | bytes 196616 | tf_op jit(solution)/shard_map/ppermute | solution.py:337
  57.9 6.5 %collective-permute-start.8 = (f32[32,512]{1,0:T(8,128)S(1)}, f32[32,512]{1,0:T(8,128)S(1)}, u32[]{:S(2)}, u32[]{:S(2)}) collective-permute-start(f32[32,512]{1,0:T(8,128)S(1)} %get-tuple-element.29), channel_id=1, source_target_pairs={{0,128},{64,192},{128,0},{192,64},{1,129},{65,193},{129,1},{193,65... | collective-permute-start | bytes 196616 | tf_op jit(solution)/shard_map/ppermute | solution.py:337
  61.5 4.3 %collective-permute-start.9 = (f32[32,512]{1,0:T(8,128)S(1)}, f32[32,512]{1,0:T(8,128)S(1)}, u32[]{:S(2)}, u32[]{:S(2)}) collective-permute-start(f32[32,512]{1,0:T(8,128)S(1)} %get-tuple-element.30), channel_id=1, source_target_pairs={{0,192},{64,0},{128,64},{192,128},{1,193},{65,1},{129,65},{193,129... | collective-permute-start | bytes 196616 | tf_op jit(solution)/shard_map/ppermute | solution.py:337

commit v4 on v3

--- a/solution.py
+++ b/solution.py
@@ -19,7 +19,7 @@
 GRID = 2048
 COLS = 512
 WIDE = COLS + LANES
-MOST = 20
+MOST = 32
 FINISH = 8
 SPREAD = 8
 VMEM = pl.BlockSpec(memory_space=pltpu.VMEM)
@@ -34,7 +34,6 @@
     pltpu.VMEM((DEPTHS * ROWS, WIDE), jnp.float32),
     pltpu.VMEM((DEPTHS, ROWS, COLS), jnp.float32),
     pltpu.VMEM((2 * TERMS, COMPS, LANES), jnp.float32),
-    pltpu.SemaphoreType.DMA((5 + 2 * DEPTHS,)),
 ] + [pltpu.VMEM((SPAN, COMPS, WIDE), jnp.float32)] * TERMS
 
 
@@ -153,26 +152,19 @@
 def main_kernel(
     head, tail, above, below, own, edge_above, edge_below, omega_ref, taps_ref, *refs
 ):
-    images, (slow, wide, mixed, held, taps, sems, *terms) = refs[:DEPTHS], refs[DEPTHS:]
-    here = lax.axis_index("slab")
-    copies = []
-
-    def bring(source, target):
-        copy = pltpu.make_async_copy(source, target, sems.at[len(copies)])
-        copy.start()
-        copies.append(copy)
-
+    images, (slow, wide, mixed, held, taps, *terms) = refs[:DEPTHS], refs[DEPTHS:]
+    here = lax.axis_index("slab")
     begin = ROWS - HALO
-    bring(above, terms[0].at[begin:ROWS])
-    bring(head, terms[0].at[ROWS : ROWS + HALO])
-    bring(tail.at[HALO - begin :], terms[0].at[ROWS + HALO : 2 * ROWS])
-    bring(below, terms[0].at[2 * ROWS : 2 * ROWS + HALO])
-    bring(own, slow.at[:, ROWS : 2 * ROWS])
+    terms[0][begin:ROWS] = above[...]
+    terms[0][ROWS : ROWS + HALO] = head[...]
+    terms[0][ROWS + HALO : 2 * ROWS] = tail[HALO - begin :]
+    terms[0][2 * ROWS : 2 * ROWS + HALO] = below[...]
+    slow[:, ROWS : 2 * ROWS] = own[...]
     low = 0
     for depth in range(DEPTHS):
         count = ROWS - 8 * depth
-        bring(edge_above.at[low : low + count], slow.at[depth, ROWS - count : ROWS])
-        bring(edge_below.at[low : low + count], slow.at[depth, 2 * ROWS : 2 * ROWS + count])
+        slow[depth, ROWS - count : ROWS] = edge_above[low : low + count]
+        slow[depth, 2 * ROWS : 2 * ROWS + count] = edge_below[low : low + count]
         low += count
     matrix = shuffle(1)[:, :COLS]
     sublane = lax.broadcasted_iota(jnp.int32, (COMPS, LANES), 0)
@@ -185,7 +177,7 @@
         return vector
 
     def tap(part, order):
-        return of_frequency(lambda freq: taps_ref[(freq * TERMS + order) * 2 + part])
+        return of_frequency(lambda freq: taps_ref[freq, order, part])
 
     omega = of_frequency(lambda freq: 0.5 * omega_ref[freq])
     straight_taps = [tap(0, order) for order in range(TERMS)]
@@ -194,9 +186,6 @@
         taps[order] = straight_taps[order]
         taps[TERMS + order] = crossed_taps[order]
 
-    for copy in copies[4:]:
-        copy.wait()
-
     def coefficient(index):
         return jnp.where(real, -float(SINE[index]), float(COSINE[index])).astype(jnp.float32)
 
@@ -229,9 +218,6 @@
                 wide[start + row] = jnp.broadcast_to(line, (COMPS, WIDE))
 
         covering_loop(lower + 1, upper - 1, SPREAD, spread)
-        if depth == 0:
-            for copy in copies[:4]:
-                copy.wait()
         for order in range(1, TERMS):
 
             def apply(start, count):
@@ -368,8 +354,8 @@
     edge_below, edge_above = beside(first, last)
     images = call(
         main_kernel, "migrate",
-        (head, tail, above, below, own, edge_above, edge_below, angular_freq, filter_taps.reshape(-1)),
-        [ANY] * 7 + [SMEM] * 2, [(ROWS, COLS)] * DEPTHS, SCRATCH,
+        (head, tail, above, below, own, edge_above, edge_below, angular_freq, filter_taps),
+        [VMEM] * 7 + [SMEM] * 2, [(ROWS, COLS)] * DEPTHS, SCRATCH,
     )
     return call(
         join_kernel, "join", around(images), [ANY] * DEPTHS, [(1, ROWS, GRID)], [dma((DEPTHS,))], ANY

time: 66.7 us -> 65 us (0.975)
  Pallas kernels: 27.1 us -> 25.2 us
    pallas_call x5, Pallas kernels: 27.1 us -> 25.2 us  [call(): pl.pallas_call(kernel, out_shape=[jax.ShapeDtypeStruct(shape, f32) for sh...]
where the time goes in v4:
time: 65 us; the launch traced here: 64.8 us
  starting transfers between devices  27.5 us (42%)
  Pallas kernels  25.2 us (39%)
  waiting for transfers between devices  10 us (15%)
  local copies, waits for them, and re-layouts  1.7 us (3%)
    pallas_call x5, Pallas kernels, call(): pl.pallas_call(kernel, out_shape=[jax.ShapeDtypeStruct(shape, f32) for sh...  25.2 us
    ppermute x4, starting transfers between devices, beside(): return (lax.ppermute(first, 'tile', up), lax.ppermute(last, 'tile', down))  17.2 us
    ppermute x6, starting transfers between devices, around(): lax.ppermute(pieces[k], 'slab', [(i, (i + k) % slabs) for i in range(slab...  10.3 us
    ppermute x6, waiting for transfers between devices, around(): lax.ppermute(pieces[k], 'slab', [(i, (i + k) % slabs) for i in range(slab...  7.08 us
    ppermute x4, waiting for transfers between devices, beside(): return (lax.ppermute(first, 'tile', up), lax.ppermute(last, 'tile', down))  2.97 us
    unnamed x9, local copies, waits for them, and re-layouts  1.7 us
  transfers between devices with their start and end apart: 10, of which 7 were waited for; matrix products, arithmetic and copies ran while one was open for 0% of the time, Pallas kernels for 1%

profile of v4, /device:TPU:6, one launch (start us, length us, event | category | flops | bytes accessed | tf_op | source)
XLA Modules:
  0.0 64.8 jit_solution(5763783772782589122)
XLA Ops:
  0.0 0.0 copy-start
  0.0 1.6 %copy-done = f32[4,2,32,2048]{3,2,1,0:T(8,128)S(1)} copy-done((f32[4,2,32,2048]{3,2,1,0:T(8,128)S(1)}, f32[4,2,32,2048]{3,2,1,0:T(8,128)}, u32[]{:S(2)}) %copy-start) | copy-done | bytes 2097176
  1.6 0.0 copy-start.1
  1.6 0.0 copy-start.3
  1.6 0.0 copy-start.2
  1.6 1.5 %wave.1 = (f32[28,8,640]{2,1,0:T(8,128)S(1)}, f32[28,8,640]{2,1,0:T(8,128)S(1)}) custom-call(f32[4,2,32,2048]{3,2,1,0:T(8,128)S(1)} %copy-done), custom_call_target="tpu_custom_call" | custom-call | tf_op jit(solution)/shard_map/wave/pallas_call | solution.py:311
  3.1 7.5 %collective-permute-start.1 = (f32[28,8,640]{2,1,0:T(8,128)S(1)}, f32[28,8,640]{2,1,0:T(8,128)S(1)}, u32[]{:S(2)}, u32[]{:S(2)}) collective-permute-start(f32[28,8,640]{2,1,0:T(8,128)S(1)} %get-tuple-element.18.head), channel_id=1, source_target_pairs={{1,0},{2,1},{3,2},{4,3},{5,4},{6,5},{7,6},{8,7},{9,8},{10,9},{11,1... | collective-permute-start | bytes 1720328 | tf_op jit(solution)/shard_map/ppermute | solution.py:330
  10.5 1.9 %collective-permute-start = (f32[28,8,640]{2,1,0:T(8,128)S(1)}, f32[28,8,640]{2,1,0:T(8,128)S(1)}, u32[]{:S(2)}, u32[]{:S(2)}) collective-permute-start(f32[28,8,640]{2,1,0:T(8,128)S(1)} %get-tuple-element.19.tail), channel_id=1, source_target_pairs={{0,1},{1,2},{2,3},{3,4},{4,5},{5,6},{6,7},{7,8},{8,9},{9,10},{10,1... | collective-permute-start | bytes 1720328 | tf_op jit(solution)/shard_map/ppermute | solution.py:330
  12.5 0.0 copy-done.1
  12.5 0.1 slow.1
  12.6 1.7 %collective-permute-start.2 = (f32[32,640]{1,0:T(8,128)S(1)}, f32[32,640]{1,0:T(8,128)S(1)}, u32[]{:S(2)}, u32[]{:S(2)}) collective-permute-start(f32[32,640]{1,0:T(8,128)S(1)} %get-tuple-element.21), channel_id=1, source_target_pairs={{0,64},{64,128},{128,192},{192,0},{1,65},{65,129},{129,193},{193,1... | collective-permute-start | bytes 245768 | tf_op jit(solution)/shard_map/ppermute | solution.py:323
  14.2 2.9 %collective-permute-start.3 = (f32[32,640]{1,0:T(8,128)S(1)}, f32[32,640]{1,0:T(8,128)S(1)}, u32[]{:S(2)}, u32[]{:S(2)}) collective-permute-start(f32[32,640]{1,0:T(8,128)S(1)} %get-tuple-element.22), channel_id=1, source_target_pairs={{0,128},{64,192},{128,0},{192,64},{1,129},{65,193},{129,1},{193,65... | collective-permute-start | bytes 245768 | tf_op jit(solution)/shard_map/ppermute | solution.py:323
  17.1 1.3 %collective-permute-start.4 = (f32[32,640]{1,0:T(8,128)S(1)}, f32[32,640]{1,0:T(8,128)S(1)}, u32[]{:S(2)}, u32[]{:S(2)}) collective-permute-start(f32[32,640]{1,0:T(8,128)S(1)} %get-tuple-element.23), channel_id=1, source_target_pairs={{0,192},{64,0},{128,64},{192,128},{1,193},{65,1},{129,65},{193,129... | collective-permute-start | bytes 245768 | tf_op jit(solution)/shard_map/ppermute | solution.py:323
  18.5 0.0 collective-permute-done.2.refs_1_
  18.5 1.9 %collective-permute-done.3.refs_2_ = f32[32,640]{1,0:T(8,128)S(1)} collective-permute-done((f32[32,640]{1,0:T(8,128)S(1)}, f32[32,640]{1,0:T(8,128)S(1)}, u32[]{:S(2)}, u32[]{:S(2)}) %collective-permute-start.3) | collective-permute-done | bytes 81952 | tf_op jit(solution)/shard_map/ppermute | solution.py:323
  20.4 1.1 %collective-permute-done.4.refs_3_ = f32[32,640]{1,0:T(8,128)S(1)} collective-permute-done((f32[32,640]{1,0:T(8,128)S(1)}, f32[32,640]{1,0:T(8,128)S(1)}, u32[]{:S(2)}, u32[]{:S(2)}) %collective-permute-start.4) | collective-permute-done | bytes 81952 | tf_op jit(solution)/shard_map/ppermute | solution.py:323
  21.6 0.8 %edges.1 = (f32[4,32,640]{2,1,0:T(8,128)S(1)}, f32[80,640]{1,0:T(8,128)S(1)}, f32[80,640]{1,0:T(8,128)S(1)}) custom-call(f32[32,640]{1,0:T(8,128)S(1)} %get-tuple-element.20.refs_0_, f32[32,640]{1,0:T(8,128)S(1)} %collective-permute-done.2.refs_1_, f32[32,640]{1,0:T(8,128)S(1)} %collective-permute-done.3.refs_2_, f32[32,640]{1,0:T(8,128)S(1)} %collective-permute-done.4.refs_3_), custom_call_target="tpu_custom_call" | custom-call | tf_op jit(solution)/shard_map/edges/pallas_call | solution.py:311
  22.3 1.9 %collective-permute-start.5 = (f32[80,640]{1,0:T(8,128)S(1)}, f32[80,640]{1,0:T(8,128)S(1)}, u32[]{:S(2)}, u32[]{:S(2)}) collective-permute-start(f32[80,640]{1,0:T(8,128)S(1)} %get-tuple-element.25), channel_id=1, source_target_pairs={{0,1},{1,2},{2,3},{3,4},{4,5},{5,6},{6,7},{7,8},{8,9},{9,10},{10,1... | collective-permute-start | bytes 614408 | tf_op jit(solution)/shard_map/ppermute | solution.py:330
  24.3 5.9 %collective-permute-start.6 = (f32[80,640]{1,0:T(8,128)S(1)}, f32[80,640]{1,0:T(8,128)S(1)}, u32[]{:S(2)}, u32[]{:S(2)}) collective-permute-start(f32[80,640]{1,0:T(8,128)S(1)} %get-tuple-element.26), channel_id=1, source_target_pairs={{1,0},{2,1},{3,2},{4,3},{5,4},{6,5},{7,6},{8,7},{9,8},{10,9},{11,1... | collective-permute-start | bytes 614408 | tf_op jit(solution)/shard_map/ppermute | solution.py:330
  30.2 0.0 copy-done.3
  30.2 0.1 copy.5.taps_ref
  30.3 1.2 %collective-permute-done.5.edge_above = f32[80,640]{1,0:T(8,128)S(1)} collective-permute-done((f32[80,640]{1,0:T(8,128)S(1)}, f32[80,640]{1,0:T(8,128)S(1)}, u32[]{:S(2)}, u32[]{:S(2)}) %collective-permute-start.5) | collective-permute-done | bytes 204832 | tf_op jit(solution)/shard_map/ppermute | solution.py:330
  31.5 1.8 %collective-permute-done.6.edge_below = f32[80,640]{1,0:T(8,128)S(1)} collective-permute-done((f32[80,640]{1,0:T(8,128)S(1)}, f32[80,640]{1,0:T(8,128)S(1)}, u32[]{:S(2)}, u32[]{:S(2)}) %collective-permute-start.6) | collective-permute-done | bytes 204832 | tf_op jit(solution)/shard_map/ppermute | solution.py:330
  33.3 0.0 collective-permute-done.1.below
  33.3 0.0 collective-permute-done.above
  33.3 0.0 copy-done.2
  33.3 22.2 %migrate.1 = (f32[32,512]{1,0:T(8,128)S(1)}, f32[32,512]{1,0:T(8,128)S(1)}, f32[32,512]{1,0:T(8,128)S(1)}, f32[32,512]{1,0:T(8,128)S(1)}) custom-call(f32[28,8,640]{2,1,0:T(8,128)S(1)} %get-tuple-element.18.head, f32[28,8,640]{2,1,0:T(8,128)S(1)} %get-tuple-element.19.tail, f32[28,8,640]{2,1,0:T(8,128)S(1)} %collective-permute-done.above, ...), custom_call_target="tpu_custom_call" | custom-call | tf_op jit(solution)/shard_map/migrate/pallas_call | solution.py:311
  55.5 0.6 collective-permute-start.7
  56.1 3.5 %collective-permute-start.8 = (f32[32,512]{1,0:T(8,128)S(1)}, f32[32,512]{1,0:T(8,128)S(1)}, u32[]{:S(2)}, u32[]{:S(2)}) collective-permute-start(f32[32,512]{1,0:T(8,128)S(1)} %get-tuple-element.29), channel_id=1, source_target_pairs={{0,128},{64,192},{128,0},{192,64},{1,129},{65,193},{129,1},{193,65... | collective-permute-start | bytes 196616 | tf_op jit(solution)/shard_map/ppermute | solution.py:323
  59.6 0.3 collective-permute-start.9
  59.9 1.2 %collective-permute-done.7.refs_1_ = f32[32,512]{1,0:T(8,128)S(1)} collective-permute-done((f32[32,512]{1,0:T(8,128)S(1)}, f32[32,512]{1,0:T(8,128)S(1)}, u32[]{:S(2)}, u32[]{:S(2)}) %collective-permute-start.7) | collective-permute-done | bytes 65568 | tf_op jit(solution)/shard_map/ppermute | solution.py:323
  61.1 1.5 %collective-permute-done.8.refs_2_ = f32[32,512]{1,0:T(8,128)S(1)} collective-permute-done((f32[32,512]{1,0:T(8,128)S(1)}, f32[32,512]{1,0:T(8,128)S(1)}, u32[]{:S(2)}, u32[]{:S(2)}) %collective-permute-start.8) | collective-permute-done | bytes 65568 | tf_op jit(solution)/shard_map/ppermute | solution.py:323
  62.5 1.3 %collective-permute-done.9.refs_3_ = f32[32,512]{1,0:T(8,128)S(1)} collective-permute-done((f32[32,512]{1,0:T(8,128)S(1)}, f32[32,512]{1,0:T(8,128)S(1)}, u32[]{:S(2)}, u32[]{:S(2)}) %collective-permute-start.9) | collective-permute-done | bytes 65568 | tf_op jit(solution)/shard_map/ppermute | solution.py:323
  63.9 0.7 %join.1 = f32[1,32,2048]{2,1,0:T(8,128)} custom-call(f32[32,512]{1,0:T(8,128)S(1)} %get-tuple-element.27.refs_0_, f32[32,512]{1,0:T(8,128)S(1)} %collective-permute-done.7.refs_1_, f32[32,512]{1,0:T(8,128)S(1)} %collective-permute-done.8.refs_2_, f32[32,512]{1,0:T(8,128)S(1)} %collective-permute-done.9.refs_3_), custom_call_target="tpu_custom_call" | custom-call | tf_op jit(solution)/shard_map/join/pallas_call | solution.py:311
Async XLA Ops:
  0.0 1.6 %copy-start = (f32[4,2,32,2048]{3,2,1,0:T(8,128)S(1)}, f32[4,2,32,2048]{3,2,1,0:T(8,128)}, u32[]{:S(2)}) copy-start(f32[4,2,32,2048]{3,2,1,0:T(8,128)} %wave_ref.1) | copy-start | bytes 6291460
  1.6 10.9 %copy-start.1 = (f32[1,32,2048]{2,1,0:T(8,128)S(1)}, f32[1,32,2048]{2,1,0:T(8,128)}, u32[]{:S(2)}) copy-start(f32[1,32,2048]{2,1,0:T(8,128)} %slow_ref.1) | copy-start | bytes 786436
  1.6 28.6 %copy-start.3 = (f32[4,8,2]{1,2,0:T(2,128)S(1)}, f32[4,8,2]{1,2,0:T(2,128)}, u32[]{:S(2)}) copy-start(f32[4,8,2]{1,2,0:T(2,128)} %param.7) | copy-start | bytes 772
  1.6 31.7 %copy-start.2 = (f32[4]{0:T(128)S(1)}, f32[4]{0:T(128)}, u32[]{:S(2)}) copy-start(f32[4]{0:T(128)} %omega_ref.1) | copy-start | bytes 52
  3.1 30.2 %collective-permute-start.1 = (f32[28,8,640]{2,1,0:T(8,128)S(1)}, f32[28,8,640]{2,1,0:T(8,128)S(1)}, u32[]{:S(2)}, u32[]{:S(2)}) collective-permute-start(f32[28,8,640]{2,1,0:T(8,128)S(1)} %get-tuple-element.18.head), channel_id=1, source_target_pairs={{1,0},{2,1},{3,2},{4,3},{5,4},{6,5},{7,6},{8,7},{9,8},{10,9},{11,1... | collective-permute-start | bytes 1720328 | tf_op jit(solution)/shard_map/ppermute | solution.py:330
  10.5 22.7 %collective-permute-start = (f32[28,8,640]{2,1,0:T(8,128)S(1)}, f32[28,8,640]{2,1,0:T(8,128)S(1)}, u32[]{:S(2)}, u32[]{:S(2)}) collective-permute-start(f32[28,8,640]{2,1,0:T(8,128)S(1)} %get-tuple-element.19.tail), channel_id=1, source_target_pairs={{0,1},{1,2},{2,3},{3,4},{4,5},{5,6},{6,7},{7,8},{8,9},{9,10},{10,1... | collective-permute-start | bytes 1720328 | tf_op jit(solution)/shard_map/ppermute | solution.py:330
  12.6 5.9 %collective-permute-start.2 = (f32[32,640]{1,0:T(8,128)S(1)}, f32[32,640]{1,0:T(8,128)S(1)}, u32[]{:S(2)}, u32[]{:S(2)}) collective-permute-start(f32[32,640]{1,0:T(8,128)S(1)} %get-tuple-element.21), channel_id=1, source_target_pairs={{0,64},{64,128},{128,192},{192,0},{1,65},{65,129},{129,193},{193,1... | collective-permute-start | bytes 245768 | tf_op jit(solution)/shard_map/ppermute | solution.py:323
  14.2 6.2 %collective-permute-start.3 = (f32[32,640]{1,0:T(8,128)S(1)}, f32[32,640]{1,0:T(8,128)S(1)}, u32[]{:S(2)}, u32[]{:S(2)}) collective-permute-start(f32[32,640]{1,0:T(8,128)S(1)} %get-tuple-element.22), channel_id=1, source_target_pairs={{0,128},{64,192},{128,0},{192,64},{1,129},{65,193},{129,1},{193,65... | collective-permute-start | bytes 245768 | tf_op jit(solution)/shard_map/ppermute | solution.py:323
  17.1 4.4 %collective-permute-start.4 = (f32[32,640]{1,0:T(8,128)S(1)}, f32[32,640]{1,0:T(8,128)S(1)}, u32[]{:S(2)}, u32[]{:S(2)}) collective-permute-start(f32[32,640]{1,0:T(8,128)S(1)} %get-tuple-element.23), channel_id=1, source_target_pairs={{0,192},{64,0},{128,64},{192,128},{1,193},{65,1},{129,65},{193,129... | collective-permute-start | bytes 245768 | tf_op jit(solution)/shard_map/ppermute | solution.py:323
  22.3 9.2 %collective-permute-start.5 = (f32[80,640]{1,0:T(8,128)S(1)}, f32[80,640]{1,0:T(8,128)S(1)}, u32[]{:S(2)}, u32[]{:S(2)}) collective-permute-start(f32[80,640]{1,0:T(8,128)S(1)} %get-tuple-element.25), channel_id=1, source_target_pairs={{0,1},{1,2},{2,3},{3,4},{4,5},{5,6},{6,7},{7,8},{8,9},{9,10},{10,1... | collective-permute-start | bytes 614408 | tf_op jit(solution)/shard_map/ppermute | solution.py:330
  24.3 9.0 %collective-permute-start.6 = (f32[80,640]{1,0:T(8,128)S(1)}, f32[80,640]{1,0:T(8,128)S(1)}, u32[]{:S(2)}, u32[]{:S(2)}) collective-permute-start(f32[80,640]{1,0:T(8,128)S(1)} %get-tuple-element.26), channel_id=1, source_target_pairs={{1,0},{2,1},{3,2},{4,3},{5,4},{6,5},{7,6},{8,7},{9,8},{10,9},{11,1... | collective-permute-start | bytes 614408 | tf_op jit(solution)/shard_map/ppermute | solution.py:330
  55.5 5.6 %collective-permute-start.7 = (f32[32,512]{1,0:T(8,128)S(1)}, f32[32,512]{1,0:T(8,128)S(1)}, u32[]{:S(2)}, u32[]{:S(2)}) collective-permute-start(f32[32,512]{1,0:T(8,128)S(1)} %get-tuple-element.28), channel_id=1, source_target_pairs={{0,64},{64,128},{128,192},{192,0},{1,65},{65,129},{129,193},{193,1... | collective-permute-start | bytes 196616 | tf_op jit(solution)/shard_map/ppermute | solution.py:323
  56.1 6.5 %collective-permute-start.8 = (f32[32,512]{1,0:T(8,128)S(1)}, f32[32,512]{1,0:T(8,128)S(1)}, u32[]{:S(2)}, u32[]{:S(2)}) collective-permute-start(f32[32,512]{1,0:T(8,128)S(1)} %get-tuple-element.29), channel_id=1, source_target_pairs={{0,128},{64,192},{128,0},{192,64},{1,129},{65,193},{129,1},{193,65... | collective-permute-start | bytes 196616 | tf_op jit(solution)/shard_map/ppermute | solution.py:323
  59.6 4.3 %collective-permute-start.9 = (f32[32,512]{1,0:T(8,128)S(1)}, f32[32,512]{1,0:T(8,128)S(1)}, u32[]{:S(2)}, u32[]{:S(2)}) collective-permute-start(f32[32,512]{1,0:T(8,128)S(1)} %get-tuple-element.30), channel_id=1, source_target_pairs={{0,192},{64,0},{128,64},{192,128},{1,193},{65,1},{129,65},{193,129... | collective-permute-start | bytes 196616 | tf_op jit(solution)/shard_map/ppermute | solution.py:323

commit v5 on v4

--- a/solution.py
+++ b/solution.py
@@ -44,7 +44,7 @@
     return np.linalg.lstsq(rows, function(q), rcond=None)[0]
 
 
-COEFFICIENTS = 6
+COEFFICIENTS = 5
 ARGUMENT_LIMIT = 1.5
 SINE = fit(lambda q: np.sin(np.sqrt(q)) / np.sqrt(q), 0.0, ARGUMENT_LIMIT**2, COEFFICIENTS)
 COSINE = fit(lambda q: np.cos(np.sqrt(q)), 0.0, ARGUMENT_LIMIT**2, COEFFICIENTS)
@@ -278,13 +278,8 @@
 
         rows_loop(lower + TERMS - 1, upper - TERMS + 1, FINISH, finish)
 
-        def gather(index, carry):
-            start = pl.multiple_of(index * 8, 8)
-            block = terms[0][pl.ds(ROWS + start, 8)]
-            mixed[pl.ds(depth * ROWS + start, 8)] = jnp.sum(block[:, :FREQS], axis=1)
-            return carry
-
-        lax.fori_loop(0, ROWS // 8, gather, 0)
+        block = terms[0][ROWS : 2 * ROWS, :FREQS]
+        mixed[depth * ROWS : (depth + 1) * ROWS] = jnp.sum(block, axis=1)
     held[...] = exact_dot(mixed[...], matrix).reshape(held.shape)
     for shift, image in enumerate(images):
         image[...] = held[lax.rem(here + shift, DEPTHS)]

time: 65 us -> 64.5 us (level)
  no operation moved by 1% of the time
where the time goes in v5:
time: 64.5 us; the launch traced here: 64.3 us
  starting transfers between devices  27.5 us (43%)
  Pallas kernels  24.8 us (38%)
  waiting for transfers between devices  10.1 us (16%)
  local copies, waits for them, and re-layouts  1.7 us (3%)
    pallas_call x5, Pallas kernels, call(): pl.pallas_call(kernel, out_shape=[jax.ShapeDtypeStruct(shape, f32) for sh...  24.8 us
    ppermute x4, starting transfers between devices, beside(): return (lax.ppermute(first, 'tile', up), lax.ppermute(last, 'tile', down))  17.2 us
    ppermute x6, starting transfers between devices, around(): lax.ppermute(pieces[k], 'slab', [(i, (i + k) % slabs) for i in range(slab...  10.3 us
    ppermute x6, waiting for transfers between devices, around(): lax.ppermute(pieces[k], 'slab', [(i, (i + k) % slabs) for i in range(slab...  7.08 us
    ppermute x4, waiting for transfers between devices, beside(): return (lax.ppermute(first, 'tile', up), lax.ppermute(last, 'tile', down))  2.97 us
    unnamed x9, local copies, waits for them, and re-layouts  1.7 us
  transfers between devices with their start and end apart: 10, of which 7 were waited for; matrix products, arithmetic and copies ran while one was open for 0% of the time, Pallas kernels for 1%

profile of v5, /device:TPU:6, one launch (start us, length us, event | category | flops | bytes accessed | tf_op | source)
XLA Modules:
  0.0 64.3 jit_solution(3056415248905934932)
XLA Ops:
  0.0 0.0 copy-start
  0.0 1.6 %copy-done = f32[4,2,32,2048]{3,2,1,0:T(8,128)S(1)} copy-done((f32[4,2,32,2048]{3,2,1,0:T(8,128)S(1)}, f32[4,2,32,2048]{3,2,1,0:T(8,128)}, u32[]{:S(2)}) %copy-start) | copy-done | bytes 2097176
  1.6 0.0 copy-start.1
  1.6 0.0 copy-start.3
  1.6 0.0 copy-start.2
  1.6 1.5 %wave.1 = (f32[28,8,640]{2,1,0:T(8,128)S(1)}, f32[28,8,640]{2,1,0:T(8,128)S(1)}) custom-call(f32[4,2,32,2048]{3,2,1,0:T(8,128)S(1)} %copy-done), custom_call_target="tpu_custom_call" | custom-call | tf_op jit(solution)/shard_map/wave/pallas_call | solution.py:306
  3.1 7.5 %collective-permute-start.1 = (f32[28,8,640]{2,1,0:T(8,128)S(1)}, f32[28,8,640]{2,1,0:T(8,128)S(1)}, u32[]{:S(2)}, u32[]{:S(2)}) collective-permute-start(f32[28,8,640]{2,1,0:T(8,128)S(1)} %get-tuple-element.18.head), channel_id=1, source_target_pairs={{1,0},{2,1},{3,2},{4,3},{5,4},{6,5},{7,6},{8,7},{9,8},{10,9},{11,1... | collective-permute-start | bytes 1720328 | tf_op jit(solution)/shard_map/ppermute | solution.py:325
  10.5 1.9 %collective-permute-start = (f32[28,8,640]{2,1,0:T(8,128)S(1)}, f32[28,8,640]{2,1,0:T(8,128)S(1)}, u32[]{:S(2)}, u32[]{:S(2)}) collective-permute-start(f32[28,8,640]{2,1,0:T(8,128)S(1)} %get-tuple-element.19.tail), channel_id=1, source_target_pairs={{0,1},{1,2},{2,3},{3,4},{4,5},{5,6},{6,7},{7,8},{8,9},{9,10},{10,1... | collective-permute-start | bytes 1720328 | tf_op jit(solution)/shard_map/ppermute | solution.py:325
  12.5 0.0 copy-done.1
  12.5 0.1 slow.1
  12.6 1.7 %collective-permute-start.2 = (f32[32,640]{1,0:T(8,128)S(1)}, f32[32,640]{1,0:T(8,128)S(1)}, u32[]{:S(2)}, u32[]{:S(2)}) collective-permute-start(f32[32,640]{1,0:T(8,128)S(1)} %get-tuple-element.21), channel_id=1, source_target_pairs={{0,64},{64,128},{128,192},{192,0},{1,65},{65,129},{129,193},{193,1... | collective-permute-start | bytes 245768 | tf_op jit(solution)/shard_map/ppermute | solution.py:318
  14.2 2.9 %collective-permute-start.3 = (f32[32,640]{1,0:T(8,128)S(1)}, f32[32,640]{1,0:T(8,128)S(1)}, u32[]{:S(2)}, u32[]{:S(2)}) collective-permute-start(f32[32,640]{1,0:T(8,128)S(1)} %get-tuple-element.22), channel_id=1, source_target_pairs={{0,128},{64,192},{128,0},{192,64},{1,129},{65,193},{129,1},{193,65... | collective-permute-start | bytes 245768 | tf_op jit(solution)/shard_map/ppermute | solution.py:318
  17.1 1.3 %collective-permute-start.4 = (f32[32,640]{1,0:T(8,128)S(1)}, f32[32,640]{1,0:T(8,128)S(1)}, u32[]{:S(2)}, u32[]{:S(2)}) collective-permute-start(f32[32,640]{1,0:T(8,128)S(1)} %get-tuple-element.23), channel_id=1, source_target_pairs={{0,192},{64,0},{128,64},{192,128},{1,193},{65,1},{129,65},{193,129... | collective-permute-start | bytes 245768 | tf_op jit(solution)/shard_map/ppermute | solution.py:318
  18.5 0.0 collective-permute-done.2.refs_1_
  18.5 1.9 %collective-permute-done.3.refs_2_ = f32[32,640]{1,0:T(8,128)S(1)} collective-permute-done((f32[32,640]{1,0:T(8,128)S(1)}, f32[32,640]{1,0:T(8,128)S(1)}, u32[]{:S(2)}, u32[]{:S(2)}) %collective-permute-start.3) | collective-permute-done | bytes 81952 | tf_op jit(solution)/shard_map/ppermute | solution.py:318
  20.4 1.1 %collective-permute-done.4.refs_3_ = f32[32,640]{1,0:T(8,128)S(1)} collective-permute-done((f32[32,640]{1,0:T(8,128)S(1)}, f32[32,640]{1,0:T(8,128)S(1)}, u32[]{:S(2)}, u32[]{:S(2)}) %collective-permute-start.4) | collective-permute-done | bytes 81952 | tf_op jit(solution)/shard_map/ppermute | solution.py:318
  21.6 0.8 %edges.1 = (f32[4,32,640]{2,1,0:T(8,128)S(1)}, f32[80,640]{1,0:T(8,128)S(1)}, f32[80,640]{1,0:T(8,128)S(1)}) custom-call(f32[32,640]{1,0:T(8,128)S(1)} %get-tuple-element.20.refs_0_, f32[32,640]{1,0:T(8,128)S(1)} %collective-permute-done.2.refs_1_, f32[32,640]{1,0:T(8,128)S(1)} %collective-permute-done.3.refs_2_, f32[32,640]{1,0:T(8,128)S(1)} %collective-permute-done.4.refs_3_), custom_call_target="tpu_custom_call" | custom-call | tf_op jit(solution)/shard_map/edges/pallas_call | solution.py:306
  22.3 1.9 %collective-permute-start.5 = (f32[80,640]{1,0:T(8,128)S(1)}, f32[80,640]{1,0:T(8,128)S(1)}, u32[]{:S(2)}, u32[]{:S(2)}) collective-permute-start(f32[80,640]{1,0:T(8,128)S(1)} %get-tuple-element.25), channel_id=1, source_target_pairs={{0,1},{1,2},{2,3},{3,4},{4,5},{5,6},{6,7},{7,8},{8,9},{9,10},{10,1... | collective-permute-start | bytes 614408 | tf_op jit(solution)/shard_map/ppermute | solution.py:325
  24.3 5.9 %collective-permute-start.6 = (f32[80,640]{1,0:T(8,128)S(1)}, f32[80,640]{1,0:T(8,128)S(1)}, u32[]{:S(2)}, u32[]{:S(2)}) collective-permute-start(f32[80,640]{1,0:T(8,128)S(1)} %get-tuple-element.26), channel_id=1, source_target_pairs={{1,0},{2,1},{3,2},{4,3},{5,4},{6,5},{7,6},{8,7},{9,8},{10,9},{11,1... | collective-permute-start | bytes 614408 | tf_op jit(solution)/shard_map/ppermute | solution.py:325
  30.2 0.0 copy-done.3
  30.2 0.1 copy.5.taps_ref
  30.3 1.2 %collective-permute-done.5.edge_above = f32[80,640]{1,0:T(8,128)S(1)} collective-permute-done((f32[80,640]{1,0:T(8,128)S(1)}, f32[80,640]{1,0:T(8,128)S(1)}, u32[]{:S(2)}, u32[]{:S(2)}) %collective-permute-start.5) | collective-permute-done | bytes 204832 | tf_op jit(solution)/shard_map/ppermute | solution.py:325
  31.5 1.8 %collective-permute-done.6.edge_below = f32[80,640]{1,0:T(8,128)S(1)} collective-permute-done((f32[80,640]{1,0:T(8,128)S(1)}, f32[80,640]{1,0:T(8,128)S(1)}, u32[]{:S(2)}, u32[]{:S(2)}) %collective-permute-start.6) | collective-permute-done | bytes 204832 | tf_op jit(solution)/shard_map/ppermute | solution.py:325
  33.3 0.0 collective-permute-done.1.below
  33.3 0.0 collective-permute-done.above
  33.3 0.0 copy-done.2
  33.3 21.7 %migrate.1 = (f32[32,512]{1,0:T(8,128)S(1)}, f32[32,512]{1,0:T(8,128)S(1)}, f32[32,512]{1,0:T(8,128)S(1)}, f32[32,512]{1,0:T(8,128)S(1)}) custom-call(f32[28,8,640]{2,1,0:T(8,128)S(1)} %get-tuple-element.18.head, f32[28,8,640]{2,1,0:T(8,128)S(1)} %get-tuple-element.19.tail, f32[28,8,640]{2,1,0:T(8,128)S(1)} %collective-permute-done.above, ...), custom_call_target="tpu_custom_call" | custom-call | tf_op jit(solution)/shard_map/migrate/pallas_call | solution.py:306
  55.0 0.6 collective-permute-start.7
  55.6 3.5 %collective-permute-start.8 = (f32[32,512]{1,0:T(8,128)S(1)}, f32[32,512]{1,0:T(8,128)S(1)}, u32[]{:S(2)}, u32[]{:S(2)}) collective-permute-start(f32[32,512]{1,0:T(8,128)S(1)} %get-tuple-element.29), channel_id=1, source_target_pairs={{0,128},{64,192},{128,0},{192,64},{1,129},{65,193},{129,1},{193,65... | collective-permute-start | bytes 196616 | tf_op jit(solution)/shard_map/ppermute | solution.py:318
  59.1 0.3 collective-permute-start.9
  59.4 1.2 %collective-permute-done.7.refs_1_ = f32[32,512]{1,0:T(8,128)S(1)} collective-permute-done((f32[32,512]{1,0:T(8,128)S(1)}, f32[32,512]{1,0:T(8,128)S(1)}, u32[]{:S(2)}, u32[]{:S(2)}) %collective-permute-start.7) | collective-permute-done | bytes 65568 | tf_op jit(solution)/shard_map/ppermute | solution.py:318
  60.6 1.5 %collective-permute-done.8.refs_2_ = f32[32,512]{1,0:T(8,128)S(1)} collective-permute-done((f32[32,512]{1,0:T(8,128)S(1)}, f32[32,512]{1,0:T(8,128)S(1)}, u32[]{:S(2)}, u32[]{:S(2)}) %collective-permute-start.8) | collective-permute-done | bytes 65568 | tf_op jit(solution)/shard_map/ppermute | solution.py:318
  62.1 1.3 %collective-permute-done.9.refs_3_ = f32[32,512]{1,0:T(8,128)S(1)} collective-permute-done((f32[32,512]{1,0:T(8,128)S(1)}, f32[32,512]{1,0:T(8,128)S(1)}, u32[]{:S(2)}, u32[]{:S(2)}) %collective-permute-start.9) | collective-permute-done | bytes 65568 | tf_op jit(solution)/shard_map/ppermute | solution.py:318
  63.4 0.7 %join.1 = f32[1,32,2048]{2,1,0:T(8,128)} custom-call(f32[32,512]{1,0:T(8,128)S(1)} %get-tuple-element.27.refs_0_, f32[32,512]{1,0:T(8,128)S(1)} %collective-permute-done.7.refs_1_, f32[32,512]{1,0:T(8,128)S(1)} %collective-permute-done.8.refs_2_, f32[32,512]{1,0:T(8,128)S(1)} %collective-permute-done.9.refs_3_), custom_call_target="tpu_custom_call" | custom-call | tf_op jit(solution)/shard_map/join/pallas_call | solution.py:306
Async XLA Ops:
  0.0 1.6 %copy-start = (f32[4,2,32,2048]{3,2,1,0:T(8,128)S(1)}, f32[4,2,32,2048]{3,2,1,0:T(8,128)}, u32[]{:S(2)}) copy-start(f32[4,2,32,2048]{3,2,1,0:T(8,128)} %wave_ref.1) | copy-start | bytes 6291460
  1.6 10.9 %copy-start.1 = (f32[1,32,2048]{2,1,0:T(8,128)S(1)}, f32[1,32,2048]{2,1,0:T(8,128)}, u32[]{:S(2)}) copy-start(f32[1,32,2048]{2,1,0:T(8,128)} %slow_ref.1) | copy-start | bytes 786436
  1.6 28.6 %copy-start.3 = (f32[4,8,2]{1,2,0:T(2,128)S(1)}, f32[4,8,2]{1,2,0:T(2,128)}, u32[]{:S(2)}) copy-start(f32[4,8,2]{1,2,0:T(2,128)} %param.7) | copy-start | bytes 772
  1.6 31.7 %copy-start.2 = (f32[4]{0:T(128)S(1)}, f32[4]{0:T(128)}, u32[]{:S(2)}) copy-start(f32[4]{0:T(128)} %omega_ref.1) | copy-start | bytes 52
  3.1 30.2 %collective-permute-start.1 = (f32[28,8,640]{2,1,0:T(8,128)S(1)}, f32[28,8,640]{2,1,0:T(8,128)S(1)}, u32[]{:S(2)}, u32[]{:S(2)}) collective-permute-start(f32[28,8,640]{2,1,0:T(8,128)S(1)} %get-tuple-element.18.head), channel_id=1, source_target_pairs={{1,0},{2,1},{3,2},{4,3},{5,4},{6,5},{7,6},{8,7},{9,8},{10,9},{11,1... | collective-permute-start | bytes 1720328 | tf_op jit(solution)/shard_map/ppermute | solution.py:325
  10.5 22.7 %collective-permute-start = (f32[28,8,640]{2,1,0:T(8,128)S(1)}, f32[28,8,640]{2,1,0:T(8,128)S(1)}, u32[]{:S(2)}, u32[]{:S(2)}) collective-permute-start(f32[28,8,640]{2,1,0:T(8,128)S(1)} %get-tuple-element.19.tail), channel_id=1, source_target_pairs={{0,1},{1,2},{2,3},{3,4},{4,5},{5,6},{6,7},{7,8},{8,9},{9,10},{10,1... | collective-permute-start | bytes 1720328 | tf_op jit(solution)/shard_map/ppermute | solution.py:325
  12.6 5.9 %collective-permute-start.2 = (f32[32,640]{1,0:T(8,128)S(1)}, f32[32,640]{1,0:T(8,128)S(1)}, u32[]{:S(2)}, u32[]{:S(2)}) collective-permute-start(f32[32,640]{1,0:T(8,128)S(1)} %get-tuple-element.21), channel_id=1, source_target_pairs={{0,64},{64,128},{128,192},{192,0},{1,65},{65,129},{129,193},{193,1... | collective-permute-start | bytes 245768 | tf_op jit(solution)/shard_map/ppermute | solution.py:318
  14.2 6.2 %collective-permute-start.3 = (f32[32,640]{1,0:T(8,128)S(1)}, f32[32,640]{1,0:T(8,128)S(1)}, u32[]{:S(2)}, u32[]{:S(2)}) collective-permute-start(f32[32,640]{1,0:T(8,128)S(1)} %get-tuple-element.22), channel_id=1, source_target_pairs={{0,128},{64,192},{128,0},{192,64},{1,129},{65,193},{129,1},{193,65... | collective-permute-start | bytes 245768 | tf_op jit(solution)/shard_map/ppermute | solution.py:318
  17.1 4.4 %collective-permute-start.4 = (f32[32,640]{1,0:T(8,128)S(1)}, f32[32,640]{1,0:T(8,128)S(1)}, u32[]{:S(2)}, u32[]{:S(2)}) collective-permute-start(f32[32,640]{1,0:T(8,128)S(1)} %get-tuple-element.23), channel_id=1, source_target_pairs={{0,192},{64,0},{128,64},{192,128},{1,193},{65,1},{129,65},{193,129... | collective-permute-start | bytes 245768 | tf_op jit(solution)/shard_map/ppermute | solution.py:318
  22.3 9.2 %collective-permute-start.5 = (f32[80,640]{1,0:T(8,128)S(1)}, f32[80,640]{1,0:T(8,128)S(1)}, u32[]{:S(2)}, u32[]{:S(2)}) collective-permute-start(f32[80,640]{1,0:T(8,128)S(1)} %get-tuple-element.25), channel_id=1, source_target_pairs={{0,1},{1,2},{2,3},{3,4},{4,5},{5,6},{6,7},{7,8},{8,9},{9,10},{10,1... | collective-permute-start | bytes 614408 | tf_op jit(solution)/shard_map/ppermute | solution.py:325
  24.3 9.0 %collective-permute-start.6 = (f32[80,640]{1,0:T(8,128)S(1)}, f32[80,640]{1,0:T(8,128)S(1)}, u32[]{:S(2)}, u32[]{:S(2)}) collective-permute-start(f32[80,640]{1,0:T(8,128)S(1)} %get-tuple-element.26), channel_id=1, source_target_pairs={{1,0},{2,1},{3,2},{4,3},{5,4},{6,5},{7,6},{8,7},{9,8},{10,9},{11,1... | collective-permute-start | bytes 614408 | tf_op jit(solution)/shard_map/ppermute | solution.py:325
  55.0 5.6 %collective-permute-start.7 = (f32[32,512]{1,0:T(8,128)S(1)}, f32[32,512]{1,0:T(8,128)S(1)}, u32[]{:S(2)}, u32[]{:S(2)}) collective-permute-start(f32[32,512]{1,0:T(8,128)S(1)} %get-tuple-element.28), channel_id=1, source_target_pairs={{0,64},{64,128},{128,192},{192,0},{1,65},{65,129},{129,193},{193,1... | collective-permute-start | bytes 196616 | tf_op jit(solution)/shard_map/ppermute | solution.py:318
  55.6 6.5 %collective-permute-start.8 = (f32[32,512]{1,0:T(8,128)S(1)}, f32[32,512]{1,0:T(8,128)S(1)}, u32[]{:S(2)}, u32[]{:S(2)}) collective-permute-start(f32[32,512]{1,0:T(8,128)S(1)} %get-tuple-element.29), channel_id=1, source_target_pairs={{0,128},{64,192},{128,0},{192,64},{1,129},{65,193},{129,1},{193,65... | collective-permute-start | bytes 196616 | tf_op jit(solution)/shard_map/ppermute | solution.py:318
  59.1 4.3 %collective-permute-start.9 = (f32[32,512]{1,0:T(8,128)S(1)}, f32[32,512]{1,0:T(8,128)S(1)}, u32[]{:S(2)}, u32[]{:S(2)}) collective-permute-start(f32[32,512]{1,0:T(8,128)S(1)} %get-tuple-element.30), channel_id=1, source_target_pairs={{0,192},{64,0},{128,64},{192,128},{1,193},{65,1},{129,65},{193,129... | collective-permute-start | bytes 196616 | tf_op jit(solution)/shard_map/ppermute | solution.py:318
